TPU v7x, 32 devices: a whole 2x2x4 slice. The times are simulated.
32 devices in a mesh: ew: 4 (over y, x), ns: 8 (over z, core).
Axes of the slice: x: 2, y: 2, z: 4, core: 2. Of those that a mesh axis runs over, the one named last changes fastest.
Arguments:
- tokens: bfloat16 [8, 4, 2, 64, 768], P('ns', 'ew'), may hold values from -6 to 6
- vis_index: int32 [8, 4, 2, 64], P('ns', 'ew'), may hold values from 0 to 255, as said below
- counts: int32 [8, 4, 2], P('ns', 'ew'), may hold values from 32 to 64
- owners: int32 [8, 4, 2, 64, 1], P('ns', 'ew'), may hold values from 0 to 7; in each aligned block of 128 rows (0 to 127, 128 to 255, ..., all dimensions but the last counted through in order) at most 24 rows name the same one
- mask_token: bfloat16 [768], replicated, may hold values from -6 to 6
- proj_weight: bfloat16 [768, 64], replicated, may hold values from -0.21875 to 0.21875
- up_first: bfloat16 [4, 4, 64, 64], replicated, may hold values from -0.375 to 0.375
- up_second: bfloat16 [4, 4, 12, 64], replicated, may hold values from -0.375 to 0.375
- saved_pre: bfloat16 [2, 64, 64, 512], P(None, None, 'ns', 'ew'), may hold values from -6 to 6
- cotangent: bfloat16 [2, 12, 128, 1024], P(None, None, 'ns', 'ew'), may hold values from -6 to 6
Outputs:
- token_grad: bfloat16 [8, 4, 192, 768], P('ns', 'ew')
- grad_proj: float32 [768, 64], replicated
- grad_first: float32 [4, 4, 64, 64], replicated
- grad_second: float32 [4, 4, 12, 64], replicated
- grad_mask: float32 [768], replicated
Inputs may be any that keep to these rules, and one draw needn't show every extreme that they name: `vis_index`: each entry is a patch number of its tile, patches numbered row by row with 64 to a row; the 64 entries of one tile and date are distinct; the live ones are the first counts entries. `owners`: among the 128 slots of one tile, live or not, at most 24 name the same owner.
All inputs are finite; a program needn't handle non-finite values.
Results may differ from a plain program's by a relative error of at most 0.0057.
Values may be sent and summed in bfloat16 or wider, within the bound.
No kernel may reach another device: no remote copies, remote signals or barrier semaphores. Data moves between devices by JAX's collectives and lax.ppermute only.
A program may use at most 64 MiB of HBM per device.

v0:
```python
import jax
import jax.numpy as jnp
from jax import lax
from jax.sharding import PartitionSpec as P


def padded_2(block, sides, width):
    for axis, dim in sides:
        count = lax.axis_size(axis)
        forward = [(i, i + 1) for i in range(count - 1)]
        backward = [(target, source) for source, target in forward]
        low = lax.ppermute(
            lax.slice_in_dim(block, block.shape[dim] - width, None, axis=dim), axis, forward
        )
        high = lax.ppermute(lax.slice_in_dim(block, 0, width, axis=dim), axis, backward)
        block = jnp.concatenate([low, block, high], axis=dim)
    return block


def gelu_value(preact):
    return preact * jax.nn.sigmoid(1.702 * preact)


def gelu_slope(preact):
    sigmoid_value = jax.nn.sigmoid(1.702 * preact)
    return sigmoid_value + 1.702 * preact * sigmoid_value * (1.0 - sigmoid_value)


def transpose_back(inputs, padded, kernel):
    height = inputs.shape[2]
    breadth = inputs.shape[3]
    grad_inputs = None
    grad_taps = []
    for tap_y in range(4):
        for tap_x in range(4):
            window = padded[:, :, tap_y : tap_y + 2 * height : 2, tap_x : tap_x + 2 * breadth : 2]
            partial_term = jnp.einsum(
                "oi,fohw->fihw", kernel[tap_y, tap_x], window, preferred_element_type=jnp.float32
            )
            grad_inputs = partial_term if grad_inputs is None else grad_inputs + partial_term
            grad_taps.append(
                jnp.einsum("fihw,fohw->oi", inputs, window, preferred_element_type=jnp.float32)
            )
    grad_kernel = jnp.stack(grad_taps).reshape((4, 4) + kernel.shape[2:])
    return (grad_inputs, grad_kernel)


def per_device(
    tokens,
    vis_index,
    counts,
    owners,
    mask_token,
    proj_weight,
    up_first,
    up_second,
    saved_pre,
    cotangent,
):
    tile_tokens = tokens[0, 0]
    tile_index = vis_index[0, 0]
    tile_counts = counts[0, 0]
    tile_owners = owners[0, 0, :, :, 0]
    frames, slots, features = tile_tokens.shape
    channels = proj_weight.shape[1]
    tok_rows = saved_pre.shape[2] // 2
    tok_cols = saved_pre.shape[3] // 2
    patches = tok_rows * tok_cols
    is_live = jnp.arange(slots, dtype=jnp.int32)[None, :] < tile_counts[:, None]
    picks = (
        tile_index[:, :, None] == jnp.arange(patches, dtype=jnp.int32)[None, None, :]
    ) & is_live[:, :, None]
    picks_half = picks.astype(jnp.bfloat16)
    hidden_mask = 1.0 - jnp.sum(picks.astype(jnp.float32), axis=1)
    token_proj = jnp.einsum(
        "fvd,dc->fvc", tile_tokens, proj_weight, preferred_element_type=jnp.float32
    ).astype(jnp.bfloat16)
    mask_proj = jnp.dot(
        mask_token[None, :], proj_weight, preferred_element_type=jnp.float32
    ).astype(jnp.bfloat16)[0]
    placed = jnp.einsum("fvp,fvc->fcp", picks_half, token_proj, preferred_element_type=jnp.float32)
    placed = placed + hidden_mask[:, None, :] * mask_proj.astype(jnp.float32)[None, :, None]
    first_in = placed.astype(jnp.bfloat16).reshape(frames, channels, tok_rows, tok_cols)
    padded_cot = padded_2(cotangent, (("ew", 3), ("ns", 2)), 1)
    pre_wide = saved_pre.astype(jnp.float32)
    hidden = gelu_value(pre_wide).astype(jnp.bfloat16)
    grad_hidden, grad_second = transpose_back(hidden, padded_cot, up_second)
    deltas = (grad_hidden * gelu_slope(pre_wide)).astype(jnp.bfloat16)
    padded_deltas = padded_2(deltas, (("ew", 3), ("ns", 2)), 1)
    grad_grid, grad_first = transpose_back(first_in, padded_deltas, up_first)
    grad_grid = grad_grid.astype(jnp.bfloat16).reshape(frames, channels, patches)
    chosen = jnp.einsum(
        "fvp,fcp->fvc", picks_half, grad_grid, preferred_element_type=jnp.float32
    ).astype(jnp.bfloat16)
    mask_sum = jnp.einsum(
        "fp,fcp->c", hidden_mask, grad_grid.astype(jnp.float32), precision=lax.Precision.HIGHEST
    )
    grad_proj = jnp.einsum("fvd,fvc->dc", tile_tokens, chosen, preferred_element_type=jnp.float32)
    grad_proj = grad_proj + mask_token.astype(jnp.float32)[:, None] * mask_sum[None, :]
    grad_proj, grad_first, grad_second, mask_sum = lax.psum(
        (grad_proj, grad_first, grad_second, mask_sum), ("ew", "ns")
    )
    grad_mask = jnp.dot(proj_weight.astype(jnp.float32), mask_sum, precision=lax.Precision.HIGHEST)
    owner_count = lax.axis_size("ns")
    row_count = frames * slots
    capacity = 3 * row_count // (2 * owner_count)
    owner_rows = tile_owners.reshape(row_count)
    live_rows = is_live.reshape(row_count)
    owner_hits = (
        (owner_rows[:, None] == jnp.arange(owner_count, dtype=jnp.int32)[None, :])
        & live_rows[:, None]
    ).astype(jnp.int32)
    earlier = jnp.cumsum(owner_hits, axis=0, dtype=jnp.int32) - owner_hits
    place = jnp.sum(earlier * owner_hits, axis=1, dtype=jnp.int32)
    target = jnp.where(live_rows, owner_rows * capacity + place, owner_count * capacity)
    token_rows = jnp.einsum(
        "fvc,dc->fvd", chosen, proj_weight, preferred_element_type=jnp.float32
    ).astype(jnp.bfloat16)
    outgoing = jnp.zeros((owner_count * capacity, features), jnp.bfloat16)
    outgoing = outgoing.at[target].set(token_rows.reshape(row_count, features), mode="drop")
    arrived = lax.all_to_all(
        outgoing.reshape(owner_count, capacity, features),
        "ns",
        split_axis=0,
        concat_axis=0,
        tiled=True,
    )
    token_grad = arrived.reshape(owner_count * capacity, features)
    return (token_grad[None, None], grad_proj, grad_first, grad_second, grad_mask)


def solution(mesh):
    return jax.shard_map(
        per_device,
        mesh=mesh,
        in_specs=(
            P("ns", "ew", None, None, None),
            P("ns", "ew", None, None),
            P("ns", "ew", None),
            P("ns", "ew", None, None, None),
            P(),
            P(),
            P(),
            P(),
            P(None, None, "ns", "ew"),
            P(None, None, "ns", "ew"),
        ),
        out_specs=(P("ns", "ew", None, None), P(), P(), P(), P()),
        check_vma=False,
    )
```

profile of v0, /device:TPU:0, one launch (start us, length us, event | category | flops | bytes accessed | tf_op | source)
XLA Modules:
  0.0 351.5 jit_solution(11625535637131504521)
XLA Ops:
  7.2 1.0 copy.15
  8.4 4.8 %collective-permute-start = (bf16[2,12,16,1]{3,1,2,0:T(8,128)(2,1)S(1)}, bf16[2,12,16,1]{3,1,2,0:T(8,128)(2,1)S(1)}, u32[]{:S(2)}, u32[]{:S(2)}) collective-permute-start(bf16[2,12,16,1]{3,1,2,0:T(8,128)(2,1)S(1)} %get-tuple-element.17), channel_id=1, source_target_pairs={{0,8},{8,16},{16,24},{1,9},{9,17},{17,25},{2,10},{10,18},{18,26},{... | collective-permute-start | bytes 2312 | tf_op jit(solution)/shard_map/ppermute | solution.py:12
  13.3 1.3 collective-permute-start.1
  14.6 3.6 %slice.230 = bf16[2,12,8,128]{3,1,2,0:T(8,128)(2,1)S(1)} slice(bf16[2,12,16,256]{3,1,2,0:T(8,128)(2,1)S(1)} %copy.15), slice={[0:2:1], [0:12:1], [0:16:2], [0:256:2]} | slice | bytes 98304 | tf_op jit(solution)/shard_map/slice | solution.py:36
  18.7 0.7 fusion.177
  20.6 0.7 fusion.172
  24.3 3.6 %slice.228 = bf16[2,12,8,128]{3,1,2,0:T(8,128)(2,1)S(1)} slice(bf16[2,12,16,258]{3,1,2,0:T(8,128)(2,1)S(1)} %pad_maximum_fusion.3), slice={[0:2:1], [0:12:1], [0:16:2], [0:256:2]} | slice | bytes 98304 | tf_op jit(solution)/shard_map/slice | solution.py:36
  28.0 3.7 %slice.234 = bf16[2,12,8,128]{3,1,2,0:T(8,128)(2,1)S(1)} slice(bf16[2,12,16,258]{3,1,2,0:T(8,128)(2,1)S(1)} %pad_maximum_fusion.3), slice={[0:2:1], [0:12:1], [0:16:2], [3:258:2]} | slice | bytes 98304 | tf_op jit(solution)/shard_map/slice | solution.py:36
  31.7 1.5 collective-permute-start.2
  33.1 1.3 collective-permute-start.3
  35.0 3.7 %slice.232 = bf16[2,12,8,128]{3,1,2,0:T(8,128)(2,1)S(1)} slice(bf16[2,12,16,258]{3,1,2,0:T(8,128)(2,1)S(1)} %pad_maximum_fusion.3), slice={[0:2:1], [0:12:1], [0:16:2], [2:258:2]} | slice | bytes 98304 | tf_op jit(solution)/shard_map/slice | solution.py:36
  38.7 1.2 pad_maximum_fusion.2
  39.9 6.7 %slice.220 = bf16[2,12,8,128]{3,1,2,0:T(8,128)(2,1)} slice(bf16[2,12,18,258]{3,1,2,0:T(8,128)(2,1)S(1)} %pad_maximum_fusion.2), slice={[0:2:1], [0:12:1], [0:16:2], [0:256:2]} | slice | bytes 98304 | tf_op jit(solution)/shard_map/slice | solution.py:36
  46.6 6.7 %slice.222 = bf16[2,12,8,128]{3,1,2,0:T(8,128)(2,1)} slice(bf16[2,12,18,258]{3,1,2,0:T(8,128)(2,1)S(1)} %pad_maximum_fusion.2), slice={[0:2:1], [0:12:1], [0:16:2], [1:257:2]} | slice | bytes 98304 | tf_op jit(solution)/shard_map/slice | solution.py:36
  53.3 6.7 %slice.224 = bf16[2,12,8,128]{3,1,2,0:T(8,128)(2,1)} slice(bf16[2,12,18,258]{3,1,2,0:T(8,128)(2,1)S(1)} %pad_maximum_fusion.2), slice={[0:2:1], [0:12:1], [0:16:2], [2:258:2]} | slice | bytes 98304 | tf_op jit(solution)/shard_map/slice | solution.py:36
  60.1 6.7 %slice.226 = bf16[2,12,8,128]{3,1,2,0:T(8,128)(2,1)} slice(bf16[2,12,18,258]{3,1,2,0:T(8,128)(2,1)S(1)} %pad_maximum_fusion.2), slice={[0:2:1], [0:12:1], [0:16:2], [3:258:2]} | slice | bytes 98304 | tf_op jit(solution)/shard_map/slice | solution.py:36
  66.8 6.7 %slice.236 = bf16[2,12,8,128]{3,1,2,0:T(8,128)(2,1)} slice(bf16[2,12,18,258]{3,1,2,0:T(8,128)(2,1)S(1)} %pad_maximum_fusion.2), slice={[0:2:1], [0:12:1], [2:18:2], [0:256:2]} | slice | bytes 98304 | tf_op jit(solution)/shard_map/slice | solution.py:36
  73.5 6.7 %slice.238 = bf16[2,12,8,128]{3,1,2,0:T(8,128)(2,1)} slice(bf16[2,12,18,258]{3,1,2,0:T(8,128)(2,1)S(1)} %pad_maximum_fusion.2), slice={[0:2:1], [0:12:1], [2:18:2], [1:257:2]} | slice | bytes 98304 | tf_op jit(solution)/shard_map/slice | solution.py:36
  80.2 3.6 %slice.240 = bf16[2,12,8,128]{3,1,2,0:T(8,128)(2,1)S(1)} slice(bf16[2,12,18,258]{3,1,2,0:T(8,128)(2,1)S(1)} %pad_maximum_fusion.2), slice={[0:2:1], [0:12:1], [2:18:2], [2:258:2]} | slice | bytes 98304 | tf_op jit(solution)/shard_map/slice | solution.py:36
  83.9 3.7 %slice.242 = bf16[2,12,8,128]{3,1,2,0:T(8,128)(2,1)S(1)} slice(bf16[2,12,18,258]{3,1,2,0:T(8,128)(2,1)S(1)} %pad_maximum_fusion.2), slice={[0:2:1], [0:12:1], [2:18:2], [3:258:2]} | slice | bytes 98304 | tf_op jit(solution)/shard_map/slice | solution.py:36
  87.6 3.8 %slice.244 = bf16[2,12,8,128]{3,1,2,0:T(8,128)(2,1)S(1)} slice(bf16[2,12,18,258]{3,1,2,0:T(8,128)(2,1)S(1)} %pad_maximum_fusion.2), slice={[0:2:1], [0:12:1], [3:18:2], [0:256:2]} | slice | bytes 98304 | tf_op jit(solution)/shard_map/slice | solution.py:36
  91.4 3.8 %slice.246 = bf16[2,12,8,128]{3,1,2,0:T(8,128)(2,1)S(1)} slice(bf16[2,12,18,258]{3,1,2,0:T(8,128)(2,1)S(1)} %pad_maximum_fusion.2), slice={[0:2:1], [0:12:1], [3:18:2], [1:257:2]} | slice | bytes 98304 | tf_op jit(solution)/shard_map/slice | solution.py:36
  95.2 4.1 %slice.248 = bf16[2,12,8,128]{3,1,2,0:T(8,128)(2,1)S(1)} slice(bf16[2,12,18,258]{3,1,2,0:T(8,128)(2,1)S(1)} %pad_maximum_fusion.2), slice={[0:2:1], [0:12:1], [3:18:2], [2:258:2]} | slice | bytes 98304 | tf_op jit(solution)/shard_map/slice | solution.py:36
  99.3 4.1 %slice.250 = bf16[2,12,8,128]{3,1,2,0:T(8,128)(2,1)S(1)} slice(bf16[2,12,18,258]{3,1,2,0:T(8,128)(2,1)S(1)} %pad_maximum_fusion.2), slice={[0:2:1], [0:12:1], [3:18:2], [3:258:2]} | slice | bytes 98304 | tf_op jit(solution)/shard_map/slice | solution.py:36
  103.4 1.1 fusion.148
  104.6 1.1 fusion.149
  109.9 2.9 slice.266
  115.5 4.4 %collective-permute-start.4 = (bf16[2,64,8,1]{3,1,2,0:T(8,128)(2,1)S(1)}, bf16[2,64,8,1]{3,1,2,0:T(8,128)(2,1)S(1)}, u32[]{:S(2)}, u32[]{:S(2)}) collective-permute-start(bf16[2,64,8,1]{3,1,2,0:T(8,128)(2,1)S(1)} %get-tuple-element.15), channel_id=1, source_target_pairs={{0,8},{8,16},{16,24},{1,9},{9,17},{17,25},{2,10},{10,18},{18,26},{... | collective-permute-start | bytes 6152 | tf_op jit(solution)/shard_map/ppermute | solution.py:12
  119.9 1.3 collective-permute-start.5
  121.2 1.6 fusion.110
  123.0 1.5 collective-permute-done.4
  124.5 8.5 %collective-permute-done.5 = bf16[2,64,8,1]{3,1,2,0:T(8,128)(2,1)S(1)} collective-permute-done((bf16[2,64,8,1]{3,1,2,0:T(8,128)(2,1)S(1)}, bf16[2,64,8,1]{3,1,2,0:T(8,128)(2,1)S(1)}, u32[]{:S(2)}, u32[]{:S(2)}) %collective-permute-start.5) | collective-permute-done | bytes 2080 | tf_op jit(solution)/shard_map/ppermute | solution.py:15
  133.3 2.9 slice.264
  136.3 2.9 slice.270
  139.2 3.8 %collective-permute-start.6 = (bf16[2,64,1,130]{3,1,2,0:T(8,128)(2,1)S(1)}, bf16[2,64,1,130]{3,1,2,0:T(8,128)(2,1)S(1)}, u32[]{:S(2)}, u32[]{:S(2)}) collective-permute-start(bf16[2,64,1,130]{3,1,2,0:T(8,128)(2,1)S(1)} %get-tuple-element.11), channel_id=1, source_target_pairs={{0,1},{1,2},{2,3},{3,4},{4,5},{5,6},{6,7},{8,9},{9,10},{10,11},{11... | collective-permute-start | bytes 99848 | tf_op jit(solution)/shard_map/ppermute | solution.py:12
  143.0 1.5 collective-permute-start.7
  144.5 1.6 fusion.112
  146.1 1.6 fusion.107
  147.7 2.9 slice.268
  151.0 3.0 slice.262
  154.0 3.0 slice.260
  156.9 3.0 slice.258
  159.9 2.9 slice.256
  162.8 3.0 slice.276
  165.8 3.0 slice.274
  168.7 2.9 slice.272
  171.6 3.1 slice.286
  174.8 3.1 slice.284
  177.9 3.1 slice.282
  181.0 3.1 slice.280
  184.1 3.0 slice.278
  187.1 1.0 fusion.114
  188.1 0.9 fusion.116
  191.6 0.7 copy-done.4
  196.4 1.9 scatter_custom_fusion
  198.4 8.4 %all-to-all-start = ((bf16[8,24,768]{2,1,0:T(8,128)(2,1)}), bf16[8,24,768]{2,1,0:T(8,128)(2,1)S(1)}, u32[]{:S(2)}, u32[]{:S(2)}) async-start(bf16[8,24,768]{2,1,0:T(8,128)(2,1)} %bitcast.105), calls=%async_computation | async-start | bytes 589824 | tf_op jit(solution)/shard_map/all_to_all | solution.py:121
  206.8 0.9 fusion.30
  207.9 0.8 copy-done.5
  208.9 41.3 %all-reduce = (f32[4,4,12,64]{3,1,2,0:T(4,128)}, f32[64]{0:T(128)S(1)}) all-reduce(f32[4,4,12,64]{3,1,2,0:T(4,128)S(1)} %copy.70, f32[64]{0:T(128)S(1)} %convolution_bitcast_fusion.33), channel_id=1, replica_groups=mesh['ew'=4,'ns'=8] {'ew','ns'}, use_global_device_ids=true, to_apply=%region_6.7 | all-reduce | flops 12352 | bytes 98816 | tf_op jit(solution)/shard_map/psum | solution.py:100
  250.2 0.8 convolution_reduce_fusion
  251.0 90.6 %all-reduce.4.cloned.1.call-done = (f32[768,64]{0,1:T(8,128)}, f32[4,4,64,64]{3,2,1,0:T(8,128)}) async-done(((f32[768,64]{0,1:T(8,128)}, f32[4,4,64,64]{3,2,1,0:T(8,128)}), (f32[768,64]{0,1:T(8,128)}, f32[4,4,64,64]{3,2,1,0:T(8,128)})) %all-reduce.4.cloned.1.call-update) | async-done | bytes 458768 | tf_op jit(solution)/shard_map/psum | solution.py:100
  341.5 0.7 copy.271
  342.2 1.6 copy.272
  343.9 0.8 copy.273
  (183 shorter events, 19.7 us)
Async XLA Ops:
  7.2 15.1 %copy-start = (bf16[1,1,2,64,768]{4,3,2,1,0:T(8,128)(2,1)S(1)}, bf16[1,1,2,64,768]{4,3,2,1,0:T(8,128)(2,1)}, u32[]{:S(2)}) copy-start(bf16[1,1,2,64,768]{4,3,2,1,0:T(8,128)(2,1)} %param.10) | copy-start | bytes 589828
  7.2 11.0 %copy-start.44 = (s32[1,1,2]{2,1,0:T(1,128)S(1)}, s32[1,1,2]{2,1,0:T(1,128)}, u32[]{:S(2)}) copy-start(s32[1,1,2]{2,1,0:T(1,128)} %param.12) | copy-start | bytes 28
  7.2 11.3 %copy-start.1 = (bf16[2,64,8,128]{3,2,1,0:T(8,128)(2,1)S(1)}, bf16[2,64,8,128]{3,2,1,0:T(8,128)(2,1)}, u32[]{:S(2)}) copy-start(bf16[2,64,8,128]{3,2,1,0:T(8,128)(2,1)} %param.18) | copy-start | bytes 786436
  8.2 10.4 %copy-start.22 = (bf16[4,4,12,64]{3,1,2,0:T(4,128)(2,1)S(1)}, bf16[4,4,12,64]{3,1,2,0:T(4,128)(2,1)}, u32[]{:S(2)}) copy-start(bf16[4,4,12,64]{3,1,2,0:T(4,128)(2,1)} %param.17) | copy-start | bytes 73732
  8.3 11.1 %copy-start.40 = (s32[1,1,2,64]{3,2,1,0:T(2,128)S(1)}, s32[1,1,2,64]{3,2,1,0:T(2,128)}, u32[]{:S(2)}) copy-start(s32[1,1,2,64]{3,2,1,0:T(2,128)} %param.11) | copy-start | bytes 1540
  8.3 11.8 %copy-start.38 = (bf16[768]{0:T(1024)(128)(2,1)S(1)}, bf16[768]{0:T(1024)(128)(2,1)}, u32[]{:S(2)}) copy-start(bf16[768]{0:T(1024)(128)(2,1)} %param.14) | copy-start | bytes 4612
  8.3 12.3 %copy-start.39 = (s32[1,1,2,64,1]{3,4,2,1,0:T(1,128)S(1)}, s32[1,1,2,64,1]{3,4,2,1,0:T(1,128)}, u32[]{:S(2)}) copy-start(s32[1,1,2,64,1]{3,4,2,1,0:T(1,128)} %param.13) | copy-start | bytes 1540
  8.4 15.6 %collective-permute-start = (bf16[2,12,16,1]{3,1,2,0:T(8,128)(2,1)S(1)}, bf16[2,12,16,1]{3,1,2,0:T(8,128)(2,1)S(1)}, u32[]{:S(2)}, u32[]{:S(2)}) collective-permute-start(bf16[2,12,16,1]{3,1,2,0:T(8,128)(2,1)S(1)} %get-tuple-element.17), channel_id=1, source_target_pairs={{0,8},{8,16},{16,24},{1,9},{9,17},{17,25},{2,10},{10,18},{18,26},{... | collective-permute-start | bytes 2312 | tf_op jit(solution)/shard_map/ppermute | solution.py:12
  13.3 10.8 %collective-permute-start.1 = (bf16[2,12,16,1]{3,1,2,0:T(8,128)(2,1)S(1)}, bf16[2,12,16,1]{3,1,2,0:T(8,128)(2,1)S(1)}, u32[]{:S(2)}, u32[]{:S(2)}) collective-permute-start(bf16[2,12,16,1]{3,1,2,0:T(8,128)(2,1)S(1)} %get-tuple-element.18), channel_id=1, source_target_pairs={{8,0},{16,8},{24,16},{9,1},{17,9},{25,17},{10,2},{18,10},{26,18},{... | collective-permute-start | bytes 2312 | tf_op jit(solution)/shard_map/ppermute | solution.py:15
  18.3 4.0 %copy-start.42 = (pred[2,64]{1,0:T(4,128)(4,1)}, pred[2,64]{1,0:T(4,128)(4,1)S(1)}, u32[]{:S(2)}) copy-start(pred[2,64]{1,0:T(4,128)(4,1)S(1)} %iota_compare_fusion.2) | copy-start | bytes 388
  18.6 3.5 %copy-start.19 = (bf16[768,64]{0,1:T(8,128)(2,1)S(1)}, bf16[768,64]{0,1:T(8,128)(2,1)}, u32[]{:S(2)}) copy-start(bf16[768,64]{0,1:T(8,128)(2,1)} %param.15) | copy-start | bytes 294916
  24.0 10.7 %copy-start.17 = (bf16[2,12,16,1]{3,1,2,0:T(8,128)(2,1)}, bf16[2,12,16,1]{3,1,2,0:T(8,128)(2,1)S(1)}, u32[]{:S(2)}) copy-start(bf16[2,12,16,1]{3,1,2,0:T(8,128)(2,1)S(1)} %collective-permute-done) | copy-start | bytes 2308
  24.0 10.7 %copy-start.18 = (bf16[2,12,16,1]{3,1,2,0:T(8,128)(2,1)}, bf16[2,12,16,1]{3,1,2,0:T(8,128)(2,1)S(1)}, u32[]{:S(2)}) copy-start(bf16[2,12,16,1]{3,1,2,0:T(8,128)(2,1)S(1)} %collective-permute-done.1) | copy-start | bytes 2308
  31.7 7.0 %collective-permute-start.2 = (bf16[2,12,1,258]{3,1,2,0:T(8,128)(2,1)S(1)}, bf16[2,12,1,258]{3,1,2,0:T(8,128)(2,1)S(1)}, u32[]{:S(2)}, u32[]{:S(2)}) collective-permute-start(bf16[2,12,1,258]{3,1,2,0:T(8,128)(2,1)S(1)} %get-tuple-element.13), channel_id=1, source_target_pairs={{0,1},{1,2},{2,3},{3,4},{4,5},{5,6},{6,7},{8,9},{9,10},{10,11},{11... | collective-permute-start | bytes 37160 | tf_op jit(solution)/shard_map/ppermute | solution.py:12
  33.1 5.6 %collective-permute-start.3 = (bf16[2,12,1,258]{3,1,2,0:T(8,128)(2,1)S(1)}, bf16[2,12,1,258]{3,1,2,0:T(8,128)(2,1)S(1)}, u32[]{:S(2)}, u32[]{:S(2)}) collective-permute-start(bf16[2,12,1,258]{3,1,2,0:T(8,128)(2,1)S(1)} %get-tuple-element.14), channel_id=1, source_target_pairs={{1,0},{2,1},{3,2},{4,3},{5,4},{6,5},{7,6},{9,8},{10,9},{11,10},{12... | collective-permute-start | bytes 37160 | tf_op jit(solution)/shard_map/ppermute | solution.py:15
  53.3 50.1 %copy-start.35 = (bf16[1,1,12,64]{3,1,2,0:T(2,128)(2,1)S(1)}, bf16[1,1,12,64]{3,1,2,0:T(2,128)(2,1)}, u32[]{:S(2)}) copy-start(bf16[1,1,12,64]{3,1,2,0:T(2,128)(2,1)} %get-tuple-element.30) | copy-start | bytes 4612
  83.9 23.8 %copy-start.8 = (bf16[2,12,8,128]{3,1,2,0:T(8,128)(2,1)}, bf16[2,12,8,128]{3,1,2,0:T(8,128)(2,1)S(1)}, u32[]{:S(2)}) copy-start(bf16[2,12,8,128]{3,1,2,0:T(8,128)(2,1)S(1)} %slice.240) | copy-start | bytes 147460
  83.9 20.7 %copy-start.34 = (bf16[1,1,12,64]{3,1,2,0:T(2,128)(2,1)S(1)}, bf16[1,1,12,64]{3,1,2,0:T(2,128)(2,1)}, u32[]{:S(2)}) copy-start(bf16[1,1,12,64]{3,1,2,0:T(2,128)(2,1)} %get-tuple-element.31) | copy-start | bytes 4612
  87.6 19.7 %copy-start.6 = (bf16[2,12,8,128]{3,1,2,0:T(8,128)(2,1)}, bf16[2,12,8,128]{3,1,2,0:T(8,128)(2,1)S(1)}, u32[]{:S(2)}) copy-start(bf16[2,12,8,128]{3,1,2,0:T(8,128)(2,1)S(1)} %slice.242) | copy-start | bytes 147460
  103.4 2.3 copy-start.14
  103.4 2.3 copy-start.33
  104.6 1.4 copy-start.32
  105.7 0.7 copy-start.31
  106.0 0.7 copy-start.30
  106.3 0.7 copy-start.29
  106.6 0.7 copy-start.28
  106.9 0.7 copy-start.27
  107.2 0.8 copy-start.10
  107.2 0.8 copy-start.26
  107.6 0.9 copy-start.11
  107.6 0.8 copy-start.25
  107.9 0.9 copy-start.15
  109.8 3.3 copy-start.13
  109.8 3.5 copy-start.12
  113.9 0.9 copy-start.9
  114.1 0.9 copy-start.7
  115.5 9.0 %collective-permute-start.4 = (bf16[2,64,8,1]{3,1,2,0:T(8,128)(2,1)S(1)}, bf16[2,64,8,1]{3,1,2,0:T(8,128)(2,1)S(1)}, u32[]{:S(2)}, u32[]{:S(2)}) collective-permute-start(bf16[2,64,8,1]{3,1,2,0:T(8,128)(2,1)S(1)} %get-tuple-element.15), channel_id=1, source_target_pairs={{0,8},{8,16},{16,24},{1,9},{9,17},{17,25},{2,10},{10,18},{18,26},{... | collective-permute-start | bytes 6152 | tf_op jit(solution)/shard_map/ppermute | solution.py:12
  119.9 13.1 %collective-permute-start.5 = (bf16[2,64,8,1]{3,1,2,0:T(8,128)(2,1)S(1)}, bf16[2,64,8,1]{3,1,2,0:T(8,128)(2,1)S(1)}, u32[]{:S(2)}, u32[]{:S(2)}) collective-permute-start(bf16[2,64,8,1]{3,1,2,0:T(8,128)(2,1)S(1)} %get-tuple-element.16), channel_id=1, source_target_pairs={{8,0},{16,8},{24,16},{9,1},{17,9},{25,17},{10,2},{18,10},{26,18},{... | collective-permute-start | bytes 6152 | tf_op jit(solution)/shard_map/ppermute | solution.py:15
  123.0 1.5 copy-start.23
  139.2 11.4 %collective-permute-start.6 = (bf16[2,64,1,130]{3,1,2,0:T(8,128)(2,1)S(1)}, bf16[2,64,1,130]{3,1,2,0:T(8,128)(2,1)S(1)}, u32[]{:S(2)}, u32[]{:S(2)}) collective-permute-start(bf16[2,64,1,130]{3,1,2,0:T(8,128)(2,1)S(1)} %get-tuple-element.11), channel_id=1, source_target_pairs={{0,1},{1,2},{2,3},{3,4},{4,5},{5,6},{6,7},{8,9},{9,10},{10,11},{11... | collective-permute-start | bytes 99848 | tf_op jit(solution)/shard_map/ppermute | solution.py:12
  143.0 7.7 %collective-permute-start.7 = (bf16[2,64,1,130]{3,1,2,0:T(8,128)(2,1)S(1)}, bf16[2,64,1,130]{3,1,2,0:T(8,128)(2,1)S(1)}, u32[]{:S(2)}, u32[]{:S(2)}) collective-permute-start(bf16[2,64,1,130]{3,1,2,0:T(8,128)(2,1)S(1)} %get-tuple-element.12), channel_id=1, source_target_pairs={{1,0},{2,1},{3,2},{4,3},{5,4},{6,5},{7,6},{9,8},{10,9},{11,10},{12... | collective-permute-start | bytes 99848 | tf_op jit(solution)/shard_map/ppermute | solution.py:15
  187.1 1.9 copy-start.21
  190.3 1.0 copy-start.2
  190.3 1.0 copy-start.3
  191.4 0.9 copy-start.4
  192.3 0.7 copy-start.41
  192.3 0.7 copy-start.43
  192.3 0.9 copy-start.37
  195.4 0.9 copy-start.20
  196.3 10.6 %copy-start.36 = (f32[768]{0:T(1024)S(1)}, f32[768]{0:T(1024)}, u32[]{:S(2)}) copy-start(f32[768]{0:T(1024)} %convert_element_type.51) | copy-start | bytes 9220
  198.4 52.6 %all-to-all-start = ((bf16[8,24,768]{2,1,0:T(8,128)(2,1)}), bf16[8,24,768]{2,1,0:T(8,128)(2,1)S(1)}, u32[]{:S(2)}, u32[]{:S(2)}) async-start(bf16[8,24,768]{2,1,0:T(8,128)(2,1)} %bitcast.105), calls=%async_computation | async-start | bytes 589824 | tf_op jit(solution)/shard_map/all_to_all | solution.py:121
  206.8 1.9 copy-start.24
  206.8 134.8 %all-reduce.4.cloned.1.call-start = ((), (), s32[]{:S(2)}) async-start(), calls=%async_computation.1 | async-start | bytes 1441792 | tf_op jit(solution)/shard_map/psum | solution.py:100
  207.9 0.8 copy-start.5
  341.5 2.3 copy-start.16
Sparse Core Ops, SparseCore 0:
  213.5 128.0 all-reduce.3
where the time goes:
time: 353 us; the launch traced here: 352 us
  local copies, waits for them, and re-layouts  137 us (39%)
  waiting for transfers between devices  101 us (29%)
  blocking collectives  41.3 us (12%)
  starting transfers between devices  28.2 us (8%)
  matrix products  23.8 us (7%)
  between operations  15.2 us (4%)
  other arithmetic  5.32 us (2%)
    slice x32, local copies, waits for them, and re-layouts, transpose_back(): padded[:, :, tap_y:tap_y + 2 * height:2, tap_x:tap_x + 2 * breadth:2]  126 us
    psum x1, waiting for transfers between devices, per_device(): lax.psum((grad_proj, grad_first, grad_second, mask_sum), ('ew', 'ns'))  90.6 us
    psum x1, blocking collectives, per_device(): lax.psum((grad_proj, grad_first, grad_second, mask_sum), ('ew', 'ns'))  41.3 us
    dot_general x32, matrix products, transpose_back(): jnp.einsum('oi,fohw->fihw', kernel[tap_y, tap_x], window, preferred_eleme...  15.5 us
    ppermute x4, starting transfers between devices, padded_2(): lax.ppermute(lax.slice_in_dim(block, block.shape[dim] - width, None, axis...  14.5 us
    ppermute x4, waiting for transfers between devices, padded_2(): lax.ppermute(lax.slice_in_dim(block, 0, width, axis=dim), axis, backward)  8.46 us
    all_to_all x1, starting transfers between devices, per_device(): lax.all_to_all(outgoing.reshape(owner_count, capacity, features), 'ns', s...  8.37 us
    unnamed x96, local copies, waits for them, and re-layouts  7.92 us
  transfers between devices with their start and end apart: 10, of which 3 were waited for; matrix products, arithmetic and copies ran while one was open for 7% of the time, Pallas kernels for 0%

commit v1 on v0

v1 whole, which is shorter than its diff:
```python
import functools

import jax
import jax.numpy as jnp
import numpy as np
from jax import lax
from jax.experimental import pallas as pl
from jax.experimental.pallas import tpu as pltpu
from jax.sharding import PartitionSpec as P

BF = jnp.bfloat16
F32 = jnp.float32
VMEM = pl.BlockSpec(memory_space=pltpu.VMEM)
GROUP = 16
GRAD_ROWS = 1024
PROJ_AT = 512
SECOND_AT = 896
MASK_ROW = SECOND_AT + 12


def nn(a, b):
    return lax.dot_general(a, b, (((1,), (0,)), ((), ())), preferred_element_type=F32)


def nt(a, b):
    return lax.dot_general(a, b, (((1,), (1,)), ((), ())), preferred_element_type=F32)


def tn(a, b):
    return lax.dot_general(a, b, (((0,), (0,)), ((), ())), preferred_element_type=F32)


def iota(shape, dim):
    return lax.broadcasted_iota(jnp.int32, shape, dim)


def one_hot(shape, pairs, shift=0):
    matrix = np.zeros(shape, np.float32)
    for row, col in pairs:
        matrix[row, col + shift] = 1.0
    return matrix


def column_tables(cols):
    half = cols // 2
    fine = 2 * cols

    def hidden_cols(arrangement):
        if arrangement == 0:
            return [2 * j for j in range(half)] + [2 * j + 1 for j in range(half)]
        return [2 * j + 2 for j in range(half)] + [2 * j - 1 for j in range(half)]

    def pixel_row(x):
        return x if 0 <= x < fine else (x if x >= fine else fine + 6 + x)

    def hidden_row(x):
        return x if 0 <= x <= cols else cols + 1

    pixels = np.zeros((fine + 128, 4 * 2 * cols), np.float32)
    cells = np.zeros((2 * cols, 2 * cols), np.float32)
    for arrangement in range(2):
        for lane, col in enumerate(hidden_cols(arrangement)):
            cells[hidden_row(col), arrangement * cols + lane] = 1.0
            for tap in range(4):
                pixels[pixel_row(2 * col + tap - 1), (tap * 2 + arrangement) * cols + lane] = 1.0
    return pixels, cells


def pack_kernel(cot_ref, pre_ref, edge_ref, g_ref, p_ref, own_ref, a_ref, b_ref, cot_wide, pre_wide):
    frames, bands, prow, pcol = cot_ref.shape
    _, chans, rows, cols = pre_ref.shape
    wide_rows = frames * GROUP * prow
    halves = range(pcol // cols)
    for f in range(frames):
        for o in range(GROUP):
            at = (f * GROUP + o) * prow
            band = cot_ref[f, o].astype(F32) if o < bands else jnp.zeros((prow, pcol), F32)
            for h in halves:
                cot_wide[pl.ds(h * wide_rows + at, prow), :] = band[:, h * cols : (h + 1) * cols]
        for c in range(chans):
            pre_wide[pl.ds((f * chans + c) * rows, rows), :] = pre_ref[f, c].astype(F32)
    for f in range(frames):
        for y in range(prow):
            for h in halves:
                g_ref[pl.ds((f * prow + y) * GROUP, GROUP), h * cols : (h + 1) * cols] = cot_wide[
                    pl.ds(h * wide_rows + f * GROUP * prow + y, GROUP, stride=prow), :
                ].astype(BF)
        for r in range(rows):
            p_ref[pl.ds((f * rows + r) * chans, chans), :] = pre_wide[
                pl.ds(f * chans * rows + r, chans, stride=rows), :
            ].astype(BF)
    pick_g = edge_ref[:, :pcol]
    pick_p = edge_ref[:, pcol:]
    edges_p = nt(pick_p, p_ref[...])
    edges_g = nt(pick_g, g_ref[...])
    width = edges_g.shape[1]
    own_ref[:, :width] = (edges_g + edges_p[:, :width]).astype(BF)
    own_ref[:, width:] = edges_p[:, width:].astype(BF)

    def message(out_ref, top):
        first = 0 if top else prow - 3
        line = 0 if top else rows - 1
        for f in range(frames):
            out_ref[pl.ds(f * 3 * GROUP, 3 * GROUP), :] = g_ref[
                pl.ds((f * prow + first) * GROUP, 3 * GROUP), :
            ]
            out_ref[pl.ds(frames * 3 * GROUP, chans), f * cols : (f + 1) * cols] = p_ref[
                pl.ds((f * rows + line) * chans, chans), :
            ]
        at = frames * 3 * GROUP + chans
        out_ref[pl.ds(at, 16), :] = jnp.zeros((16, pcol), BF)
        out_ref[pl.ds(at, 16), : frames * 3 * GROUP] = nt(
            pick_g, out_ref[pl.ds(0, frames * 3 * GROUP), :]
        ).astype(BF)
        for f in range(frames):
            out_ref[pl.ds(at, 16), cols + f * chans : cols + (f + 1) * chans] = nt(
                pick_p, p_ref[pl.ds((f * rows + line) * chans, chans), :]
            ).astype(BF)

    even = lax.rem(lax.axis_index("ns"), 2) == 0

    @pl.when(even)
    def _():
        message(a_ref, False)
        message(b_ref, True)

    @pl.when(jnp.logical_not(even))
    def _():
        message(a_ref, True)
        message(b_ref, False)


def token_kernel(
    capacity, ids_ref, tokens_ref, mask_ref, proj_ref, first_ref, second_ref,
    grid_ref, pick_ref, hidden_ref, route_ref, wab_ref, w2_ref,
):
    slots_all = tokens_ref.shape[0]
    frames, slots, patches = pick_ref.shape
    chans = proj_ref.shape[1]
    bands = second_ref.shape[2]
    owners = route_ref.shape[0] // GROUP
    half = capacity // 2
    eye = (iota((chans, chans), 0) == iota((chans, chans), 1)).astype(BF)
    pad = jnp.zeros((GROUP - bands, chans), BF)
    taps = []
    for b in range(4):
        for a in range(4):
            taps.append(jnp.concatenate([second_ref[a, b], pad], axis=0))
    w2_ref[...] = nt(eye, jnp.concatenate(taps, axis=0)).astype(BF)
    left = (iota((2 * chans, chans), 0) == iota((2 * chans, chans), 1)).astype(BF)
    right = (iota((2 * chans, chans), 0) == iota((2 * chans, chans), 1) + chans).astype(BF)
    for arrangement, (lo, hi) in enumerate(((1, 2), (3, 0))):
        taps_lo = jnp.concatenate([first_ref[a, lo] for a in range(4)], axis=0)
        taps_hi = jnp.concatenate([first_ref[a, hi] for a in range(4)], axis=0)
        wab_ref[:, arrangement * 4 * chans : (arrangement + 1) * 4 * chans] = (
            nt(left, taps_lo) + nt(right, taps_hi)
        ).astype(BF)
    vis = ids_ref[0:1, :]
    owner = ids_ref[1:2, :]
    live = ids_ref[2:3, :]
    wanted = jnp.where(live > 0, vis, patches)
    square = (slots_all, slots_all)
    column = jnp.sum(
        jnp.where(iota(square, 0) == iota(square, 1), wanted.astype(F32), 0.0), axis=1, keepdims=True
    ).astype(jnp.int32)
    token_proj = nn(tokens_ref[...], proj_ref[...]).astype(BF)
    mask_proj = nn(jnp.broadcast_to(mask_ref[...], (16, mask_ref.shape[1])), proj_ref[...]).astype(BF)
    row0 = iota((16, patches), 0) == 0
    lane = iota((chans, 2 * chans), 1)
    for f in range(frames):
        hits = iota((slots, patches), 1) == column[f * slots : (f + 1) * slots]
        picks = hits.astype(F32)
        pick_ref[f] = picks.astype(BF)
        unseen = jnp.where(row0, 1.0 - jnp.sum(picks, axis=0, keepdims=True), 0.0).astype(BF)
        hidden_ref[:, f * patches : (f + 1) * patches] = unseen
        grid = tn(token_proj[f * slots : (f + 1) * slots], picks.astype(BF)) + tn(mask_proj, unseen)
        for pair in range(patches // (2 * chans)):
            straight = grid[:, pair * 2 * chans : (pair + 1) * 2 * chans]
            turned = pltpu.roll(straight, chans, 1)
            k = f * (patches // (2 * chans)) + pair
            zero = jnp.zeros_like(straight)
            grid_ref[k, :chans, : 2 * chans] = jnp.where(lane < chans, straight, zero).astype(BF)
            grid_ref[k, chans:, : 2 * chans] = jnp.where(lane < chans, zero, turned).astype(BF)
            grid_ref[k, :chans, 2 * chans :] = jnp.where(lane < chans, turned, zero).astype(BF)
            grid_ref[k, chans:, 2 * chans :] = jnp.where(lane < chans, zero, straight).astype(BF)
    own_rows = -(-owners // 16) * 16
    hit = (iota((own_rows, slots_all), 0) == jnp.where(live > 0, owner, -1)).astype(F32)
    before = (iota(square, 0) < iota(square, 1)).astype(BF)
    earlier = nn(hit.astype(BF), before)
    place = jnp.sum(earlier * hit, axis=0, keepdims=True).astype(jnp.int32)
    for h in range(2):
        inside = (live > 0) & (place >= h * half) & (place < (h + 1) * half)
        target = jnp.where(inside, owner * GROUP + place - h * half, -1)
        route_ref[:, h * slots_all : (h + 1) * slots_all] = (
            iota((owners * GROUP, slots_all), 0) == target
        ).astype(F32).astype(BF)


def tile_kernel(
    n_ew, rows_each, g_ref, p_ref, ra_ref, rb_ref, ea_ref, eb_ref, pix_ref, cell_ref, halo_ref,
    grid_ref, pick_ref, hidden_ref, route_ref, wab_ref, w2_ref, tokens_ref, mask_ref,
    out_ref, ext, wide, wins, pres, deltas, routed,
):
    frames, slots, patches = pick_ref.shape
    chans = w2_ref.shape[0]
    pcol = g_ref.shape[1]
    cols = p_ref.shape[1]
    rows = p_ref.shape[0] // (frames * chans)
    prow = 2 * rows
    n_ns = route_ref.shape[0] // GROUP
    ns = lax.axis_index("ns")
    ew = lax.axis_index("ew")
    even_ns = lax.rem(ns, 2) == 0
    even_ew = lax.rem(ew, 2) == 0
    ra, rb = ra_ref[...], rb_ref[...]
    north = jnp.where(even_ns, rb, ra)
    south = jnp.where(even_ns, ra, rb)
    ea, eb = ea_ref[...], eb_ref[...]
    sides = jnp.concatenate([jnp.where(even_ew, ea, eb), jnp.where(even_ew, eb, ea)], axis=0)
    own_len = frames * rows * chans
    xa = sides[:, own_len : own_len + pcol]
    xb = sides[:, own_len + pcol : own_len + 2 * pcol]
    side_n = jnp.where(even_ns, xb, xa)
    side_s = jnp.where(even_ns, xa, xb)
    pick_g = halo_ref[:, :128]
    pick_p = halo_ref[:, 128:256]
    g_len = frames * prow * GROUP
    edge = frames * 3 * GROUP
    own_g = tn(sides[:, :g_len], pick_g).astype(BF)
    north_g = tn(side_n[:, :128], pick_g).astype(BF)
    south_g = tn(side_s[:, :128], pick_g).astype(BF)
    own_p = tn(sides[:, :own_len], pick_p).astype(BF)
    north_p = tn(side_n[:, 128:256], pick_p).astype(BF)
    south_p = tn(side_s[:, 128:256], pick_p).astype(BF)
    tall = (prow + 6) * GROUP
    high = (rows + 2) * chans
    for f in range(frames):
        base = f * tall
        top, mid, low = 3 * GROUP, prow * GROUP, 3 * GROUP
        ext[pl.ds(base, top), :pcol] = north[f * top : (f + 1) * top]
        ext[pl.ds(base, top), pcol:] = north_g[f * top : (f + 1) * top]
        ext[pl.ds(base + top, mid), :pcol] = g_ref[pl.ds(f * mid, mid), :]
        ext[pl.ds(base + top, mid), pcol:] = own_g[f * mid : (f + 1) * mid]
        ext[pl.ds(base + top + mid, low), :pcol] = south[f * low : (f + 1) * low]
        ext[pl.ds(base + top + mid, low), pcol:] = south_g[f * low : (f + 1) * low]
        base = f * high
        mid = rows * chans
        wide[pl.ds(base, chans), :cols] = north[edge : edge + chans, f * cols : (f + 1) * cols]
        wide[pl.ds(base, chans), cols:] = north_p[f * chans : (f + 1) * chans]
        wide[pl.ds(base + chans, mid), :cols] = p_ref[pl.ds(f * mid, mid), :]
        wide[pl.ds(base + chans, mid), cols:] = own_p[f * mid : (f + 1) * mid]
        wide[pl.ds(base + chans + mid, chans), :cols] = south[
            edge : edge + chans, f * cols : (f + 1) * cols
        ]
        wide[pl.ds(base + chans + mid, chans), cols:] = south_p[f * chans : (f + 1) * chans]
    for f in range(frames):
        block = ext[pl.ds(f * tall, tall), :]
        for b in range(4):
            lanes = slice(b * 2 * cols, (b + 1) * 2 * cols)
            wins[pl.ds(f * tall, tall), lanes] = nn(block, pix_ref[:, lanes]).astype(BF)
        pres[pl.ds(f * high, high), :] = nn(wide[pl.ds(f * high, high), :], cell_ref[...])
    w2 = w2_ref[...]
    lane = iota((chans, 2 * cols), 1)
    outside_col = ((lane == cols + cols // 2 - 1) & (ew == n_ew - 1)) | (
        (lane == cols + cols // 2) & (ew == 0)
    )
    zero = jnp.zeros((chans, cols), BF)
    grad_second = None
    for f in range(frames):
        for i in range(rows + 2):
            at = f * tall + 2 * i * GROUP
            taps = [wins[pl.ds(at, 4 * GROUP), b * 2 * cols : (b + 1) * 2 * cols] for b in range(4)]
            grad_hidden = nn(w2, jnp.concatenate(taps, axis=0))
            v = pres[pl.ds(f * high + i * chans, chans), :]
            s = 0.5 + 0.5 * jnp.tanh(0.851 * v)
            delta = grad_hidden * (s + 1.702 * v * s * (1.0 - s))
            drop = outside_col
            if i == 0:
                drop = drop | (ns == 0)
            if i == rows + 1:
                drop = drop | (ns == n_ns - 1)
            deltas[pl.ds(f * high + i * chans, chans), :] = jnp.where(drop, 0.0, delta).astype(BF)
            if 1 <= i <= rows:
                hid = (v[:, :cols] * s[:, :cols]).astype(BF)
                lhs = jnp.concatenate(
                    [
                        jnp.concatenate([taps[0][:, :cols], taps[2][:, :cols]], axis=1),
                        jnp.concatenate([taps[1][:, :cols], taps[3][:, :cols]], axis=1),
                    ],
                    axis=0,
                )
                rhs = jnp.concatenate(
                    [
                        jnp.concatenate([hid, zero], axis=1),
                        jnp.concatenate([zero, hid], axis=1),
                    ],
                    axis=0,
                )
                term = nt(lhs, rhs)
                grad_second = term if grad_second is None else grad_second + term
    wab = wab_ref[...]
    half_lane = iota((chans, cols), 1) < cols // 2
    grad_first = None
    grids = []
    for f in range(frames):
        parts = []
        for pair in range(rows // 4):
            cells = []
            for odd in range(2):
                at = f * high + (2 * pair + odd) * 2 * chans
                slab = deltas[pl.ds(at, 4 * chans), :]
                cells.append(jnp.concatenate([slab[:, :cols], slab[:, cols:]], axis=0))
            both = jnp.concatenate(cells, axis=1)
            term = nt(both, grid_ref[f * (rows // 4) + pair])
            grad_first = term if grad_first is None else grad_first + term
            turn = nn(wab, both)
            here = jnp.where(half_lane, turn[:chans, :cols], turn[chans:, cols:])
            there = jnp.where(half_lane, turn[:chans, cols:], turn[chans:, :cols])
            parts.append(here + pltpu.roll(there, cols // 2, 1))
        grids.append(jnp.concatenate(parts, axis=1).astype(BF))
    none = jnp.zeros((chans, patches), BF)
    mask_sum = nt(hidden_ref[...], jnp.concatenate(grids, axis=1))
    lower = [nt(pick_ref[f], jnp.concatenate([grids[f], none], axis=0)) for f in range(frames)]
    upper = [nt(pick_ref[f], jnp.concatenate([none, grids[f]], axis=0)) for f in range(frames)]
    chosen = jnp.concatenate(lower + upper, axis=0).astype(BF)
    routed[...] = nn(route_ref[...], chosen).astype(BF)
    features = tokens_ref.shape[1]
    tokens = tokens_ref[...]
    split = jnp.concatenate([tokens[:, : features // 2], tokens[:, features // 2 :]], axis=0)
    hi = mask_sum.astype(BF).astype(F32)
    lo = mask_sum - hi
    nothing = jnp.zeros_like(hi)
    hi_left = jnp.concatenate([hi, nothing], axis=1)[0:1]
    hi_right = jnp.concatenate([nothing, hi], axis=1)[0:1]
    lo_left = jnp.concatenate([lo, nothing], axis=1)[0:1]
    lo_right = jnp.concatenate([nothing, lo], axis=1)[0:1]
    line = iota((16, 2 * chans), 0)
    mask_rows = jnp.where(line == 0, hi_left, 0.0) + jnp.where(line == 1, hi_right, 0.0)
    mask_rows = mask_rows + jnp.where(line == 2, lo_left, 0.0) + jnp.where(line == 3, lo_right, 0.0)
    mask_token = mask_ref[...].astype(F32)
    line = iota((16, features // 2), 0)
    spread = jnp.where(
        (line == 0) | (line == 2),
        mask_token[:, : features // 2],
        jnp.where((line == 1) | (line == 3), mask_token[:, features // 2 :], 0.0),
    )
    grad_proj = tn(split, chosen) + tn(spread.astype(BF), mask_rows.astype(BF))
    mark = iota(grad_second.shape, 0) == MASK_ROW - SECOND_AT
    grad_second = jnp.where(mark, hi_left + lo_right, grad_second)
    total = jnp.concatenate([grad_first, grad_proj, grad_second], axis=0).astype(BF)
    count = out_ref.shape[0]
    for d in range(GRAD_ROWS // rows_each):
        out_ref[d, :rows_each, :] = total[d * rows_each : (d + 1) * rows_each]
    if count * rows_each > GRAD_ROWS:

        @pl.loop(GRAD_ROWS // rows_each, count)
        def _(d):
            out_ref[d, :rows_each, :] = jnp.zeros((rows_each, 2 * chans), BF)

    def place(d):
        source = pl.multiple_of(lax.rem(d, n_ns) * GROUP, GROUP)
        out_ref[d, rows_each:, :] = routed[pl.ds(source, GROUP), :]

    if count <= 64:
        for d in range(count):
            out_ref[d, rows_each:, :] = routed[pl.ds((d % n_ns) * GROUP, GROUP), :]
    else:
        pl.loop(0, count)(place)


def owner_kernel(n_ns, capacity, rows_each, got_ref, proj_ref, sum_ref, token_ref):
    count = got_ref.shape[0]
    chans = proj_ref.shape[1]
    if count <= 64:
        total = got_ref[0, :rows_each, :].astype(F32)
        for d in range(1, count):
            total = total + got_ref[d, :rows_each, :].astype(F32)
    else:
        total = lax.fori_loop(
            0,
            count,
            lambda d, acc: acc + got_ref[d, :rows_each, :].astype(F32),
            jnp.zeros((rows_each, 2 * chans), F32),
        )
    share = total.astype(BF)
    if count <= 64:
        for d in range(count):
            sum_ref[d] = share
    else:

        @pl.loop(0, count)
        def _(d):
            sum_ref[d] = share

    half = capacity // 2
    ew = lax.axis_index("ew")
    arrived = jnp.concatenate(
        [got_ref[ew * n_ns + s, rows_each:, :] for s in range(n_ns)], axis=0
    )
    shape = (n_ns * capacity, n_ns * GROUP)
    row, col = iota(shape, 0), iota(shape, 1)
    slot = lax.rem(row, capacity)
    source = (row // capacity) * GROUP + lax.rem(slot, half)
    picked = nn((source == col).astype(F32).astype(BF), arrived)
    second = lax.rem(iota(picked.shape, 0), capacity) >= half
    picked = jnp.where(second, pltpu.roll(picked, chans, 1), picked)[:, :chans].astype(BF)
    token_ref[...] = nt(picked, proj_ref[...]).astype(BF)


def finish_kernel(got_ref, proj_ref, proj_out, first_out, second_out, mask_out):
    chans = proj_ref.shape[1]
    bands = second_out.shape[2]
    rows_each = got_ref.shape[1]
    parts = [got_ref[d] for d in range(GRAD_ROWS // rows_each)]
    total = jnp.concatenate(parts, axis=0).astype(F32)
    turned = pltpu.roll(total, chans, 1)
    low, high = total[:, :chans], turned[:, :chans]
    for arrangement, taps in enumerate(((1, 2), (3, 0))):
        for a in range(4):
            at = (arrangement * 4 + a) * chans
            first_out[a, taps[0]] = low[at : at + chans]
            first_out[a, taps[1]] = high[at : at + chans]
    features = proj_ref.shape[0]
    proj_out[: features // 2, :] = low[PROJ_AT : PROJ_AT + features // 2]
    proj_out[features // 2 :, :] = high[PROJ_AT : PROJ_AT + features // 2]
    for b in range(2):
        for a in range(4):
            at = SECOND_AT + (b * 4 + a) * GROUP
            second_out[a, b] = low[at : at + bands]
            second_out[a, b + 2] = high[at : at + bands]
    mask_sum = low[MASK_ROW : MASK_ROW + 1] + high[MASK_ROW : MASK_ROW + 1]
    hi = mask_sum.astype(BF).astype(F32)
    mid = (mask_sum - hi).astype(BF).astype(F32)
    lo = mask_sum - hi - mid
    line = iota((16, chans), 0)
    rows = jnp.where(line == 0, hi, 0.0) + jnp.where(line == 1, mid, 0.0) + jnp.where(line == 2, lo, 0.0)
    mask_out[...] = jnp.sum(nt(rows.astype(BF), proj_ref[...]), axis=0, keepdims=True)


def swap(block, axis, offset):
    count = lax.axis_size(axis)
    pairs = [(i, ((i + offset) ^ 1) - offset) for i in range(count)]
    return lax.ppermute(block, axis, [(i, j) for i, j in pairs if 0 <= j < count])


def call(kernel, outs, args, scratch=(), flops=0, limit=None):
    return pl.pallas_call(
        kernel,
        out_shape=outs,
        in_specs=[VMEM] * len(args),
        out_specs=jax.tree.map(lambda _: VMEM, outs),
        scratch_shapes=list(scratch),
        compiler_params=pltpu.CompilerParams(vmem_limit_bytes=limit),
        cost_estimate=pl.CostEstimate(flops=flops, bytes_accessed=1 << 20, transcendentals=0),
    )(*args)


def per_device(
    n_ew, n_ns, tokens, vis_index, counts, owners, mask_token, proj_weight, up_first, up_second, saved_pre, cotangent
):
    frames, slots, features = tokens.shape[2:]
    _, chans, rows, cols = saved_pre.shape
    prow, pcol = cotangent.shape[2:]
    patches = rows * cols // 4
    count = n_ew * n_ns
    capacity = 3 * frames * slots // (2 * n_ns)
    rows_each = -(-GRAD_ROWS // count)
    rows_each = -(-rows_each // 16) * 16
    slots_all = frames * slots
    shape = jax.ShapeDtypeStruct

    pixels, cells = column_tables(cols)
    pixels, cells = jnp.asarray(pixels, BF), jnp.asarray(cells, BF)
    edge_pairs = [(0, 0), (1, 1), (2, 2), (3, pcol - 3), (4, pcol - 2), (5, pcol - 1)]
    edge_pairs += [(8, pcol), (9, pcol + cols - 1)]
    edges = jnp.asarray(one_hot((16, pcol + cols), edge_pairs), BF)
    halo_pairs = [(0, 0), (1, 1), (2, 2), (16 + 3, 3), (16 + 4, 4), (16 + 5, 5)]
    halo_pairs += [(8, 128), (16 + 9, 129)]
    halos = jnp.asarray(one_hot((32, 256), halo_pairs), BF)

    msg_rows = frames * 3 * GROUP + chans + 16
    own_g, own_p, own_edges, send_a, send_b = call(
        pack_kernel,
        (
            shape((frames * prow * GROUP, pcol), BF),
            shape((frames * rows * chans, cols), BF),
            shape((16, frames * rows * chans), BF),
            shape((msg_rows, pcol), BF),
            shape((msg_rows, pcol), BF),
        ),
        (cotangent, saved_pre, edges),
        [
            pltpu.VMEM((frames * GROUP * prow * pcol // cols, cols), F32),
            pltpu.VMEM((frames * chans * rows, cols), F32),
        ],
        flops=1 << 22,
    )
    got_a = swap(send_a, "ns", 0)
    got_b = swap(send_b, "ns", 1)

    live = jnp.arange(slots, dtype=jnp.int32)[None, :] < counts[0, 0][:, None]
    ids = jnp.stack(
        [
            vis_index.reshape(slots_all),
            owners.reshape(slots_all),
            live.astype(jnp.int32).reshape(slots_all),
        ]
    )
    ids = jnp.concatenate([ids, jnp.zeros((5, slots_all), jnp.int32)], axis=0)
    tile_tokens = tokens.reshape(slots_all, features)
    mask_row = mask_token.reshape(1, features)
    grid, picks, hidden, route, wab, w2 = call(
        functools.partial(token_kernel, capacity),
        (
            shape((frames * rows // 4, 2 * chans, 2 * cols), BF),
            shape((frames, slots, patches), BF),
            shape((16, frames * patches), BF),
            shape((n_ns * GROUP, 2 * slots_all), BF),
            shape((2 * chans, 8 * chans), BF),
            shape((chans, 16 * GROUP), BF),
        ),
        (ids, tile_tokens, mask_row, proj_weight, up_first, up_second),
        flops=1 << 24,
    )

    side = jnp.concatenate([own_edges, got_a[msg_rows - 16 :], got_b[msg_rows - 16 :]], axis=1)
    side_a = swap(side, "ew", 0)
    side_b = swap(side, "ew", 1)

    outgoing = call(
        functools.partial(tile_kernel, n_ew, rows_each),
        shape((count, rows_each + GROUP, 2 * chans), BF),
        (
            own_g, own_p, got_a, got_b, side_a, side_b, pixels, cells, halos,
            grid, picks, hidden, route, wab, w2, tile_tokens, mask_row,
        ),
        [
            pltpu.VMEM((frames * (prow + 6) * GROUP, pcol + 128), BF),
            pltpu.VMEM((frames * (rows + 2) * chans, 2 * cols), BF),
            pltpu.VMEM((frames * (prow + 6) * GROUP, 8 * cols), BF),
            pltpu.VMEM((frames * (rows + 2) * chans, 2 * cols), F32),
            pltpu.VMEM((frames * (rows + 2) * chans, 2 * cols), BF),
            pltpu.VMEM((n_ns * GROUP, 2 * chans), BF),
        ],
        flops=1 << 28,
        limit=40 << 20,
    )
    arrived = lax.all_to_all(outgoing, ("ew", "ns"), 0, 0, tiled=True)
    shares, token_grad = call(
        functools.partial(owner_kernel, n_ns, capacity, rows_each),
        (
            shape((count, rows_each, 2 * chans), BF),
            shape((n_ns * capacity, features), BF),
        ),
        (arrived, proj_weight),
        flops=1 << 24,
        limit=40 << 20,
    )
    summed = lax.all_to_all(shares, ("ew", "ns"), 0, 0, tiled=True)
    summed = summed[: GRAD_ROWS // rows_each]
    grad_proj, grad_first, grad_second, grad_mask = call(
        finish_kernel,
        (
            shape((features, chans), F32),
            shape((4, 4, chans, chans), F32),
            shape((4, 4, up_second.shape[2], chans), F32),
            shape((1, features), F32),
        ),
        (summed, proj_weight),
        flops=1 << 20,
    )
    return (token_grad[None, None], grad_proj, grad_first, grad_second, grad_mask.reshape(features))


def solution(mesh):
    return jax.shard_map(
        functools.partial(per_device, mesh.shape["ew"], mesh.shape["ns"]),
        mesh=mesh,
        in_specs=(
            P("ns", "ew", None, None, None),
            P("ns", "ew", None, None),
            P("ns", "ew", None),
            P("ns", "ew", None, None, None),
            P(),
            P(),
            P(),
            P(),
            P(None, None, "ns", "ew"),
            P(None, None, "ns", "ew"),
        ),
        out_specs=(P("ns", "ew", None, None), P(), P(), P(), P()),
        check_vma=False,
    )
```

time: 353 us -> 71.1 us (0.20)
  local copies, waits for them, and re-layouts: 137 us -> 14.2 us
  waiting for transfers between devices: 101 us -> 0.01 us
  matrix products: 23.8 us -> 0 us
  starting transfers between devices: 28.2 us -> 7.05 us
  between operations: 15.2 us -> 0.77 us
  Pallas kernels: 0 us -> 11.4 us
  blocking collectives: 41.3 us -> 32.7 us
    slice x37 -> x2, local copies, waits for them, and re-layouts: 127 us -> 0.01 us  [the longest x1 0.01 us: per_device(): got_a[msg_rows - 16:]]
    psum x1 -> x0, waiting for transfers between devices: 90.6 us -> none  [per_device(): lax.psum((grad_proj, grad_first, grad_second, mask_sum), ('ew', 'ns'))]
    psum x1 -> x0, blocking collectives: 41.3 us -> none  [per_device(): lax.psum((grad_proj, grad_first, grad_second, mask_sum), ('ew', 'ns'))]
    all_to_all x0 -> x2, blocking collectives: none -> 32.7 us  [the longest x1 20 us: per_device(): arrived = lax.all_to_all(outgoing, ('ew', 'ns'), 0, 0, tiled=True)]
    dot_general x71 -> x0, matrix products: 23.8 us -> none  [the longest x32 15.5 us: transpose_back(): jnp.einsum('oi,fohw->fihw', kernel[tap_y, tap_x], window, preferred_eleme...]
    ppermute x8 -> x4, starting transfers between devices: 19.8 us -> 7.05 us  [swap(): lax.ppermute(block, axis, [(i, j) for i, j in pairs if 0 <= j < count])]
    pallas_call x0 -> x5, Pallas kernels: none -> 11.4 us  [call(): pl.pallas_call(kernel, out_shape=outs, in_specs=[VMEM] * len(args), out_s...]
    ppermute x8 -> x4, waiting for transfers between devices: 9.99 us -> 0.01 us  [swap(): lax.ppermute(block, axis, [(i, j) for i, j in pairs if 0 <= j < count])]
  transfers between devices with their start and end apart: 10 -> 4, of which waited for: 3 -> 0; matrix products, arithmetic and copies ran while one was open for 7% -> 12% of each run, Pallas kernels for 0% -> 4%
where the time goes in v1:
time: 71.1 us; the launch traced here: 70.3 us
  blocking collectives  32.7 us (46%)
  local copies, waits for them, and re-layouts  14.2 us (20%)
  Pallas kernels  11.4 us (16%)
  starting transfers between devices  7.05 us (10%)
  other arithmetic  4.1 us (6%)
  between operations  0.77 us (1%)
    all_to_all x1, blocking collectives, per_device(): arrived = lax.all_to_all(outgoing, ('ew', 'ns'), 0, 0, tiled=True)  20 us
    all_to_all x1, blocking collectives, per_device(): summed = lax.all_to_all(shares, ('ew', 'ns'), 0, 0, tiled=True)  12.8 us
    unnamed x37, local copies, waits for them, and re-layouts  11.9 us
    pallas_call x5, Pallas kernels, call(): pl.pallas_call(kernel, out_shape=outs, in_specs=[VMEM] * len(args), out_s...  11.4 us
    ppermute x4, starting transfers between devices, swap(): lax.ppermute(block, axis, [(i, j) for i, j in pairs if 0 <= j < count])  7.05 us
  transfers between devices with their start and end apart: 4, of which 0 were waited for; matrix products, arithmetic and copies ran while one was open for 12% of the time, Pallas kernels for 4%

profile of v1, /device:TPU:0, one launch (start us, length us, event | category | flops | bytes accessed | tf_op | source)
XLA Modules:
  0.0 70.3 jit_solution(13004878713013372556)
XLA Ops:
  0.6 0.0 copy-start.2
  0.6 2.7 %shard_map.173 = (bf16[512,256]{1,0:T(8,128)(2,1)}, bf16[1024,128]{1,0:T(8,128)(2,1)}, bf16[16,1024]{1,0:T(8,128)(2,1)}, bf16[176,256]{1,0:T(8,128)(2,1)}, bf16[176,256]{1,0:T(8,128)(2,1)}) custom-call(bf16[2,12,16,256]{3,2,1,0:T(8,128)(2,1)} %cot_ref.1, bf16[2,64,8,128]{3,2,1,0:T(8,128)(2,1)} %pre_ref.1, bf16[16,384]{1,0:T(8,128)(2,1)} %constant.12.clone.edge_ref), custom_call_target="tpu_custom_call" | custom-call | flops 4194304 | bytes 1048576 | tf_op jit(solution)/shard_map/pallas_call | solution.py:447
  3.3 0.5 collective-permute-start
  3.8 0.7 collective-permute-start.1
  4.5 0.7 %compare_convert_fusion = s32[2,64]{1,0:T(2,128)S(1)} fusion(s32[2]{0:T(128)} %bitcast.7), kind=kLoop, calls=%fused_computation.2 | loop fusion | flops 256 | bytes 520 | tf_op jit(solution)/shard_map/convert_element_type | solution.py:506
  5.2 0.8 %stack_reshape.7 = s32[1,128]{1,0:T(1,128)S(1)} reshape(s32[1,1,2,64]{3,2,1,0:T(2,128)} %param.15) | data formatting | bytes 1024 | tf_op jit(solution)/shard_map/stack;reshape | solution.py:502
  6.0 0.5 broadcast.10
  6.5 1.3 %reduce.4 = s32[2,64]{1,0:T(2,128)S(1)} reduce(s32[1,1,2,64,1]{3,4,2,1,0:T(1,128)} %param.17, s32[]{:T(128)} %broadcast.10), dimensions={0,1,4}, to_apply=%param.17.reduce_sub_computation.3 | reduce | bytes 1028 | tf_op args[3]
  7.8 0.1 stack_reshape.8
  7.9 0.1 pad.3.clone
  8.0 0.1 reshape.50
  8.1 0.0 collective-permute-done.ra_ref
  8.1 0.0 collective-permute-done.1.rb_ref
  8.1 0.8 %pad_maximum_fusion = bf16[16,1536]{1,0:T(8,128)(2,1)S(1)} fusion(bf16[16,256]{1,0:T(8,128)(2,1)S(1)} %slice.9, bf16[16,256]{1,0:T(8,128)(2,1)S(1)} %slice.8, bf16[16,1024]{1,0:T(8,128)(2,1)} %get-tuple-element.26), kind=kLoop, calls=%fused_computation | loop fusion | flops 147456 | bytes 98304 | tf_op jit(solution)/shard_map/concatenate | solution.py:526
  8.9 0.7 collective-permute-start.3
  9.5 5.3 %collective-permute-start.2 = (bf16[16,1536]{1,0:T(8,128)(2,1)S(1)}, bf16[16,1536]{1,0:T(8,128)(2,1)S(1)}, u32[]{:S(2)}, u32[]{:S(2)}) collective-permute-start(bf16[16,1536]{1,0:T(8,128)(2,1)S(1)} %pad_maximum_fusion), channel_id=1, source_target_pairs={{0,8},{8,0},{16,24},{24,16},{1,9},{9,1},{17,25},{25,17},{2,10},{10... | collective-permute-start | bytes 147464 | tf_op jit(solution)/shard_map/ppermute | solution.py:443
  14.8 0.7 add_add_fusion.ids_ref
  15.4 1.3 %reshape.48.mask_ref = bf16[1,768]{1,0:T(2,128)(2,1)} reshape(bf16[768]{0:T(1024)(128)(2,1)} %param.18) | data formatting | bytes 3072 | tf_op jit(solution)/shard_map/reshape | solution.py:511
  16.7 1.4 %copy.20.second_ref = bf16[4,4,12,64]{3,2,1,0:T(8,128)(2,1)} copy(bf16[4,4,12,64]{3,1,2,0:T(4,128)(2,1)} %param.21) | data formatting | bytes 49152 | tf_op args[7]
  18.2 0.0 copy-start.6
  18.2 1.7 %copy.19.proj_ref = bf16[768,64]{1,0:T(8,128)(2,1)} copy(bf16[768,64]{0,1:T(8,128)(2,1)} %param.19) | data formatting | bytes 196608 | tf_op args[5]
  19.9 0.0 copy-start.1
  19.9 0.0 copy-start.3
  19.9 0.0 copy-start.4
  19.9 0.0 copy-start.12
  19.9 2.6 %shard_map.174 = (bf16[4,128,256]{2,1,0:T(8,128)(2,1)}, bf16[2,64,256]{2,1,0:T(8,128)(2,1)}, bf16[16,512]{1,0:T(8,128)(2,1)}, bf16[128,256]{1,0:T(8,128)(2,1)}, ...) custom-call(s32[8,128]{1,0:T(8,128)} %add_add_fusion.ids_ref, bf16[128,768]{1,0:T(8,128)(2,1)} %bitcast.4, ...), custom_call_target="tpu_custom_call" | custom-call | flops 16777216 | bytes 1048576 | tf_op jit(solution)/shard_map/pallas_call | solution.py:447
  22.5 0.0 collective-permute-done.3.eb_ref
  22.5 0.0 collective-permute-done.2.ea_ref
  22.5 0.0 copy-start.11
  22.5 0.0 copy-done.2
  22.5 0.0 copy-done.6
  22.5 0.0 copy-done.1
  22.5 0.0 copy-done.3
  22.6 0.0 copy-done.4
  22.6 0.0 copy-done.12
  22.6 0.6 copy-done.11
  23.2 0.0 copy-start.5
  23.2 0.9 %copy-done.5 = bf16[4,128,256]{2,1,0:T(8,128)(2,1)S(1)} copy-done((bf16[4,128,256]{2,1,0:T(8,128)(2,1)S(1)}, bf16[4,128,256]{2,1,0:T(8,128)(2,1)}, u32[]{:S(2)}) %copy-start.5) | copy-done | bytes 262168
  24.1 0.0 copy-start.7
  24.1 0.9 %copy-done.7 = bf16[128,512]{1,0:T(8,128)(2,1)S(1)} copy-done((bf16[128,512]{1,0:T(8,128)(2,1)S(1)}, bf16[128,512]{1,0:T(8,128)(2,1)}, u32[]{:S(2)}) %copy-start.7) | copy-done | bytes 131096
  25.0 0.0 copy-start.8
  25.0 0.8 %copy-done.8 = bf16[2,64,256]{2,1,0:T(8,128)(2,1)S(1)} copy-done((bf16[2,64,256]{2,1,0:T(8,128)(2,1)S(1)}, bf16[2,64,256]{2,1,0:T(8,128)(2,1)}, u32[]{:S(2)}) %copy-start.8) | copy-done | bytes 65560
  25.9 0.0 copy-start.9
  25.9 0.8 %copy-done.9 = bf16[128,256]{1,0:T(8,128)(2,1)S(1)} copy-done((bf16[128,256]{1,0:T(8,128)(2,1)S(1)}, bf16[128,256]{1,0:T(8,128)(2,1)}, u32[]{:S(2)}) %copy-start.9) | copy-done | bytes 65560
  26.7 0.0 copy-start.10
  26.7 0.8 %copy-done.10 = bf16[64,256]{1,0:T(8,128)(2,1)S(1)} copy-done((bf16[64,256]{1,0:T(8,128)(2,1)S(1)}, bf16[64,256]{1,0:T(8,128)(2,1)}, u32[]{:S(2)}) %copy-start.10) | copy-done | bytes 32792
  27.5 0.0 copy-start.13
  27.5 0.7 %copy-done.13 = bf16[16,512]{1,0:T(8,128)(2,1)S(1)} copy-done((bf16[16,512]{1,0:T(8,128)(2,1)S(1)}, bf16[16,512]{1,0:T(8,128)(2,1)}, u32[]{:S(2)}) %copy-start.13) | copy-done | bytes 16408
  28.2 2.9 %shard_map.175 = bf16[32,48,128]{2,1,0:T(8,128)(2,1)S(1)} custom-call(bf16[512,256]{1,0:T(8,128)(2,1)S(1)} %copy-done.3, bf16[1024,128]{1,0:T(8,128)(2,1)S(1)} %copy-done.4, bf16[176,256]{1,0:T(8,128)(2,1)S(1)} %collective-permute-done.ra_ref, bf16[176,256]{1,0:T(8,128)(2,1)S(1)} %collective-permute-done.1.rb_ref, ...), custom_call_target="tpu_custom_call" | custom-call | flops 268435456 | bytes 1048576 | tf_op jit(solution)/shard_map/pallas_call | solution.py:447
  31.1 0.0 copy-start
  31.1 20.0 %all_to_all.10.got_ref = bf16[32,48,128]{2,1,0:T(8,128)(2,1)S(1)} all-to-all(bf16[32,48,128]{2,1,0:T(8,128)(2,1)S(1)} %shard_map.175), channel_id=1, replica_groups=mesh['ew'=4,'ns'=8] {'ew','ns'}, dimensions={0} | all-to-all | bytes 786432 | tf_op jit(solution)/shard_map/all_to_all | solution.py:548
  51.1 0.0 copy-done
  51.1 1.2 %shard_map.176 = (bf16[32,32,128]{2,1,0:T(8,128)(2,1)S(1)}, bf16[192,768]{1,0:T(8,128)(2,1)}) custom-call(bf16[32,48,128]{2,1,0:T(8,128)(2,1)S(1)} %all_to_all.10.got_ref, bf16[768,64]{1,0:T(8,128)(2,1)S(1)} %copy-done), custom_call_target="tpu_custom_call" | custom-call | flops 16777216 | bytes 1048576 | tf_op jit(solution)/shard_map/pallas_call | solution.py:447
  52.3 12.8 %all_to_all.11.got_ref = bf16[32,32,128]{2,1,0:T(8,128)(2,1)} all-to-all(bf16[32,32,128]{2,1,0:T(8,128)(2,1)S(1)} %get-tuple-element.34), channel_id=1, replica_groups=mesh['ew'=4,'ns'=8] {'ew','ns'}, dimensions={0} | all-to-all | bytes 524288 | tf_op jit(solution)/shard_map/all_to_all | solution.py:559
  65.0 2.1 %shard_map.177 = (f32[768,64]{1,0:T(8,128)}, f32[4,4,64,64]{3,2,1,0:T(8,128)}, f32[4,4,12,64]{3,2,1,0:T(8,128)}, f32[1,768]{1,0:T(1,128)}) custom-call(bf16[32,32,128]{2,1,0:T(8,128)(2,1)} %all_to_all.11.got_ref, bf16[768,64]{1,0:T(8,128)(2,1)} %copy.19.proj_ref), custom_call_target="tpu_custom_call" | custom-call | flops 1048576 | bytes 1048576 | tf_op jit(solution)/shard_map/pallas_call | solution.py:447
  67.1 0.0 copy-start.14
  67.1 1.9 %copy.23 = f32[768,64]{0,1:T(8,128)} copy(f32[768,64]{1,0:T(8,128)} %get-tuple-element.40) | data formatting | bytes 393216
  69.0 0.0 copy-done.14
  69.0 0.0 copy-start.15
  69.0 0.7 copy.24
  69.7 0.0 copy-done.15
  69.7 0.6 reduce.1
  (3 shorter events, 0.0 us)
Async XLA Ops:
  0.6 21.9 %copy-start.2 = (bf16[384,1024]{1,0:T(8,128)(2,1)S(1)}, bf16[384,1024]{1,0:T(8,128)(2,1)}, u32[]{:S(2)}) copy-start(bf16[384,1024]{1,0:T(8,128)(2,1)} %constant.10.clone.pix_ref) | copy-start | bytes 2359300
  3.3 4.7 %collective-permute-start = (bf16[176,256]{1,0:T(8,128)(2,1)}, bf16[176,256]{1,0:T(8,128)(2,1)S(1)}, u32[]{:S(2)}, u32[]{:S(2)}) collective-permute-start(bf16[176,256]{1,0:T(8,128)(2,1)} %get-tuple-element.24), channel_id=1, source_target_pairs={{0,1},{1,0},{2,3},{3,2},{4,5},{5,4},{6,7},{7,6},{8,9},{9,8},{10,11... | collective-permute-start | bytes 270344 | tf_op jit(solution)/shard_map/ppermute | solution.py:443
  3.8 4.3 %collective-permute-start.1 = (bf16[176,256]{1,0:T(8,128)(2,1)}, bf16[176,256]{1,0:T(8,128)(2,1)S(1)}, u32[]{:S(2)}, u32[]{:S(2)}) collective-permute-start(bf16[176,256]{1,0:T(8,128)(2,1)} %get-tuple-element.25), channel_id=1, source_target_pairs={{1,2},{2,1},{3,4},{4,3},{5,6},{6,5},{9,10},{10,9},{11,12},{12,11},... | collective-permute-start | bytes 270344 | tf_op jit(solution)/shard_map/ppermute | solution.py:443
  8.9 13.6 %collective-permute-start.3 = (bf16[16,1536]{1,0:T(8,128)(2,1)S(1)}, bf16[16,1536]{1,0:T(8,128)(2,1)S(1)}, u32[]{:S(2)}, u32[]{:S(2)}) collective-permute-start(bf16[16,1536]{1,0:T(8,128)(2,1)S(1)} %pad_maximum_fusion), channel_id=1, source_target_pairs={{8,16},{16,8},{9,17},{17,9},{10,18},{18,10},{11,19},{19,11},{12,20... | collective-permute-start | bytes 147464 | tf_op jit(solution)/shard_map/ppermute | solution.py:443
  9.5 13.0 %collective-permute-start.2 = (bf16[16,1536]{1,0:T(8,128)(2,1)S(1)}, bf16[16,1536]{1,0:T(8,128)(2,1)S(1)}, u32[]{:S(2)}, u32[]{:S(2)}) collective-permute-start(bf16[16,1536]{1,0:T(8,128)(2,1)S(1)} %pad_maximum_fusion), channel_id=1, source_target_pairs={{0,8},{8,0},{16,24},{24,16},{1,9},{9,1},{17,25},{25,17},{2,10},{10... | collective-permute-start | bytes 147464 | tf_op jit(solution)/shard_map/ppermute | solution.py:443
  18.2 4.4 %copy-start.6 = (bf16[256,256]{1,0:T(8,128)(2,1)S(1)}, bf16[256,256]{1,0:T(8,128)(2,1)}, u32[]{:S(2)}) copy-start(bf16[256,256]{1,0:T(8,128)(2,1)} %constant.11.clone.cell_ref) | copy-start | bytes 393220
  19.9 2.6 %copy-start.1 = (bf16[1,1,2,64,768]{4,3,2,1,0:T(8,128)(2,1)S(1)}, bf16[1,1,2,64,768]{4,3,2,1,0:T(8,128)(2,1)}, u32[]{:S(2)}) copy-start(bf16[1,1,2,64,768]{4,3,2,1,0:T(8,128)(2,1)} %param.14) | copy-start | bytes 589828
  19.9 2.6 %copy-start.3 = (bf16[512,256]{1,0:T(8,128)(2,1)S(1)}, bf16[512,256]{1,0:T(8,128)(2,1)}, u32[]{:S(2)}) copy-start(bf16[512,256]{1,0:T(8,128)(2,1)} %get-tuple-element.22.g_ref) | copy-start | bytes 786436
  19.9 2.7 %copy-start.4 = (bf16[1024,128]{1,0:T(8,128)(2,1)S(1)}, bf16[1024,128]{1,0:T(8,128)(2,1)}, u32[]{:S(2)}) copy-start(bf16[1024,128]{1,0:T(8,128)(2,1)} %get-tuple-element.23.p_ref) | copy-start | bytes 786436
  19.9 2.7 %copy-start.12 = (bf16[32,256]{1,0:T(8,128)(2,1)S(1)}, bf16[32,256]{1,0:T(8,128)(2,1)}, u32[]{:S(2)}) copy-start(bf16[32,256]{1,0:T(8,128)(2,1)} %constant.13.clone.halo_ref) | copy-start | bytes 49156
  22.5 0.7 copy-start.11
  23.2 0.9 %copy-start.5 = (bf16[4,128,256]{2,1,0:T(8,128)(2,1)S(1)}, bf16[4,128,256]{2,1,0:T(8,128)(2,1)}, u32[]{:S(2)}) copy-start(bf16[4,128,256]{2,1,0:T(8,128)(2,1)} %get-tuple-element.27.grid_ref) | copy-start | bytes 786436
  24.1 0.9 %copy-start.7 = (bf16[128,512]{1,0:T(8,128)(2,1)S(1)}, bf16[128,512]{1,0:T(8,128)(2,1)}, u32[]{:S(2)}) copy-start(bf16[128,512]{1,0:T(8,128)(2,1)} %get-tuple-element.31.wab_ref) | copy-start | bytes 393220
  25.0 0.8 %copy-start.8 = (bf16[2,64,256]{2,1,0:T(8,128)(2,1)S(1)}, bf16[2,64,256]{2,1,0:T(8,128)(2,1)}, u32[]{:S(2)}) copy-start(bf16[2,64,256]{2,1,0:T(8,128)(2,1)} %get-tuple-element.28.pick_ref) | copy-start | bytes 196612
  25.9 0.8 %copy-start.9 = (bf16[128,256]{1,0:T(8,128)(2,1)S(1)}, bf16[128,256]{1,0:T(8,128)(2,1)}, u32[]{:S(2)}) copy-start(bf16[128,256]{1,0:T(8,128)(2,1)} %get-tuple-element.30.route_ref) | copy-start | bytes 196612
  26.7 0.8 %copy-start.10 = (bf16[64,256]{1,0:T(8,128)(2,1)S(1)}, bf16[64,256]{1,0:T(8,128)(2,1)}, u32[]{:S(2)}) copy-start(bf16[64,256]{1,0:T(8,128)(2,1)} %get-tuple-element.32.w2_ref) | copy-start | bytes 98308
  27.5 0.7 %copy-start.13 = (bf16[16,512]{1,0:T(8,128)(2,1)S(1)}, bf16[16,512]{1,0:T(8,128)(2,1)}, u32[]{:S(2)}) copy-start(bf16[16,512]{1,0:T(8,128)(2,1)} %get-tuple-element.29.hidden_ref) | copy-start | bytes 49156
  31.1 20.0 %copy-start = (bf16[768,64]{1,0:T(8,128)(2,1)S(1)}, bf16[768,64]{1,0:T(8,128)(2,1)}, u32[]{:S(2)}) copy-start(bf16[768,64]{1,0:T(8,128)(2,1)} %copy.19.proj_ref) | copy-start | bytes 294916
  67.1 1.9 %copy-start.14 = (f32[4,4,12,64]{3,2,1,0:T(8,128)S(1)}, f32[4,4,12,64]{3,2,1,0:T(8,128)}, u32[]{:S(2)}) copy-start(f32[4,4,12,64]{3,2,1,0:T(8,128)} %get-tuple-element.42) | copy-start | bytes 147460
  69.0 0.7 copy-start.15

commit v2 on v1

--- a/solution.py
+++ b/solution.py
@@ -34,13 +34,6 @@
     return lax.broadcasted_iota(jnp.int32, shape, dim)
 
 
-def one_hot(shape, pairs, shift=0):
-    matrix = np.zeros(shape, np.float32)
-    for row, col in pairs:
-        matrix[row, col + shift] = 1.0
-    return matrix
-
-
 def column_tables(cols):
     half = cols // 2
     fine = 2 * cols
@@ -66,86 +59,106 @@
     return pixels, cells
 
 
-def pack_kernel(cot_ref, pre_ref, edge_ref, g_ref, p_ref, own_ref, a_ref, b_ref, cot_wide, pre_wide):
+def spread(ref, wide, group):
+    frames, real, rows, cols = ref.shape
+    for f in range(frames):
+        for o in range(group):
+            value = ref[f, o].astype(F32) if o < real else jnp.zeros((rows, cols), F32)
+            for h in range(cols // 128):
+                wide[pl.ds(((h * frames + f) * group + o) * rows, rows), :] = value[:, h * 128 : (h + 1) * 128]
+
+
+def gathered(wide, h, frames, group, rows, f, r):
+    return wide[pl.ds((h * frames + f) * group * rows + r, group, stride=rows), :].astype(BF)
+
+
+def edge_tables(pcol, cols):
+    row, col = iota((16, pcol), 0), iota((16, pcol), 1)
+    pick_g = ((row < 3) & (col == row)) | ((row >= 3) & (row < 6) & (col == row + pcol - 6))
+    row, col = iota((16, cols), 0), iota((16, cols), 1)
+    pick_p = ((row == 8) & (col == 0)) | ((row == 9) & (col == cols - 1))
+    return pick_g.astype(F32).astype(BF), pick_p.astype(F32).astype(BF)
+
+
+def send_kernel(cot_ref, pre_ref, a_ref, b_ref, cot_wide, pre_wide):
     frames, bands, prow, pcol = cot_ref.shape
     _, chans, rows, cols = pre_ref.shape
-    wide_rows = frames * GROUP * prow
-    halves = range(pcol // cols)
-    for f in range(frames):
-        for o in range(GROUP):
-            at = (f * GROUP + o) * prow
-            band = cot_ref[f, o].astype(F32) if o < bands else jnp.zeros((prow, pcol), F32)
-            for h in halves:
-                cot_wide[pl.ds(h * wide_rows + at, prow), :] = band[:, h * cols : (h + 1) * cols]
-        for c in range(chans):
-            pre_wide[pl.ds((f * chans + c) * rows, rows), :] = pre_ref[f, c].astype(F32)
+    spread(cot_ref, cot_wide, GROUP)
+    spread(pre_ref, pre_wide, chans)
+    pick_g, pick_p = edge_tables(pcol, cols)
+    at = frames * 3 * GROUP
+
+    def message(out_ref, top):
+        first = 0 if top else prow - 3
+        line = 0 if top else rows - 1
+        for f in range(frames):
+            for y in range(3):
+                for h in range(pcol // 128):
+                    out_ref[pl.ds((f * 3 + y) * GROUP, GROUP), h * 128 : (h + 1) * 128] = gathered(
+                        cot_wide, h, frames, GROUP, prow, f, first + y
+                    )
+            out_ref[pl.ds(at, chans), f * cols : (f + 1) * cols] = gathered(
+                pre_wide, 0, frames, chans, rows, f, line
+            )
+        out_ref[pl.ds(at + chans, 16), :] = jnp.zeros((16, pcol), BF)
+        out_ref[pl.ds(at + chans, 16), :at] = nt(pick_g, out_ref[pl.ds(0, at), :]).astype(BF)
+        for f in range(frames):
+            out_ref[pl.ds(at + chans, 16), cols + f * chans : cols + (f + 1) * chans] = nt(
+                pick_p, out_ref[pl.ds(at, chans), f * cols : (f + 1) * cols]
+            ).astype(BF)
+
+    even = lax.rem(lax.axis_index("ns"), 2) == 0
+
+    @pl.when(even)
+    def _():
+        message(a_ref, False)
+        message(b_ref, True)
+
+    @pl.when(jnp.logical_not(even))
+    def _():
+        message(a_ref, True)
+        message(b_ref, False)
+
+
+def layout_kernel(cot_ref, pre_ref, g_ref, p_ref, own_ref, cot_wide, pre_wide):
+    frames, bands, prow, pcol = cot_ref.shape
+    _, chans, rows, cols = pre_ref.shape
+    spread(cot_ref, cot_wide, GROUP)
+    spread(pre_ref, pre_wide, chans)
     for f in range(frames):
         for y in range(prow):
-            for h in halves:
-                g_ref[pl.ds((f * prow + y) * GROUP, GROUP), h * cols : (h + 1) * cols] = cot_wide[
-                    pl.ds(h * wide_rows + f * GROUP * prow + y, GROUP, stride=prow), :
-                ].astype(BF)
+            for h in range(pcol // 128):
+                g_ref[pl.ds((f * prow + y) * GROUP, GROUP), h * 128 : (h + 1) * 128] = gathered(
+                    cot_wide, h, frames, GROUP, prow, f, y
+                )
         for r in range(rows):
-            p_ref[pl.ds((f * rows + r) * chans, chans), :] = pre_wide[
-                pl.ds(f * chans * rows + r, chans, stride=rows), :
-            ].astype(BF)
-    pick_g = edge_ref[:, :pcol]
-    pick_p = edge_ref[:, pcol:]
+            p_ref[pl.ds((f * rows + r) * chans, chans), :] = gathered(pre_wide, 0, frames, chans, rows, f, r)
+    pick_g, pick_p = edge_tables(pcol, cols)
     edges_p = nt(pick_p, p_ref[...])
     edges_g = nt(pick_g, g_ref[...])
     width = edges_g.shape[1]
     own_ref[:, :width] = (edges_g + edges_p[:, :width]).astype(BF)
     own_ref[:, width:] = edges_p[:, width:].astype(BF)
 
-    def message(out_ref, top):
-        first = 0 if top else prow - 3
-        line = 0 if top else rows - 1
-        for f in range(frames):
-            out_ref[pl.ds(f * 3 * GROUP, 3 * GROUP), :] = g_ref[
-                pl.ds((f * prow + first) * GROUP, 3 * GROUP), :
-            ]
-            out_ref[pl.ds(frames * 3 * GROUP, chans), f * cols : (f + 1) * cols] = p_ref[
-                pl.ds((f * rows + line) * chans, chans), :
-            ]
-        at = frames * 3 * GROUP + chans
-        out_ref[pl.ds(at, 16), :] = jnp.zeros((16, pcol), BF)
-        out_ref[pl.ds(at, 16), : frames * 3 * GROUP] = nt(
-            pick_g, out_ref[pl.ds(0, frames * 3 * GROUP), :]
-        ).astype(BF)
-        for f in range(frames):
-            out_ref[pl.ds(at, 16), cols + f * chans : cols + (f + 1) * chans] = nt(
-                pick_p, p_ref[pl.ds((f * rows + line) * chans, chans), :]
-            ).astype(BF)
-
-    even = lax.rem(lax.axis_index("ns"), 2) == 0
-
-    @pl.when(even)
-    def _():
-        message(a_ref, False)
-        message(b_ref, True)
-
-    @pl.when(jnp.logical_not(even))
-    def _():
-        message(a_ref, True)
-        message(b_ref, False)
-
 
 def token_kernel(
-    capacity, ids_ref, tokens_ref, mask_ref, proj_ref, first_ref, second_ref,
+    capacity, counts_ref, vis_ref, owners_ref, tokens_ref, mask_ref, proj_ref, first_ref, second_ref,
     grid_ref, pick_ref, hidden_ref, route_ref, wab_ref, w2_ref,
 ):
     slots_all = tokens_ref.shape[0]
     frames, slots, patches = pick_ref.shape
-    chans = proj_ref.shape[1]
-    bands = second_ref.shape[2]
+    chans = proj_ref.shape[0]
+    bands = second_ref.shape[1]
     owners = route_ref.shape[0] // GROUP
     half = capacity // 2
     eye = (iota((chans, chans), 0) == iota((chans, chans), 1)).astype(BF)
-    pad = jnp.zeros((GROUP - bands, chans), BF)
+    pad = jnp.zeros((GROUP - bands, chans), F32)
     taps = []
     for b in range(4):
         for a in range(4):
-            taps.append(jnp.concatenate([second_ref[a, b], pad], axis=0))
+            here = iota((bands, 4, chans), 1) == b
+            tap = jnp.sum(jnp.where(here, second_ref[a].astype(F32), 0.0), axis=1)
+            taps.append(jnp.concatenate([tap, pad], axis=0).astype(BF))
     w2_ref[...] = nt(eye, jnp.concatenate(taps, axis=0)).astype(BF)
     left = (iota((2 * chans, chans), 0) == iota((2 * chans, chans), 1)).astype(BF)
     right = (iota((2 * chans, chans), 0) == iota((2 * chans, chans), 1) + chans).astype(BF)
@@ -155,16 +168,22 @@
         wab_ref[:, arrangement * 4 * chans : (arrangement + 1) * 4 * chans] = (
             nt(left, taps_lo) + nt(right, taps_hi)
         ).astype(BF)
-    vis = ids_ref[0:1, :]
-    owner = ids_ref[1:2, :]
-    live = ids_ref[2:3, :]
+    vis = jnp.concatenate([vis_ref[f : f + 1, :] for f in range(frames)], axis=1)
+    owner = jnp.concatenate([owners_ref[f] for f in range(frames)], axis=1)
+    slot = iota((1, slots_all), 1)
+    live = jnp.zeros((1, slots_all), jnp.int32)
+    for f in range(frames):
+        inside = (slot >= f * slots) & (slot < f * slots + counts_ref[0, f])
+        live = jnp.where(inside, 1, live)
     wanted = jnp.where(live > 0, vis, patches)
     square = (slots_all, slots_all)
     column = jnp.sum(
         jnp.where(iota(square, 0) == iota(square, 1), wanted.astype(F32), 0.0), axis=1, keepdims=True
     ).astype(jnp.int32)
-    token_proj = nn(tokens_ref[...], proj_ref[...]).astype(BF)
-    mask_proj = nn(jnp.broadcast_to(mask_ref[...], (16, mask_ref.shape[1])), proj_ref[...]).astype(BF)
+    token_proj = nt(tokens_ref[...], proj_ref[...]).astype(BF)
+    features = mask_ref.shape[0]
+    mask_row = mask_ref[...].astype(F32).reshape(1, features)
+    mask_proj = nt(jnp.broadcast_to(mask_row, (16, features)).astype(BF), proj_ref[...]).astype(BF)
     row0 = iota((16, patches), 0) == 0
     lane = iota((chans, 2 * chans), 1)
     for f in range(frames):
@@ -197,7 +216,7 @@
 
 
 def tile_kernel(
-    n_ew, rows_each, g_ref, p_ref, ra_ref, rb_ref, ea_ref, eb_ref, pix_ref, cell_ref, halo_ref,
+    n_ew, rows_each, g_ref, p_ref, ra_ref, rb_ref, ea_ref, eb_ref, pix_ref, cell_ref,
     grid_ref, pick_ref, hidden_ref, route_ref, wab_ref, w2_ref, tokens_ref, mask_ref,
     out_ref, ext, wide, wins, pres, deltas, routed,
 ):
@@ -222,8 +241,11 @@
     xb = sides[:, own_len + pcol : own_len + 2 * pcol]
     side_n = jnp.where(even_ns, xb, xa)
     side_s = jnp.where(even_ns, xa, xb)
-    pick_g = halo_ref[:, :128]
-    pick_p = halo_ref[:, 128:256]
+    row, col = iota((32, 128), 0), iota((32, 128), 1)
+    pick_g = ((row < 3) & (col == row)) | ((row >= 19) & (row < 22) & (col == row - 16))
+    pick_g = pick_g.astype(F32).astype(BF)
+    pick_p = ((row == 8) & (col == 0)) | ((row == 25) & (col == 1))
+    pick_p = pick_p.astype(F32).astype(BF)
     g_len = frames * prow * GROUP
     edge = frames * 3 * GROUP
     own_g = tn(sides[:, :g_len], pick_g).astype(BF)
@@ -325,29 +347,20 @@
     chosen = jnp.concatenate(lower + upper, axis=0).astype(BF)
     routed[...] = nn(route_ref[...], chosen).astype(BF)
     features = tokens_ref.shape[1]
-    tokens = tokens_ref[...]
-    split = jnp.concatenate([tokens[:, : features // 2], tokens[:, features // 2 :]], axis=0)
     hi = mask_sum.astype(BF).astype(F32)
     lo = mask_sum - hi
-    nothing = jnp.zeros_like(hi)
-    hi_left = jnp.concatenate([hi, nothing], axis=1)[0:1]
-    hi_right = jnp.concatenate([nothing, hi], axis=1)[0:1]
-    lo_left = jnp.concatenate([lo, nothing], axis=1)[0:1]
-    lo_right = jnp.concatenate([nothing, lo], axis=1)[0:1]
-    line = iota((16, 2 * chans), 0)
-    mask_rows = jnp.where(line == 0, hi_left, 0.0) + jnp.where(line == 1, hi_right, 0.0)
-    mask_rows = mask_rows + jnp.where(line == 2, lo_left, 0.0) + jnp.where(line == 3, lo_right, 0.0)
-    mask_token = mask_ref[...].astype(F32)
-    line = iota((16, features // 2), 0)
-    spread = jnp.where(
-        (line == 0) | (line == 2),
-        mask_token[:, : features // 2],
-        jnp.where((line == 1) | (line == 3), mask_token[:, features // 2 :], 0.0),
-    )
-    grad_proj = tn(split, chosen) + tn(spread.astype(BF), mask_rows.astype(BF))
+    line = iota(hi.shape, 0)
+    mask_rows = jnp.where(line == 0, hi[0:1], jnp.where(line == 1, lo[0:1], 0.0)).astype(BF)
+    line = iota((16, features), 0)
+    mask_row = mask_ref[...].astype(F32).reshape(1, features)
+    spread_row = jnp.where(line < 2, mask_row, 0.0).astype(BF)
+    slots_all = tokens_ref.shape[0]
+    grad_proj = tn(chosen[:slots_all, :chans], tokens_ref[...]) + tn(mask_rows, spread_row)
+    grad_proj = [grad_proj[:, k * 128 : (k + 1) * 128] for k in range(features // 128)]
+    both = jnp.concatenate([hi[0:1], lo[0:1]], axis=1)
     mark = iota(grad_second.shape, 0) == MASK_ROW - SECOND_AT
-    grad_second = jnp.where(mark, hi_left + lo_right, grad_second)
-    total = jnp.concatenate([grad_first, grad_proj, grad_second], axis=0).astype(BF)
+    grad_second = jnp.where(mark, both, grad_second)
+    total = jnp.concatenate([grad_first, *grad_proj, grad_second], axis=0).astype(BF)
     count = out_ref.shape[0]
     for d in range(GRAD_ROWS // rows_each):
         out_ref[d, :rows_each, :] = total[d * rows_each : (d + 1) * rows_each]
@@ -370,7 +383,7 @@
 
 def owner_kernel(n_ns, capacity, rows_each, got_ref, proj_ref, sum_ref, token_ref):
     count = got_ref.shape[0]
-    chans = proj_ref.shape[1]
+    chans = proj_ref.shape[0]
     if count <= 64:
         total = got_ref[0, :rows_each, :].astype(F32)
         for d in range(1, count):
@@ -404,37 +417,40 @@
     picked = nn((source == col).astype(F32).astype(BF), arrived)
     second = lax.rem(iota(picked.shape, 0), capacity) >= half
     picked = jnp.where(second, pltpu.roll(picked, chans, 1), picked)[:, :chans].astype(BF)
-    token_ref[...] = nt(picked, proj_ref[...]).astype(BF)
+    token_ref[...] = nn(picked, proj_ref[...]).astype(BF)
 
 
 def finish_kernel(got_ref, proj_ref, proj_out, first_out, second_out, mask_out):
-    chans = proj_ref.shape[1]
-    bands = second_out.shape[2]
+    chans, features = proj_ref.shape
+    bands = second_out.shape[1]
     rows_each = got_ref.shape[1]
     parts = [got_ref[d] for d in range(GRAD_ROWS // rows_each)]
     total = jnp.concatenate(parts, axis=0).astype(F32)
-    turned = pltpu.roll(total, chans, 1)
-    low, high = total[:, :chans], turned[:, :chans]
     for arrangement, taps in enumerate(((1, 2), (3, 0))):
+        rows = total[arrangement * 4 * chans : (arrangement + 1) * 4 * chans]
+        turned = pltpu.roll(rows, chans, 1)
         for a in range(4):
-            at = (arrangement * 4 + a) * chans
-            first_out[a, taps[0]] = low[at : at + chans]
-            first_out[a, taps[1]] = high[at : at + chans]
-    features = proj_ref.shape[0]
-    proj_out[: features // 2, :] = low[PROJ_AT : PROJ_AT + features // 2]
-    proj_out[features // 2 :, :] = high[PROJ_AT : PROJ_AT + features // 2]
+            first_out[a, taps[0]] = rows[a * chans : (a + 1) * chans, :chans]
+            first_out[a, taps[1]] = turned[a * chans : (a + 1) * chans, :chans]
+    for k in range(features // 128):
+        at = PROJ_AT + k * chans
+        proj_out[:, k * 128 : (k + 1) * 128] = total[at : at + chans]
+    rows = total[SECOND_AT:]
+    turned = pltpu.roll(rows, chans, 1)
     for b in range(2):
         for a in range(4):
-            at = SECOND_AT + (b * 4 + a) * GROUP
-            second_out[a, b] = low[at : at + bands]
-            second_out[a, b + 2] = high[at : at + bands]
-    mask_sum = low[MASK_ROW : MASK_ROW + 1] + high[MASK_ROW : MASK_ROW + 1]
+            at = (b * 4 + a) * GROUP
+            second_out[a, :, b, :] = rows[at : at + bands, :chans]
+            second_out[a, :, b + 2, :] = turned[at : at + bands, :chans]
+    at = MASK_ROW - SECOND_AT
+    mask_sum = rows[at : at + 1, :chans] + turned[at : at + 1, :chans]
     hi = mask_sum.astype(BF).astype(F32)
     mid = (mask_sum - hi).astype(BF).astype(F32)
     lo = mask_sum - hi - mid
     line = iota((16, chans), 0)
-    rows = jnp.where(line == 0, hi, 0.0) + jnp.where(line == 1, mid, 0.0) + jnp.where(line == 2, lo, 0.0)
-    mask_out[...] = jnp.sum(nt(rows.astype(BF), proj_ref[...]), axis=0, keepdims=True)
+    split = jnp.where(line == 0, hi, jnp.where(line == 1, mid, jnp.where(line == 2, lo, 0.0)))
+    grad_mask = jnp.sum(nn(split.astype(BF), proj_ref[...]), axis=0, keepdims=True)
+    mask_out[...] = grad_mask.reshape(features)
 
 
 def swap(block, axis, offset):
@@ -443,11 +459,11 @@
     return lax.ppermute(block, axis, [(i, j) for i, j in pairs if 0 <= j < count])
 
 
-def call(kernel, outs, args, scratch=(), flops=0, limit=None):
+def call(kernel, outs, args, scratch=(), flops=0, limit=8 << 20, scalars=0):
     return pl.pallas_call(
         kernel,
         out_shape=outs,
-        in_specs=[VMEM] * len(args),
+        in_specs=[pl.BlockSpec(memory_space=pltpu.SMEM)] * scalars + [VMEM] * (len(args) - scalars),
         out_specs=jax.tree.map(lambda _: VMEM, outs),
         scratch_shapes=list(scratch),
         compiler_params=pltpu.CompilerParams(vmem_limit_bytes=limit),
@@ -460,7 +476,7 @@
 ):
     frames, slots, features = tokens.shape[2:]
     _, chans, rows, cols = saved_pre.shape
-    prow, pcol = cotangent.shape[2:]
+    bands, prow, pcol = cotangent.shape[1:]
     patches = rows * cols // 4
     count = n_ew * n_ns
     capacity = 3 * frames * slots // (2 * n_ns)
@@ -471,44 +487,37 @@
 
     pixels, cells = column_tables(cols)
     pixels, cells = jnp.asarray(pixels, BF), jnp.asarray(cells, BF)
-    edge_pairs = [(0, 0), (1, 1), (2, 2), (3, pcol - 3), (4, pcol - 2), (5, pcol - 1)]
-    edge_pairs += [(8, pcol), (9, pcol + cols - 1)]
-    edges = jnp.asarray(one_hot((16, pcol + cols), edge_pairs), BF)
-    halo_pairs = [(0, 0), (1, 1), (2, 2), (16 + 3, 3), (16 + 4, 4), (16 + 5, 5)]
-    halo_pairs += [(8, 128), (16 + 9, 129)]
-    halos = jnp.asarray(one_hot((32, 256), halo_pairs), BF)
-
     msg_rows = frames * 3 * GROUP + chans + 16
-    own_g, own_p, own_edges, send_a, send_b = call(
-        pack_kernel,
+    wide = [
+        pltpu.VMEM((frames * GROUP * prow * pcol // 128, 128), F32),
+        pltpu.VMEM((frames * chans * rows, cols), F32),
+    ]
+    send_a, send_b = call(
+        send_kernel,
+        (shape((msg_rows, pcol), BF), shape((msg_rows, pcol), BF)),
+        (cotangent, saved_pre),
+        wide,
+        flops=1 << 22,
+    )
+    got_a = swap(send_a, "ns", 0)
+    got_b = swap(send_b, "ns", 1)
+    own_g, own_p, own_edges = call(
+        layout_kernel,
         (
             shape((frames * prow * GROUP, pcol), BF),
             shape((frames * rows * chans, cols), BF),
             shape((16, frames * rows * chans), BF),
-            shape((msg_rows, pcol), BF),
-            shape((msg_rows, pcol), BF),
         ),
-        (cotangent, saved_pre, edges),
-        [
-            pltpu.VMEM((frames * GROUP * prow * pcol // cols, cols), F32),
-            pltpu.VMEM((frames * chans * rows, cols), F32),
-        ],
+        (cotangent, saved_pre),
+        wide,
         flops=1 << 22,
     )
-    got_a = swap(send_a, "ns", 0)
-    got_b = swap(send_b, "ns", 1)
-
-    live = jnp.arange(slots, dtype=jnp.int32)[None, :] < counts[0, 0][:, None]
-    ids = jnp.stack(
-        [
-            vis_index.reshape(slots_all),
-            owners.reshape(slots_all),
-            live.astype(jnp.int32).reshape(slots_all),
-        ]
-    )
-    ids = jnp.concatenate([ids, jnp.zeros((5, slots_all), jnp.int32)], axis=0)
+    side = jnp.concatenate([own_edges, got_a[msg_rows - 16 :], got_b[msg_rows - 16 :]], axis=1)
+    side_a = swap(side, "ew", 0)
+    side_b = swap(side, "ew", 1)
+
     tile_tokens = tokens.reshape(slots_all, features)
-    mask_row = mask_token.reshape(1, features)
+    proj = proj_weight.T
     grid, picks, hidden, route, wab, w2 = call(
         functools.partial(token_kernel, capacity),
         (
@@ -519,20 +528,25 @@
             shape((2 * chans, 8 * chans), BF),
             shape((chans, 16 * GROUP), BF),
         ),
-        (ids, tile_tokens, mask_row, proj_weight, up_first, up_second),
+        (
+            counts.reshape(1, frames),
+            vis_index.reshape(frames, slots),
+            owners.reshape(frames, 1, slots),
+            tile_tokens,
+            mask_token,
+            proj,
+            up_first,
+            up_second.transpose(0, 2, 1, 3),
+        ),
         flops=1 << 24,
-    )
-
-    side = jnp.concatenate([own_edges, got_a[msg_rows - 16 :], got_b[msg_rows - 16 :]], axis=1)
-    side_a = swap(side, "ew", 0)
-    side_b = swap(side, "ew", 1)
-
+        scalars=1,
+    )
     outgoing = call(
         functools.partial(tile_kernel, n_ew, rows_each),
         shape((count, rows_each + GROUP, 2 * chans), BF),
         (
-            own_g, own_p, got_a, got_b, side_a, side_b, pixels, cells, halos,
-            grid, picks, hidden, route, wab, w2, tile_tokens, mask_row,
+            own_g, own_p, got_a, got_b, side_a, side_b, pixels, cells,
+            grid, picks, hidden, route, wab, w2, tile_tokens, mask_token,
         ),
         [
             pltpu.VMEM((frames * (prow + 6) * GROUP, pcol + 128), BF),
@@ -543,7 +557,7 @@
             pltpu.VMEM((n_ns * GROUP, 2 * chans), BF),
         ],
         flops=1 << 28,
-        limit=40 << 20,
+        limit=24 << 20,
     )
     arrived = lax.all_to_all(outgoing, ("ew", "ns"), 0, 0, tiled=True)
     shares, token_grad = call(
@@ -552,24 +566,23 @@
             shape((count, rows_each, 2 * chans), BF),
             shape((n_ns * capacity, features), BF),
         ),
-        (arrived, proj_weight),
+        (arrived, proj),
         flops=1 << 24,
-        limit=40 << 20,
     )
     summed = lax.all_to_all(shares, ("ew", "ns"), 0, 0, tiled=True)
     summed = summed[: GRAD_ROWS // rows_each]
     grad_proj, grad_first, grad_second, grad_mask = call(
         finish_kernel,
         (
-            shape((features, chans), F32),
+            shape((chans, features), F32),
             shape((4, 4, chans, chans), F32),
-            shape((4, 4, up_second.shape[2], chans), F32),
-            shape((1, features), F32),
+            shape((4, bands, 4, chans), F32),
+            shape((features,), F32),
         ),
-        (summed, proj_weight),
+        (summed, proj),
         flops=1 << 20,
     )
-    return (token_grad[None, None], grad_proj, grad_first, grad_second, grad_mask.reshape(features))
+    return (token_grad[None, None], grad_proj.T, grad_first, grad_second.transpose(0, 2, 1, 3), grad_mask)
 
 
 def solution(mesh):

time: 71.1 us -> 55.1 us (0.77)
  local copies, waits for them, and re-layouts: 14.2 us -> 3.68 us
  Pallas kernels: 11.4 us -> 7.29 us
  other arithmetic: 4.1 us -> 0.01 us
  blocking collectives: 32.7 us -> 35.3 us
    unnamed x37 -> x24, local copies, waits for them, and re-layouts: 11.9 us -> 3.68 us
    pallas_call x5 -> x6, Pallas kernels: 11.4 us -> 7.29 us  [call(): pl.pallas_call(kernel, out_shape=outs, in_specs=[pl.BlockSpec(memory_spac...]
    all_to_all x1, blocking collectives: 20 us -> 22.9 us  [per_device(): arrived = lax.all_to_all(outgoing, ('ew', 'ns'), 0, 0, tiled=True)]
    unnamed x1 -> x0, other arithmetic: 1.34 us -> none
    reshape x1 -> x0, local copies, waits for them, and re-layouts: 1.28 us -> none  [per_device(): mask_row = mask_token.reshape(1, features)]
    another operation x2 -> x0, local copies, waits for them, and re-layouts: 0.84 us -> none  [per_device(): jnp.stack([vis_index.reshape(slots_all), owners.reshape(slots_all), live....]
    concatenate x1, other arithmetic: 0.76 us -> 0.01 us  [per_device(): jnp.concatenate([own_edges, got_a[msg_rows - 16:], got_b[msg_rows - 16:]]...]
    convert_element_type x1 -> x0, other arithmetic: 0.73 us -> none  [per_device(): live.astype(jnp.int32).reshape(slots_all)]
  transfers between devices with their start and end apart: 4 -> 4, of which waited for: 0 -> 1; matrix products, arithmetic and copies ran while one was open for 12% -> 0% of each run, Pallas kernels for 4% -> 3%
where the time goes in v2:
time: 55.1 us; the launch traced here: 54.8 us
  blocking collectives  35.3 us (64%)
  Pallas kernels  7.29 us (13%)
  starting transfers between devices  7.26 us (13%)
  local copies, waits for them, and re-layouts  3.68 us (7%)
  between operations  0.77 us (1%)
    all_to_all x1, blocking collectives, per_device(): arrived = lax.all_to_all(outgoing, ('ew', 'ns'), 0, 0, tiled=True)  22.9 us
    all_to_all x1, blocking collectives, per_device(): summed = lax.all_to_all(shares, ('ew', 'ns'), 0, 0, tiled=True)  12.4 us
    pallas_call x6, Pallas kernels, call(): pl.pallas_call(kernel, out_shape=outs, in_specs=[pl.BlockSpec(memory_spac...  7.29 us
    ppermute x4, starting transfers between devices, swap(): lax.ppermute(block, axis, [(i, j) for i, j in pairs if 0 <= j < count])  7.26 us
    unnamed x24, local copies, waits for them, and re-layouts  3.68 us
  transfers between devices with their start and end apart: 4, of which 1 were waited for; matrix products, arithmetic and copies ran while one was open for 0% of the time, Pallas kernels for 3%

profile of v2, /device:TPU:0, one launch (start us, length us, event | category | flops | bytes accessed | tf_op | source)
XLA Modules:
  0.0 54.8 jit_solution(18487417741795848)
XLA Ops:
  0.6 0.0 copy-start
  0.6 0.9 %copy-done = bf16[2,64,8,128]{3,2,1,0:T(8,128)(2,1)S(1)} copy-done((bf16[2,64,8,128]{3,2,1,0:T(8,128)(2,1)S(1)}, bf16[2,64,8,128]{3,2,1,0:T(8,128)(2,1)}, u32[]{:S(2)}) %copy-start) | copy-done | bytes 262168
  1.6 0.0 copy-start.2
  1.6 0.9 %copy-done.2 = bf16[2,12,16,256]{3,2,1,0:T(8,128)(2,1)S(1)} copy-done((bf16[2,12,16,256]{3,2,1,0:T(8,128)(2,1)S(1)}, bf16[2,12,16,256]{3,2,1,0:T(8,128)(2,1)}, u32[]{:S(2)}) %copy-start.2) | copy-done | bytes 196632
  2.5 0.0 copy-start.7
  2.5 0.4 shard_map.156
  2.9 0.5 collective-permute-start
  3.4 0.0 copy-start.3
  3.4 0.0 copy-start.5
  3.4 0.8 %collective-permute-start.1 = (bf16[176,256]{1,0:T(8,128)(2,1)S(1)}, bf16[176,256]{1,0:T(8,128)(2,1)S(1)}, u32[]{:S(2)}, u32[]{:S(2)}) collective-permute-start(bf16[176,256]{1,0:T(8,128)(2,1)S(1)} %get-tuple-element.25), channel_id=1, source_target_pairs={{1,2},{2,1},{3,4},{4,3},{5,6},{6,5},{9,10},{10,9},{11,12},{12,11},... | collective-permute-start | bytes 270344 | tf_op jit(solution)/shard_map/ppermute | solution.py:459
  4.1 0.5 shard_map.155
  4.7 0.0 copy-start.1
  4.7 0.0 collective-permute-done.ra_ref
  4.7 0.0 collective-permute-done.1.rb_ref
  4.7 0.0 copy-start.10
  4.7 0.7 %collective-permute-start.3 = (bf16[16,1536]{1,0:T(8,128)(2,1)S(1)}, bf16[16,1536]{1,0:T(8,128)(2,1)S(1)}, u32[]{:S(2)}, u32[]{:S(2)}) collective-permute-start(bf16[16,1536]{1,0:T(8,128)(2,1)S(1)} %pad_maximum_fusion), channel_id=1, source_target_pairs={{8,16},{16,8},{9,17},{17,9},{10,18},{18,10},{11,19},{19,11},{12,20... | collective-permute-start | bytes 147464 | tf_op jit(solution)/shard_map/ppermute | solution.py:459
  5.4 5.3 %collective-permute-start.2 = (bf16[16,1536]{1,0:T(8,128)(2,1)S(1)}, bf16[16,1536]{1,0:T(8,128)(2,1)S(1)}, u32[]{:S(2)}, u32[]{:S(2)}) collective-permute-start(bf16[16,1536]{1,0:T(8,128)(2,1)S(1)} %pad_maximum_fusion), channel_id=1, source_target_pairs={{0,8},{8,0},{16,24},{24,16},{1,9},{9,1},{17,25},{25,17},{2,10},{10... | collective-permute-start | bytes 147464 | tf_op jit(solution)/shard_map/ppermute | solution.py:459
  10.8 0.0 copy-start.8
  10.8 0.0 copy-start.9
  10.8 0.0 copy-start.11
  10.8 0.0 copy-done.7
  10.8 0.0 copy-done.3
  10.8 0.0 copy-done.5
  10.8 0.0 copy-done.1
  10.8 0.0 copy-done.10
  10.8 0.6 %copy-done.8 = bf16[768]{0:T(1024)(128)(2,1)S(1)} copy-done((bf16[768]{0:T(1024)(128)(2,1)S(1)}, bf16[768]{0:T(1024)(128)(2,1)}, u32[]{:S(2)}) %copy-start.8) | copy-done | bytes 1560
  11.4 0.0 copy-done.9
  11.4 0.0 copy-done.11
  11.4 0.0 copy-start.6
  11.5 1.4 %shard_map.157 = (bf16[4,128,256]{2,1,0:T(8,128)(2,1)S(1)}, bf16[2,64,256]{2,1,0:T(8,128)(2,1)S(1)}, bf16[16,512]{1,0:T(8,128)(2,1)S(1)}, bf16[128,256]{1,0:T(8,...) custom-call(s32[1,2]{1,0:T(1,128)S(1)} %bitcast.19, s32[2,64]{1,0:T(2,128)S(1)} %bitcast.17, ...), custom_call_target="tpu_custom_call" | custom-call | flops 16777216 | bytes 1048576 | tf_op jit(solution)/shard_map/pallas_call | solution.py:463
  12.8 0.0 collective-permute-done.3.eb_ref
  12.8 0.4 collective-permute-done.2.ea_ref
  13.3 0.0 copy-done.6
  13.3 0.0 copy-start.4
  13.3 1.1 %copy-done.4 = bf16[384,1024]{1,0:T(8,128)(2,1)S(1)} copy-done((bf16[384,1024]{1,0:T(8,128)(2,1)S(1)}, bf16[384,1024]{1,0:T(8,128)(2,1)}, u32[]{:S(2)}) %copy-start.4) | copy-done | bytes 786456
  14.4 2.8 %shard_map.158 = bf16[32,48,128]{2,1,0:T(8,128)(2,1)S(1)} custom-call(bf16[512,256]{1,0:T(8,128)(2,1)S(1)} %get-tuple-element.22.g_ref, bf16[1024,128]{1,0:T(8,128)(2,1)S(1)} %get-tuple-element.23.p_ref, bf16[176,256]{1,0:T(8,128)(2,1)S(1)} %collective-permute-done.ra_ref, bf16[176,256]{1,0:T(8,128)(2,1)S(1)} %collective-permute-done.1.rb_ref, ...), custom_call_target="tpu_custom_call" | custom-call | flops 268435456 | bytes 1048576 | tf_op jit(solution)/shard_map/pallas_call | solution.py:463
  17.2 22.9 %all_to_all.10.got_ref = bf16[32,48,128]{2,1,0:T(8,128)(2,1)S(1)} all-to-all(bf16[32,48,128]{2,1,0:T(8,128)(2,1)S(1)} %shard_map.158), channel_id=1, replica_groups=mesh['ew'=4,'ns'=8] {'ew','ns'}, dimensions={0} | all-to-all | bytes 786432 | tf_op jit(solution)/shard_map/all_to_all | solution.py:562
  40.2 1.2 %shard_map.159 = (bf16[32,32,128]{2,1,0:T(8,128)(2,1)S(1)}, bf16[192,768]{1,0:T(8,128)(2,1)}) custom-call(bf16[32,48,128]{2,1,0:T(8,128)(2,1)S(1)} %all_to_all.10.got_ref, bf16[64,768]{1,0:T(8,128)(2,1)S(1)} %bitcast.12), custom_call_target="tpu_custom_call" | custom-call | flops 16777216 | bytes 1048576 | tf_op jit(solution)/shard_map/pallas_call | solution.py:463
  41.4 12.4 %all_to_all.11.got_ref = bf16[32,32,128]{2,1,0:T(8,128)(2,1)S(1)} all-to-all(bf16[32,32,128]{2,1,0:T(8,128)(2,1)S(1)} %get-tuple-element.34), channel_id=1, replica_groups=mesh['ew'=4,'ns'=8] {'ew','ns'}, dimensions={0} | all-to-all | bytes 524288 | tf_op jit(solution)/shard_map/all_to_all | solution.py:572
  53.8 1.0 %shard_map.160 = (f32[64,768]{1,0:T(8,128)}, f32[4,4,64,64]{3,2,1,0:T(8,128)}, f32[4,12,4,64]{3,2,1,0:T(4,128)}, f32[768]{0:T(1024)}) custom-call(bf16[32,32,128]{2,1,0:T(8,128)(2,1)S(1)} %all_to_all.11.got_ref, bf16[64,768]{1,0:T(8,128)(2,1)S(1)} %bitcast.13), custom_call_target="tpu_custom_call" | custom-call | flops 1048576 | bytes 1048576 | tf_op jit(solution)/shard_map/pallas_call | solution.py:463
  (3 shorter events, 0.0 us)
Async XLA Ops:
  0.6 1.0 %copy-start = (bf16[2,64,8,128]{3,2,1,0:T(8,128)(2,1)S(1)}, bf16[2,64,8,128]{3,2,1,0:T(8,128)(2,1)}, u32[]{:S(2)}) copy-start(bf16[2,64,8,128]{3,2,1,0:T(8,128)(2,1)} %pre_ref.3) | copy-start | bytes 786436
  1.6 0.9 %copy-start.2 = (bf16[2,12,16,256]{3,2,1,0:T(8,128)(2,1)S(1)}, bf16[2,12,16,256]{3,2,1,0:T(8,128)(2,1)}, u32[]{:S(2)}) copy-start(bf16[2,12,16,256]{3,2,1,0:T(8,128)(2,1)} %cot_ref.3) | copy-start | bytes 589828
  2.5 8.2 %copy-start.7 = (bf16[4,4,12,64]{3,1,2,0:T(4,128)(2,1)S(1)}, bf16[4,4,12,64]{3,1,2,0:T(4,128)(2,1)}, u32[]{:S(2)}) copy-start(bf16[4,4,12,64]{3,1,2,0:T(4,128)(2,1)} %param.19) | copy-start | bytes 73732
  2.9 1.8 %collective-permute-start = (bf16[176,256]{1,0:T(8,128)(2,1)S(1)}, bf16[176,256]{1,0:T(8,128)(2,1)S(1)}, u32[]{:S(2)}, u32[]{:S(2)}) collective-permute-start(bf16[176,256]{1,0:T(8,128)(2,1)S(1)} %get-tuple-element.24), channel_id=1, source_target_pairs={{0,1},{1,0},{2,3},{3,2},{4,5},{5,4},{6,7},{7,6},{8,9},{9,8},{10,11... | collective-permute-start | bytes 270344 | tf_op jit(solution)/shard_map/ppermute | solution.py:459
  3.4 7.4 %copy-start.3 = (bf16[1,1,2,64,768]{4,3,2,1,0:T(8,128)(2,1)S(1)}, bf16[1,1,2,64,768]{4,3,2,1,0:T(8,128)(2,1)}, u32[]{:S(2)}) copy-start(bf16[1,1,2,64,768]{4,3,2,1,0:T(8,128)(2,1)} %param.12) | copy-start | bytes 589828
  3.4 7.4 %copy-start.5 = (bf16[4,4,64,64]{3,2,1,0:T(8,128)(2,1)S(1)}, bf16[4,4,64,64]{3,2,1,0:T(8,128)(2,1)}, u32[]{:S(2)}) copy-start(bf16[4,4,64,64]{3,2,1,0:T(8,128)(2,1)} %first_ref.1) | copy-start | bytes 393220
  3.4 1.3 %collective-permute-start.1 = (bf16[176,256]{1,0:T(8,128)(2,1)S(1)}, bf16[176,256]{1,0:T(8,128)(2,1)S(1)}, u32[]{:S(2)}, u32[]{:S(2)}) collective-permute-start(bf16[176,256]{1,0:T(8,128)(2,1)S(1)} %get-tuple-element.25), channel_id=1, source_target_pairs={{1,2},{2,1},{3,4},{4,3},{5,6},{6,5},{9,10},{10,9},{11,12},{12,11},... | collective-permute-start | bytes 270344 | tf_op jit(solution)/shard_map/ppermute | solution.py:459
  4.7 6.1 %copy-start.1 = (bf16[768,64]{0,1:T(8,128)(2,1)S(1)}, bf16[768,64]{0,1:T(8,128)(2,1)}, u32[]{:S(2)}) copy-start(bf16[768,64]{0,1:T(8,128)(2,1)} %param.17) | copy-start | bytes 294916
  4.7 6.1 %copy-start.10 = (s32[1,1,2,64,1]{3,4,2,1,0:T(1,128)S(1)}, s32[1,1,2,64,1]{3,4,2,1,0:T(1,128)}, u32[]{:S(2)}) copy-start(s32[1,1,2,64,1]{3,4,2,1,0:T(1,128)} %param.15) | copy-start | bytes 1540
  4.7 8.1 %collective-permute-start.3 = (bf16[16,1536]{1,0:T(8,128)(2,1)S(1)}, bf16[16,1536]{1,0:T(8,128)(2,1)S(1)}, u32[]{:S(2)}, u32[]{:S(2)}) collective-permute-start(bf16[16,1536]{1,0:T(8,128)(2,1)S(1)} %pad_maximum_fusion), channel_id=1, source_target_pairs={{8,16},{16,8},{9,17},{17,9},{10,18},{18,10},{11,19},{19,11},{12,20... | collective-permute-start | bytes 147464 | tf_op jit(solution)/shard_map/ppermute | solution.py:459
  5.4 7.8 %collective-permute-start.2 = (bf16[16,1536]{1,0:T(8,128)(2,1)S(1)}, bf16[16,1536]{1,0:T(8,128)(2,1)S(1)}, u32[]{:S(2)}, u32[]{:S(2)}) collective-permute-start(bf16[16,1536]{1,0:T(8,128)(2,1)S(1)} %pad_maximum_fusion), channel_id=1, source_target_pairs={{0,8},{8,0},{16,24},{24,16},{1,9},{9,1},{17,25},{25,17},{2,10},{10... | collective-permute-start | bytes 147464 | tf_op jit(solution)/shard_map/ppermute | solution.py:459
  10.8 0.7 %copy-start.8 = (bf16[768]{0:T(1024)(128)(2,1)S(1)}, bf16[768]{0:T(1024)(128)(2,1)}, u32[]{:S(2)}) copy-start(bf16[768]{0:T(1024)(128)(2,1)} %mask_ref.3) | copy-start | bytes 4612
  10.8 0.7 %copy-start.9 = (s32[1,1,2,64]{3,2,1,0:T(2,128)S(1)}, s32[1,1,2,64]{3,2,1,0:T(2,128)}, u32[]{:S(2)}) copy-start(s32[1,1,2,64]{3,2,1,0:T(2,128)} %param.13) | copy-start | bytes 1540
  10.8 0.7 %copy-start.11 = (s32[1,1,2]{2,1,0:T(1,128)S(1)}, s32[1,1,2]{2,1,0:T(1,128)}, u32[]{:S(2)}) copy-start(s32[1,1,2]{2,1,0:T(1,128)} %param.14) | copy-start | bytes 28
  11.4 1.8 %copy-start.6 = (bf16[256,256]{1,0:T(8,128)(2,1)S(1)}, bf16[256,256]{1,0:T(8,128)(2,1)}, u32[]{:S(2)}) copy-start(bf16[256,256]{1,0:T(8,128)(2,1)} %constant.5.clone.cell_ref) | copy-start | bytes 393220
  13.3 1.1 %copy-start.4 = (bf16[384,1024]{1,0:T(8,128)(2,1)S(1)}, bf16[384,1024]{1,0:T(8,128)(2,1)}, u32[]{:S(2)}) copy-start(bf16[384,1024]{1,0:T(8,128)(2,1)} %constant.4.clone.pix_ref) | copy-start | bytes 2359300

commit v3 on v2

v3 whole, which is shorter than its diff:
```python
import functools

import jax
import jax.numpy as jnp
import numpy as np
from jax import lax
from jax.experimental import pallas as pl
from jax.experimental.pallas import tpu as pltpu
from jax.sharding import PartitionSpec as P

BF = jnp.bfloat16
F32 = jnp.float32
VMEM = pl.BlockSpec(memory_space=pltpu.VMEM)
SMEM = pl.BlockSpec(memory_space=pltpu.SMEM)
GROUP = 16
GRAD_ROWS = 1024
PROJ_AT = 512
SECOND_AT = 896
MASK_ROW = SECOND_AT + 12


def nn(a, b):
    return lax.dot_general(a, b, (((1,), (0,)), ((), ())), preferred_element_type=F32)


def nt(a, b):
    return lax.dot_general(a, b, (((1,), (1,)), ((), ())), preferred_element_type=F32)


def tn(a, b):
    return lax.dot_general(a, b, (((0,), (0,)), ((), ())), preferred_element_type=F32)


def iota(shape, dim):
    return lax.broadcasted_iota(jnp.int32, shape, dim)


def hidden_columns(cols, lanes):
    lane = lax.rem(lanes, cols)
    right = lane >= cols // 2
    own = 2 * jnp.where(right, lane - cols // 2, lane) + jnp.where(right, 1, 0)
    shifted = own + jnp.where(right, -2, 2)
    return jnp.where(lax.rem(lanes // cols, 2) == 0, own, shifted)


def column_tables(cols, pix_ref, cell_ref):
    fine = 2 * cols
    lanes = iota((1, fine), 1)
    hidden = hidden_columns(cols, lanes)
    for tap in range(4):
        pixel = 2 * hidden + tap - 1
        pixel = jnp.where(pixel < 0, fine + 6 + pixel, pixel)
        table = iota((fine + 128, fine), 0) == pixel
        pix_ref[:, tap * fine : (tap + 1) * fine] = table.astype(F32).astype(BF)
    cell = jnp.where(hidden < 0, cols + 1, hidden)
    cell_ref[...] = (iota((fine, fine), 0) == cell).astype(F32).astype(BF)


def spread(ref, wide, group):
    frames, real, rows, cols = ref.shape
    for f in range(frames):
        for o in range(group):
            value = ref[f, o].astype(F32) if o < real else jnp.zeros((rows, cols), F32)
            for h in range(cols // 128):
                wide[pl.ds(((h * frames + f) * group + o) * rows, rows), :] = value[:, h * 128 : (h + 1) * 128]


def gathered(wide, h, frames, group, rows, f, r):
    return wide[pl.ds((h * frames + f) * group * rows + r, group, stride=rows), :].astype(BF)


def edge_tables(pcol, cols):
    row, col = iota((16, pcol), 0), iota((16, pcol), 1)
    pick_g = ((row < 3) & (col == row)) | ((row >= 3) & (row < 6) & (col == row + pcol - 6))
    row, col = iota((16, cols), 0), iota((16, cols), 1)
    pick_p = ((row == 6) & (col == 0)) | ((row == 7) & (col == cols - 1))
    return pick_g.astype(F32).astype(BF), pick_p.astype(F32).astype(BF)


def cell_layout_kernel(pre_ref, p_ref, edge_ref, pre_wide):
    frames, chans, rows, cols = pre_ref.shape
    spread(pre_ref, pre_wide, chans)
    for r in range(rows):
        for f in range(frames):
            p_ref[pl.ds((r * frames + f) * chans, chans), :] = gathered(pre_wide, 0, frames, chans, rows, f, r)
    edges = nt(edge_tables(2 * cols, cols)[1], p_ref[...])[:8]
    line = frames * chans
    last = (rows - 1) * line
    edge_ref[...] = jnp.concatenate([edges[:, :line], edges[:, last:], edges[:, line:last]], axis=1)


def pixel_layout_kernel(cot_ref, edge_ref, g_ref, own_ref, cot_wide):
    frames, bands, prow, pcol = cot_ref.shape
    spread(cot_ref, cot_wide, GROUP)
    for f in range(frames):
        for y in range(prow):
            for h in range(pcol // 128):
                g_ref[pl.ds((f * prow + y) * GROUP, GROUP), h * 128 : (h + 1) * 128] = gathered(
                    cot_wide, h, frames, GROUP, prow, f, y
                )
    edges = nt(edge_tables(pcol, pcol // 2)[0], g_ref[...])[:8]
    width = edges.shape[1]
    below = edge_ref[...]
    own_ref[...] = jnp.concatenate([edges + below[:, :width], below[:, width:]], axis=1).astype(BF)


def row_messages(g_ref, p_ref, ga_ref, pa_ref, gb_ref, pb_ref):
    deep, pcol = ga_ref.shape[0], g_ref.shape[1]
    chans, cols = pa_ref.shape[0], p_ref.shape[1]
    frames = pa_ref.shape[1] // cols
    tall = g_ref.shape[0] // frames
    high = p_ref.shape[0]

    def message(g_out, p_out, top):
        for f in range(frames):
            at = f * tall if top else (f + 1) * tall - deep
            g_out[:, f * pcol : (f + 1) * pcol] = g_ref[pl.ds(at, deep), :]
            at = f * chans if top else high - (frames - f) * chans
            p_out[:, f * cols : (f + 1) * cols] = p_ref[pl.ds(at, chans), :]

    even = lax.rem(lax.axis_index("ns"), 2) == 0

    @pl.when(even)
    def _():
        message(ga_ref, pa_ref, False)
        message(gb_ref, pb_ref, True)

    @pl.when(jnp.logical_not(even))
    def _():
        message(ga_ref, pa_ref, True)
        message(gb_ref, pb_ref, False)


def local_kernel(
    capacity, counts_ref, g_ref, p_ref, vis_ref, owners_ref, tokens_ref, mask_ref, proj_ref, first_ref, second_ref,
    ga_ref, pa_ref, gb_ref, pb_ref, grid_ref, pick_ref, hidden_ref, route_ref, wab_ref, w2_ref, pix_ref, cell_ref,
):
    row_messages(g_ref, p_ref, ga_ref, pa_ref, gb_ref, pb_ref)
    column_tables(p_ref.shape[1], pix_ref, cell_ref)
    slots_all = tokens_ref.shape[0]
    frames, slots, patches = pick_ref.shape
    chans = proj_ref.shape[0]
    bands = second_ref.shape[1]
    owners = route_ref.shape[0] // GROUP
    half = capacity // 2
    eye = (iota((chans, chans), 0) == iota((chans, chans), 1)).astype(BF)
    pad = jnp.zeros((GROUP - bands, chans), F32)
    taps = []
    for b in range(4):
        for a in range(4):
            here = iota((bands, 4, chans), 1) == b
            tap = jnp.sum(jnp.where(here, second_ref[a].astype(F32), 0.0), axis=1)
            taps.append(jnp.concatenate([tap, pad], axis=0).astype(BF))
    w2_ref[...] = nt(eye, jnp.concatenate(taps, axis=0)).astype(BF)
    left = (iota((2 * chans, chans), 0) == iota((2 * chans, chans), 1)).astype(BF)
    right = (iota((2 * chans, chans), 0) == iota((2 * chans, chans), 1) + chans).astype(BF)
    for arrangement, (lo, hi) in enumerate(((1, 2), (3, 0))):
        taps_lo = jnp.concatenate([first_ref[a, lo] for a in range(4)], axis=0)
        taps_hi = jnp.concatenate([first_ref[a, hi] for a in range(4)], axis=0)
        wab_ref[:, arrangement * 4 * chans : (arrangement + 1) * 4 * chans] = (
            nt(left, taps_lo) + nt(right, taps_hi)
        ).astype(BF)
    vis = jnp.concatenate([vis_ref[f : f + 1, :] for f in range(frames)], axis=1)
    owner = jnp.concatenate([owners_ref[f] for f in range(frames)], axis=1)
    slot = iota((1, slots_all), 1)
    live = jnp.zeros((1, slots_all), jnp.int32)
    for f in range(frames):
        inside = (slot >= f * slots) & (slot < f * slots + counts_ref[0, f])
        live = jnp.where(inside, 1, live)
    wanted = jnp.where(live > 0, vis, patches)
    square = (slots_all, slots_all)
    column = jnp.sum(
        jnp.where(iota(square, 0) == iota(square, 1), wanted.astype(F32), 0.0), axis=1, keepdims=True
    ).astype(jnp.int32)
    token_proj = nt(tokens_ref[...], proj_ref[...]).astype(BF)
    features = mask_ref.shape[0]
    mask_row = mask_ref[...].astype(F32).reshape(1, features)
    mask_proj = nt(jnp.broadcast_to(mask_row, (16, features)).astype(BF), proj_ref[...]).astype(BF)
    row0 = iota((16, patches), 0) == 0
    lane = iota((chans, 2 * chans), 1)
    for f in range(frames):
        hits = iota((slots, patches), 1) == column[f * slots : (f + 1) * slots]
        picks = hits.astype(F32)
        pick_ref[f] = picks.astype(BF)
        unseen = jnp.where(row0, 1.0 - jnp.sum(picks, axis=0, keepdims=True), 0.0).astype(BF)
        hidden_ref[:, f * patches : (f + 1) * patches] = unseen
        grid = tn(token_proj[f * slots : (f + 1) * slots], picks.astype(BF)) + tn(mask_proj, unseen)
        zero = jnp.zeros((chans, 2 * chans), F32)
        for line, (group, half_at) in enumerate(((1, 0), (0, 0), (0, 1), (1, 1))):
            pair = line // 2 * 2 * chans
            straight = grid[:, pair : pair + 2 * chans]
            turned = pltpu.roll(straight, chans, 1)
            to_left, to_right = (straight, turned) if line % 2 == 0 else (turned, straight)
            at = half_at * 2 * chans
            grid_ref[f, group, :chans, at : at + 2 * chans] = jnp.where(lane < chans, to_left, zero).astype(BF)
            grid_ref[f, group, chans:, at : at + 2 * chans] = jnp.where(lane < chans, zero, to_right).astype(BF)
    own_rows = -(-owners // 16) * 16
    hit = (iota((own_rows, slots_all), 0) == jnp.where(live > 0, owner, -1)).astype(F32)
    before = (iota(square, 0) < iota(square, 1)).astype(BF)
    earlier = nn(hit.astype(BF), before)
    place = jnp.sum(earlier * hit, axis=0, keepdims=True).astype(jnp.int32)
    for h in range(2):
        inside = (live > 0) & (place >= h * half) & (place < (h + 1) * half)
        target = jnp.where(inside, owner * GROUP + place - h * half, -1)
        route_ref[:, h * slots_all : (h + 1) * slots_all] = (
            iota((owners * GROUP, slots_all), 0) == target
        ).astype(F32).astype(BF)


def side_columns(ea_ref, eb_ref, even_ew):
    ea, eb = ea_ref[...].astype(F32), eb_ref[...].astype(F32)
    return jnp.concatenate([jnp.where(even_ew, ea, eb), jnp.where(even_ew, eb, ea)], axis=0).astype(BF)


def halo_tables():
    row, col = iota((16, 128), 0), iota((16, 128), 1)
    pick_g = ((row < 3) & (col == row)) | ((row >= 11) & (row < 14) & (col == row - 8))
    pick_p = ((row == 6) & (col == 0)) | ((row == 15) & (col == 1))
    return pick_g.astype(F32).astype(BF), pick_p.astype(F32).astype(BF)


def second_backward(taps, pre, w2, drop):
    grad_hidden = nn(w2, jnp.concatenate(taps, axis=0))
    s = 0.5 + 0.5 * jnp.tanh(0.851 * pre)
    delta = grad_hidden * (s + 1.702 * pre * s * (1.0 - s))
    cols = pre.shape[1] // 2
    return jnp.where(drop, 0.0, delta).astype(BF), (pre[:, :cols] * s[:, :cols]).astype(BF)


def second_kernel_term(taps, hid):
    cols = hid.shape[1]
    zero = jnp.zeros_like(hid)
    lhs = jnp.concatenate(
        [
            jnp.concatenate([taps[0][:, :cols], taps[2][:, :cols]], axis=1),
            jnp.concatenate([taps[1][:, :cols], taps[3][:, :cols]], axis=1),
        ],
        axis=0,
    )
    rhs = jnp.concatenate(
        [jnp.concatenate([hid, zero], axis=1), jnp.concatenate([zero, hid], axis=1)], axis=0
    )
    return nt(lhs, rhs)


def outside_columns(chans, cols, n_ew, ew):
    lane = iota((chans, 2 * cols), 1)
    return ((lane == cols + cols // 2 - 1) & (ew == n_ew - 1)) | ((lane == cols + cols // 2) & (ew == 0))


def window_taps(wins, at, cols):
    return [wins[pl.ds(at, 4 * GROUP), b * 2 * cols : (b + 1) * 2 * cols] for b in range(4)]


def message_kernel(ga_ref, pa_ref, gb_ref, pb_ref, sa_ref, sb_ref, a_ref, b_ref):
    deep, span = ga_ref.shape
    corners = jnp.concatenate([sa_ref[:, :span].astype(F32), sb_ref[:, :span].astype(F32)], axis=0).astype(BF)
    for out, g, p in ((a_ref, ga_ref, pa_ref), (b_ref, gb_ref, pb_ref)):
        out[:deep, :span] = g[...]
        out[deep:, :span] = corners
        out[:, span:] = p[...]


def inner_kernel(
    n_ew, g_ref, p_ref, ea_ref, eb_ref, pix_ref, cell_ref, grid_ref, wab_ref, w2_ref,
    delta_ref, second_ref, first_ref, turn_ref, edge_ref, pre_ref, ext, wide, wins, pres,
):
    frames = grid_ref.shape[0]
    chans = w2_ref.shape[0]
    pcol, cols = g_ref.shape[1], p_ref.shape[1]
    tall = g_ref.shape[0] // frames
    rows = p_ref.shape[0] // (frames * chans)
    ew = lax.axis_index("ew")
    sides = side_columns(ea_ref, eb_ref, lax.rem(ew, 2) == 0)
    pick_g, pick_p = halo_tables()
    line = frames * chans
    ext[:, :pcol] = g_ref[...]
    ext[:, pcol:] = tn(sides[:, : frames * tall], pick_g).astype(BF)
    wide[:, :cols] = p_ref[...]
    halo = tn(sides, pick_p).astype(BF)
    wide[pl.ds(0, line), cols:] = halo[:line]
    wide[pl.ds((rows - 1) * line, line), cols:] = halo[line : 2 * line]
    wide[pl.ds(line, (rows - 2) * line), cols:] = halo[2 * line :]
    deep = 3 * GROUP
    for f in range(frames):
        block = ext[pl.ds(f * tall, tall), :]
        for b in range(4):
            lanes = slice(b * 2 * cols, (b + 1) * 2 * cols)
            wins[pl.ds(f * tall, tall), lanes] = nn(block, pix_ref[:, lanes]).astype(BF)
        edge_ref[f, 0] = wins[pl.ds(f * tall, deep), :]
        edge_ref[f, 1] = wins[pl.ds((f + 1) * tall - deep, deep), :]
    pres[...] = nn(wide[...], cell_ref[...])
    for f in range(frames):
        pre_ref[f, 0] = pres[pl.ds(f * chans, chans), :]
        pre_ref[f, 1] = pres[pl.ds((rows - 1) * line + f * chans, chans), :]
    w2 = w2_ref[...]
    wab = wab_ref[...]
    drop = outside_columns(chans, cols, n_ew, ew)
    grad_second = grad_first = None
    for f in range(frames):
        deltas = []
        for i in range(1, rows - 1):
            taps = window_taps(wins, f * tall + (2 * i - 1) * GROUP, cols)
            pre = pres[pl.ds(i * line + f * chans, chans), :]
            delta, hid = second_backward(taps, pre, w2, drop)
            deltas.append(delta)
            term = second_kernel_term(taps, hid)
            grad_second = term if grad_second is None else grad_second + term
        count = rows - 2
        for k, i in enumerate((0, 1, count - 2, count - 1)):
            delta_ref[pl.ds((f * 4 + k) * chans, chans), :] = deltas[i]
        cells = []
        for i in (0, 2):
            slab = jnp.concatenate(deltas[i : i + 4], axis=0)
            cells.append(jnp.concatenate([slab[:, :cols], slab[:, cols:]], axis=0))
        both = jnp.concatenate(cells, axis=1)
        term = nt(both, grid_ref[f, 0])
        grad_first = term if grad_first is None else grad_first + term
        turn_ref[f] = nn(wab, both)
    second_ref[...] = grad_second
    first_ref[...] = grad_first


def outer_kernel(
    n_ew, rows_each, ra_ref, rb_ref, pix_ref, cell_ref,
    delta_ref, second_ref, first_ref, turn_ref, edge_ref, pre_ref,
    grid_ref, pick_ref, hidden_ref, route_ref, wab_ref, w2_ref, tokens_ref, mask_ref,
    out_ref, ext, wide, wins, pres, routed,
):
    frames, slots, patches = pick_ref.shape
    chans = w2_ref.shape[0]
    features = tokens_ref.shape[1]
    cols = pre_ref.shape[3] // 2
    pcol = 2 * cols
    deep = 3 * GROUP
    n_ns = route_ref.shape[0] // GROUP
    ns = lax.axis_index("ns")
    ew = lax.axis_index("ew")
    even_ns = lax.rem(ns, 2) == 0
    even_ew = lax.rem(ew, 2) == 0
    ra, rb = ra_ref[...], rb_ref[...]
    north = jnp.where(even_ns, rb, ra)
    south = jnp.where(even_ns, ra, rb)
    span = frames * pcol
    tall = span // frames

    def far_sides(message):
        a, b = message[deep : deep + 8, :span].astype(F32), message[deep + 8 :, :span].astype(F32)
        return jnp.concatenate([jnp.where(even_ew, a, b), jnp.where(even_ew, b, a)], axis=0).astype(BF)

    pick_g, pick_p = halo_tables()
    line = frames * chans
    far = (far_sides(north), far_sides(south))
    for low in range(2):
        message = south if low else north
        halo_p = tn(far[low][:, (1 - low) * line : (2 - low) * line], pick_p).astype(BF)
        for f in range(frames):
            at = (f * 2 + low) * deep
            ext[pl.ds(at, deep), :pcol] = message[:deep, f * pcol : (f + 1) * pcol]
            if low:
                ext[pl.ds(at, deep), pcol:] = tn(far[low][:, f * tall : f * tall + 128], pick_g).astype(BF)[:deep]
            else:
                end = (f + 1) * tall
                ext[pl.ds(at, deep), pcol:] = tn(far[low][:, end - 128 : end], pick_g).astype(BF)[128 - deep :]
            at = (f * 2 + low) * chans
            wide[pl.ds(at, chans), :cols] = message[:, span + f * cols : span + (f + 1) * cols]
            wide[pl.ds(at, chans), cols:] = halo_p[f * chans : (f + 1) * chans]
    block = ext[...]
    for b in range(4):
        lanes = slice(b * 2 * cols, (b + 1) * 2 * cols)
        wins[:, lanes] = nn(block, pix_ref[:, lanes]).astype(BF)
    pres[...] = nn(wide[...], cell_ref[...])
    w2 = w2_ref[...]
    wab = wab_ref[...]
    drop = outside_columns(chans, cols, n_ew, ew)
    grad_second = second_ref[...]
    grad_first = first_ref[...]
    half_lane = iota((chans, cols), 1) < cols // 2
    grids = []
    for f in range(frames):
        cells = []
        for low in range(2):
            pair = []
            for k in range(2):
                inside = k == 1 - low
                beyond = wins[pl.ds((f * 2 + low) * deep, deep), :]
                window = [edge_ref[f, low], beyond] if low else [beyond, edge_ref[f, low]]
                window = jnp.concatenate(window, axis=0)[k * 2 * GROUP : (k * 2 + 4) * GROUP]
                taps = [window[:, b * 2 * cols : (b + 1) * 2 * cols] for b in range(4)]
                pre = pre_ref[f, low] if inside else pres[pl.ds((f * 2 + low) * chans, chans), :]
                gone = drop if inside else drop | (ns == (n_ns - 1 if low else 0))
                delta, hid = second_backward(taps, pre, w2, gone)
                pair.append(delta)
                if inside:
                    grad_second = grad_second + second_kernel_term(taps, hid)
            kept = delta_ref[pl.ds((f * 4 + 2 * low) * chans, 2 * chans), :]
            slab = jnp.concatenate([kept, *pair] if low else [*pair, kept], axis=0)
            cells.append(jnp.concatenate([slab[:, :cols], slab[:, cols:]], axis=0))
        both = jnp.concatenate(cells, axis=1)
        grad_first = grad_first + nt(both, grid_ref[f, 1])
        edge = nn(wab, both)
        inner = turn_ref[f]
        parts = []
        for even, odd in ((edge[:, :cols], inner[:, :cols]), (inner[:, cols:], edge[:, cols:])):
            here = jnp.where(half_lane, even[:chans], odd[chans:])
            there = jnp.where(half_lane, odd[:chans], even[chans:])
            parts.append(here + pltpu.roll(there, cols // 2, 1))
        grids.append(jnp.concatenate(parts, axis=1).astype(BF))
    none = jnp.zeros((chans, patches), BF)
    mask_sum = nt(hidden_ref[...], jnp.concatenate(grids, axis=1))
    lower = [nt(pick_ref[f], jnp.concatenate([grids[f], none], axis=0)) for f in range(frames)]
    upper = [nt(pick_ref[f], jnp.concatenate([none, grids[f]], axis=0)) for f in range(frames)]
    chosen = jnp.concatenate(lower + upper, axis=0).astype(BF)
    routed[...] = nn(route_ref[...], chosen).astype(BF)
    features = tokens_ref.shape[1]
    hi = mask_sum.astype(BF).astype(F32)
    lo = mask_sum - hi
    line = iota(hi.shape, 0)
    mask_rows = jnp.where(line == 0, hi[0:1], jnp.where(line == 1, lo[0:1], 0.0)).astype(BF)
    line = iota((16, features), 0)
    mask_row = mask_ref[...].astype(F32).reshape(1, features)
    spread_row = jnp.where(line < 2, mask_row, 0.0).astype(BF)
    slots_all = tokens_ref.shape[0]
    grad_proj = tn(chosen[:slots_all, :chans], tokens_ref[...]) + tn(mask_rows, spread_row)
    grad_proj = [grad_proj[:, k * 128 : (k + 1) * 128] for k in range(features // 128)]
    both = jnp.concatenate([hi[0:1], lo[0:1]], axis=1)
    mark = iota(grad_second.shape, 0) == MASK_ROW - SECOND_AT
    grad_second = jnp.where(mark, both, grad_second)
    total = jnp.concatenate([grad_first, *grad_proj, grad_second], axis=0).astype(BF)
    count = out_ref.shape[0]
    for d in range(GRAD_ROWS // rows_each):
        out_ref[d, :rows_each, :] = total[d * rows_each : (d + 1) * rows_each]
    if count * rows_each > GRAD_ROWS:

        @pl.loop(GRAD_ROWS // rows_each, count)
        def _(d):
            out_ref[d, :rows_each, :] = jnp.zeros((rows_each, 2 * chans), BF)

    def place(d):
        source = pl.multiple_of(lax.rem(d, n_ns) * GROUP, GROUP)
        out_ref[d, rows_each:, :] = routed[pl.ds(source, GROUP), :]

    if count <= 64:
        for d in range(count):
            out_ref[d, rows_each:, :] = routed[pl.ds((d % n_ns) * GROUP, GROUP), :]
    else:
        pl.loop(0, count)(place)


def sum_kernel(rows_each, got_ref, sum_ref):
    count = got_ref.shape[0]
    if count <= 64:
        total = got_ref[0, :rows_each, :].astype(F32)
        for d in range(1, count):
            total = total + got_ref[d, :rows_each, :].astype(F32)
    else:
        total = lax.fori_loop(
            0,
            count,
            lambda d, acc: acc + got_ref[d, :rows_each, :].astype(F32),
            jnp.zeros((rows_each, got_ref.shape[2]), F32),
        )
    share = total.astype(BF)
    if count <= 64:
        for d in range(count):
            sum_ref[d] = share
    else:

        @pl.loop(0, count)
        def _(d):
            sum_ref[d] = share


def owner_rows(n_ns, capacity, rows_each, arrived_ref, proj_ref, token_ref):
    chans = proj_ref.shape[0]
    half = capacity // 2
    ew = lax.axis_index("ew")
    arrived = jnp.concatenate(
        [arrived_ref[ew * n_ns + s, rows_each:, :] for s in range(n_ns)], axis=0
    )
    shape = (n_ns * capacity, n_ns * GROUP)
    row, col = iota(shape, 0), iota(shape, 1)
    slot = lax.rem(row, capacity)
    source = (row // capacity) * GROUP + lax.rem(slot, half)
    picked = nn((source == col).astype(F32).astype(BF), arrived)
    second = lax.rem(iota(picked.shape, 0), capacity) >= half
    picked = jnp.where(second, pltpu.roll(picked, chans, 1), picked)[:, :chans].astype(BF)
    token_ref[...] = nn(picked, proj_ref[...]).astype(BF)


def finish_kernel(
    n_ns, capacity, arrived_ref, got_ref, proj_ref, token_out, proj_out, first_out, second_out, mask_out
):
    owner_rows(n_ns, capacity, got_ref.shape[1], arrived_ref, proj_ref, token_out)
    chans, features = proj_ref.shape
    bands = second_out.shape[1]
    rows_each = got_ref.shape[1]
    parts = [got_ref[d] for d in range(GRAD_ROWS // rows_each)]
    total = jnp.concatenate(parts, axis=0).astype(F32)
    for arrangement, taps in enumerate(((1, 2), (3, 0))):
        rows = total[arrangement * 4 * chans : (arrangement + 1) * 4 * chans]
        turned = pltpu.roll(rows, chans, 1)
        for a in range(4):
            first_out[a, taps[0]] = rows[a * chans : (a + 1) * chans, :chans]
            first_out[a, taps[1]] = turned[a * chans : (a + 1) * chans, :chans]
    for k in range(features // 128):
        at = PROJ_AT + k * chans
        proj_out[:, k * 128 : (k + 1) * 128] = total[at : at + chans]
    rows = total[SECOND_AT:]
    turned = pltpu.roll(rows, chans, 1)
    for b in range(2):
        for a in range(4):
            at = (b * 4 + a) * GROUP
            second_out[a, :, b, :] = rows[at : at + bands, :chans]
            second_out[a, :, b + 2, :] = turned[at : at + bands, :chans]
    at = MASK_ROW - SECOND_AT
    mask_sum = rows[at : at + 1, :chans] + turned[at : at + 1, :chans]
    hi = mask_sum.astype(BF).astype(F32)
    mid = (mask_sum - hi).astype(BF).astype(F32)
    lo = mask_sum - hi - mid
    line = iota((16, chans), 0)
    split = jnp.where(line == 0, hi, jnp.where(line == 1, mid, jnp.where(line == 2, lo, 0.0)))
    grad_mask = jnp.sum(nn(split.astype(BF), proj_ref[...]), axis=0, keepdims=True)
    mask_out[...] = grad_mask.reshape(features)


def swap(block, axis, offset):
    count = lax.axis_size(axis)
    pairs = [(i, ((i + offset) ^ 1) - offset) for i in range(count)]
    return lax.ppermute(block, axis, [(i, j) for i, j in pairs if 0 <= j < count])


def call(kernel, outs, args, scratch=(), flops=0, limit=8 << 20, specs=None):
    return pl.pallas_call(
        kernel,
        out_shape=outs,
        in_specs=specs or [VMEM] * len(args),
        out_specs=jax.tree.map(lambda _: VMEM, outs),
        scratch_shapes=list(scratch),
        compiler_params=pltpu.CompilerParams(vmem_limit_bytes=limit),
        cost_estimate=pl.CostEstimate(flops=flops, bytes_accessed=1 << 20, transcendentals=0),
    )(*args)


def per_device(
    n_ew, n_ns, tokens, vis_index, counts, owners, mask_token, proj_weight, up_first, up_second, saved_pre, cotangent
):
    frames, slots, features = tokens.shape[2:]
    _, chans, rows, cols = saved_pre.shape
    bands, prow, pcol = cotangent.shape[1:]
    patches = rows * cols // 4
    count = n_ew * n_ns
    capacity = 3 * frames * slots // (2 * n_ns)
    rows_each = -(-GRAD_ROWS // count)
    rows_each = -(-rows_each // 16) * 16
    slots_all = frames * slots
    shape = jax.ShapeDtypeStruct

    tall = prow * GROUP
    own_p, p_edges = call(
        cell_layout_kernel,
        (shape((frames * rows * chans, cols), BF), shape((8, frames * rows * chans), F32)),
        (saved_pre,),
        [pltpu.VMEM((frames * chans * rows, cols), F32)],
        flops=1 << 31,
    )
    own_g, own_edges = call(
        pixel_layout_kernel,
        (shape((frames * tall, pcol), BF), shape((8, frames * rows * chans), BF)),
        (cotangent, p_edges),
        [pltpu.VMEM((frames * tall * pcol // 128, 128), F32)],
        flops=1 << 31,
    )
    side_b = swap(own_edges, "ew", 1)
    side_a = swap(own_edges, "ew", 0)

    tile_tokens = tokens.reshape(slots_all, features)
    proj = proj_weight.T
    g_message = shape((3 * GROUP, frames * pcol), BF)
    p_message = shape((chans, frames * cols), BF)
    g_a, p_a, g_b, p_b, grid, picks, hidden, route, wab, w2, pixels, cells = call(
        functools.partial(local_kernel, capacity),
        (
            g_message,
            p_message,
            g_message,
            p_message,
            shape((frames, 2, 2 * chans, 2 * cols), BF),
            shape((frames, slots, patches), BF),
            shape((16, frames * patches), BF),
            shape((n_ns * GROUP, 2 * slots_all), BF),
            shape((2 * chans, 8 * chans), BF),
            shape((chans, 16 * GROUP), BF),
            shape((pcol + 128, 4 * pcol), BF),
            shape((pcol, pcol), BF),
        ),
        (
            counts.reshape(1, frames),
            own_g,
            own_p,
            vis_index.reshape(frames, slots),
            owners.reshape(frames, 1, slots),
            tile_tokens,
            mask_token,
            proj,
            up_first,
            up_second.transpose(0, 2, 1, 3),
        ),
        flops=1 << 24,
        specs=[SMEM] + [VMEM] * 9,
    )
    message_shape = shape((3 * GROUP + 16, frames * (pcol + cols)), BF)
    send_a, send_b = call(
        message_kernel,
        (message_shape, message_shape),
        (g_a, p_a, g_b, p_b, side_a, side_b),
        flops=1 << 20,
    )
    got_b = swap(send_b, "ns", 1)
    got_a = swap(send_a, "ns", 0)

    delta_mid, second_mid, first_mid, turn_mid, edge_wins, edge_pre = call(
        functools.partial(inner_kernel, n_ew),
        (
            shape((frames * 4 * chans, 2 * cols), BF),
            shape((2 * 4 * GROUP, 2 * chans), F32),
            shape((8 * chans, 2 * chans), F32),
            shape((frames, 2 * chans, 2 * cols), F32),
            shape((frames, 2, 3 * GROUP, 8 * cols), BF),
            shape((frames, 2, chans, 2 * cols), F32),
        ),
        (own_g, own_p, side_a, side_b, pixels, cells, grid, wab, w2),
        [
            pltpu.VMEM((frames * tall, pcol + 128), BF),
            pltpu.VMEM((rows * frames * chans, 2 * cols), BF),
            pltpu.VMEM((frames * tall, 8 * cols), BF),
            pltpu.VMEM((rows * frames * chans, 2 * cols), F32),
        ],
        flops=1 << 27,
        limit=16 << 20,
    )
    beyond = frames * 2 * 3 * GROUP
    outgoing = call(
        functools.partial(outer_kernel, n_ew, rows_each),
        shape((count, rows_each + GROUP, 2 * chans), BF),
        (
            got_a, got_b, pixels, cells, delta_mid, second_mid, first_mid, turn_mid, edge_wins, edge_pre,
            grid, picks, hidden, route, wab, w2, tile_tokens, mask_token,
        ),
        [
            pltpu.VMEM((beyond, pcol + 128), BF),
            pltpu.VMEM((frames * 2 * chans, 2 * cols), BF),
            pltpu.VMEM((beyond, 8 * cols), BF),
            pltpu.VMEM((frames * 2 * chans, 2 * cols), F32),
            pltpu.VMEM((n_ns * GROUP, 2 * chans), BF),
        ],
        flops=1 << 27,
        limit=24 << 20,
    )
    arrived = lax.all_to_all(outgoing, ("ew", "ns"), 0, 0, tiled=True)
    shares = call(
        functools.partial(sum_kernel, rows_each),
        shape((count, rows_each, 2 * chans), BF),
        (arrived,),
        flops=1 << 24,
        limit=16 << 20,
    )
    summed = lax.all_to_all(shares, ("ew", "ns"), 0, 0, tiled=True)
    summed = summed[: GRAD_ROWS // rows_each]
    token_grad, grad_proj, grad_first, grad_second, grad_mask = call(
        functools.partial(finish_kernel, n_ns, capacity),
        (
            shape((n_ns * capacity, features), BF),
            shape((chans, features), F32),
            shape((4, 4, chans, chans), F32),
            shape((4, bands, 4, chans), F32),
            shape((features,), F32),
        ),
        (arrived, summed, proj),
        flops=1 << 20,
        limit=16 << 20,
    )
    return (token_grad[None, None], grad_proj.T, grad_first, grad_second.transpose(0, 2, 1, 3), grad_mask)


def solution(mesh):
    return jax.shard_map(
        functools.partial(per_device, mesh.shape["ew"], mesh.shape["ns"]),
        mesh=mesh,
        in_specs=(
            P("ns", "ew", None, None, None),
            P("ns", "ew", None, None),
            P("ns", "ew", None),
            P("ns", "ew", None, None, None),
            P(),
            P(),
            P(),
            P(),
            P(None, None, "ns", "ew"),
            P(None, None, "ns", "ew"),
        ),
        out_specs=(P("ns", "ew", None, None), P(), P(), P(), P()),
        check_vma=False,
    )
```

time: 55.1 us -> 52.6 us (0.955)
  starting transfers between devices: 7.26 us -> 4.33 us
  blocking collectives: 35.3 us -> 37.4 us
  local copies, waits for them, and re-layouts: 3.68 us -> 2.24 us
    ppermute x4, starting transfers between devices: 7.26 us -> 4.33 us  [swap(): lax.ppermute(block, axis, [(i, j) for i, j in pairs if 0 <= j < count])]
    all_to_all x1, blocking collectives: 22.9 us -> 25 us  [per_device(): arrived = lax.all_to_all(outgoing, ('ew', 'ns'), 0, 0, tiled=True)]
    unnamed x24 -> x20, local copies, waits for them, and re-layouts: 3.68 us -> 2.24 us
    pallas_call x6 -> x8, Pallas kernels: 7.29 us -> 7.48 us  [call(): pl.pallas_call(kernel, out_shape=outs, in_specs=specs or [VMEM] * len(arg...]
  transfers between devices with their start and end apart: 4 -> 4, of which waited for: 1 -> 0; matrix products, arithmetic and copies ran while one was open for 0% -> 0% of each run, Pallas kernels for 3% -> 7%
where the time goes in v3:
time: 52.6 us; the launch traced here: 52.3 us
  blocking collectives  37.4 us (71%)
  Pallas kernels  7.48 us (14%)
  starting transfers between devices  4.33 us (8%)
  local copies, waits for them, and re-layouts  2.24 us (4%)
  between operations  0.81 us (2%)
    all_to_all x1, blocking collectives, per_device(): arrived = lax.all_to_all(outgoing, ('ew', 'ns'), 0, 0, tiled=True)  25 us
    all_to_all x1, blocking collectives, per_device(): summed = lax.all_to_all(shares, ('ew', 'ns'), 0, 0, tiled=True)  12.4 us
    pallas_call x8, Pallas kernels, call(): pl.pallas_call(kernel, out_shape=outs, in_specs=specs or [VMEM] * len(arg...  7.48 us
    ppermute x4, starting transfers between devices, swap(): lax.ppermute(block, axis, [(i, j) for i, j in pairs if 0 <= j < count])  4.33 us
    unnamed x20, local copies, waits for them, and re-layouts  2.24 us
  transfers between devices with their start and end apart: 4, of which 0 were waited for; matrix products, arithmetic and copies ran while one was open for 0% of the time, Pallas kernels for 7%

profile of v3, /device:TPU:0, one launch (start us, length us, event | category | flops | bytes accessed | tf_op | source)
XLA Modules:
  0.0 52.3 jit_solution(756872641451979981)
XLA Ops:
  0.6 0.0 copy-start.8
  0.6 0.9 %copy-done.8 = bf16[2,64,8,128]{3,2,1,0:T(8,128)(2,1)S(1)} copy-done((bf16[2,64,8,128]{3,2,1,0:T(8,128)(2,1)S(1)}, bf16[2,64,8,128]{3,2,1,0:T(8,128)(2,1)}, u32[]{:S(2)}) %copy-start.8) | copy-done | bytes 262168
  1.6 0.0 copy-start.9
  1.6 0.3 shard_map.137
  1.9 0.6 %copy-done.9 = bf16[2,12,16,256]{3,2,1,0:T(8,128)(2,1)S(1)} copy-done((bf16[2,12,16,256]{3,2,1,0:T(8,128)(2,1)S(1)}, bf16[2,12,16,256]{3,2,1,0:T(8,128)(2,1)}, u32[]{:S(2)}) %copy-start.9) | copy-done | bytes 196632
  2.5 0.0 copy-start
  2.5 0.0 copy-start.1
  2.5 0.0 copy-start.2
  2.5 0.0 copy-start.3
  2.5 0.0 copy-start.6
  2.5 0.4 shard_map.138
  2.9 2.9 %collective-permute-start = (bf16[8,1024]{1,0:T(8,128)(2,1)S(1)}, bf16[8,1024]{1,0:T(8,128)(2,1)S(1)}, u32[]{:S(2)}, u32[]{:S(2)}) collective-permute-start(bf16[8,1024]{1,0:T(8,128)(2,1)S(1)} %get-tuple-element.41), channel_id=1, source_target_pairs={{0,8},{8,0},{16,24},{24,16},{1,9},{9,1},{17,25},{25,17},{2,10},{10... | collective-permute-start | bytes 49160 | tf_op jit(solution)/shard_map/ppermute | solution.py:530
  5.9 0.7 %collective-permute-start.1 = (bf16[8,1024]{1,0:T(8,128)(2,1)S(1)}, bf16[8,1024]{1,0:T(8,128)(2,1)S(1)}, u32[]{:S(2)}, u32[]{:S(2)}) collective-permute-start(bf16[8,1024]{1,0:T(8,128)(2,1)S(1)} %get-tuple-element.41), channel_id=1, source_target_pairs={{8,16},{16,8},{9,17},{17,9},{10,18},{18,10},{11,19},{19,11},{12,20... | collective-permute-start | bytes 49160 | tf_op jit(solution)/shard_map/ppermute | solution.py:530
  6.5 0.0 copy-start.4
  6.5 0.0 copy-start.5
  6.5 0.0 copy-start.7
  6.5 0.0 copy-done
  6.6 0.0 copy-done.1
  6.6 0.0 copy-done.2
  6.6 0.0 copy-done.3
  6.6 0.0 copy-done.6
  6.6 0.6 %copy-done.4 = bf16[768]{0:T(1024)(128)(2,1)S(1)} copy-done((bf16[768]{0:T(1024)(128)(2,1)S(1)}, bf16[768]{0:T(1024)(128)(2,1)}, u32[]{:S(2)}) %copy-start.4) | copy-done | bytes 1560
  7.2 0.0 copy-done.5
  7.2 0.0 copy-done.7
  7.2 1.7 %shard_map.139 = (bf16[48,512]{1,0:T(8,128)(2,1)S(1)}, bf16[64,256]{1,0:T(8,128)(2,1)S(1)}, bf16[48,512]{1,0:T(8,128)(2,1)S(1)}, bf16[64,256]{1,0:T(8,128)(2,1)S...) custom-call(s32[1,2]{1,0:T(1,128)S(1)} %bitcast.18, ...), custom_call_target="tpu_custom_call" | custom-call | flops 16777216 | bytes 1048576 | tf_op jit(solution)/shard_map/pallas_call | solution.py:534
  8.9 0.0 collective-permute-done.sa_ref.ea_ref
  8.9 0.0 collective-permute-done.1.sb_ref.eb_ref
  9.0 0.1 collective-permute-start.2
  9.0 0.7 %collective-permute-start.3 = (bf16[64,768]{1,0:T(8,128)(2,1)S(1)}, bf16[64,768]{1,0:T(8,128)(2,1)S(1)}, u32[]{:S(2)}, u32[]{:S(2)}) collective-permute-start(bf16[64,768]{1,0:T(8,128)(2,1)S(1)} %get-tuple-element.43), channel_id=1, source_target_pairs={{1,2},{2,1},{3,4},{4,3},{5,6},{6,5},{9,10},{10,9},{11,12},{12,11},... | collective-permute-start | bytes 294920 | tf_op jit(solution)/shard_map/ppermute | solution.py:530
  9.7 1.9 %shard_map.141 = (bf16[512,256]{1,0:T(8,128)(2,1)S(1)}, f32[128,128]{1,0:T(8,128)S(1)}, f32[512,128]{1,0:T(8,128)S(1)}, f32[2,128,256]{2,1,0:T(8,128)S(1)}, bf16...) custom-call(bf16[512,256]{1,0:T(8,128)(2,1)S(1)} %get-tuple-element.35.g_ref, ...), custom_call_target="tpu_custom_call" | custom-call | flops 134217728 | bytes 1048576 | tf_op jit(solution)/shard_map/pallas_call | solution.py:534
  11.6 0.0 collective-permute-done.2.ra_ref
  11.7 0.0 collective-permute-done.3.rb_ref
  11.7 1.7 %shard_map.142 = bf16[32,48,128]{2,1,0:T(8,128)(2,1)S(1)} custom-call(bf16[64,768]{1,0:T(8,128)(2,1)S(1)} %collective-permute-done.2.ra_ref, bf16[64,768]{1,0:T(8,128)(2,1)S(1)} %collective-permute-done.3.rb_ref, bf16[384,1024]{1,0:T(8,128)(2,1)S(1)} %get-tuple-element.44.pix_ref, bf16[256,256]{1,0:T(8,128)(2,1)S(1)} %get-tuple-element.45.cell_ref, ...), custom_call_target="tpu_custom_call" | custom-call | flops 134217728 | bytes 1048576 | tf_op jit(solution)/shard_map/pallas_call | solution.py:534
  13.4 25.0 %all_to_all.10.got_ref.arrived_ref = bf16[32,48,128]{2,1,0:T(8,128)(2,1)S(1)} all-to-all(bf16[32,48,128]{2,1,0:T(8,128)(2,1)S(1)} %shard_map.142), channel_id=1, replica_groups=mesh['ew'=4,'ns'=8] {'ew','ns'}, dimensions={0} | all-to-all | bytes 786432 | tf_op jit(solution)/shard_map/all_to_all | solution.py:660
  38.4 0.1 shard_map.143
  38.5 12.4 %all_to_all.11.got_ref = bf16[32,32,128]{2,1,0:T(8,128)(2,1)S(1)} all-to-all(bf16[32,32,128]{2,1,0:T(8,128)(2,1)S(1)} %shard_map.143), channel_id=1, replica_groups=mesh['ew'=4,'ns'=8] {'ew','ns'}, dimensions={0} | all-to-all | bytes 524288 | tf_op jit(solution)/shard_map/all_to_all | solution.py:668
  50.9 1.4 %shard_map.144 = (bf16[192,768]{1,0:T(8,128)(2,1)}, f32[64,768]{1,0:T(8,128)}, f32[4,4,64,64]{3,2,1,0:T(8,128)}, f32[4,12,4,64]{3,2,1,0:T(4,128)}, f32[768]{0:T(1024)}) custom-call(bf16[32,48,128]{2,1,0:T(8,128)(2,1)S(1)} %all_to_all.10.got_ref.arrived_ref, bf16[32,32,128]{2,1,0:T(8,128)(2,1)S(1)} %all_to_all.11.got_ref, bf16[64,768]{1,0:T(8,128)(2,1)S(1)} %bitcast.14), custom_call_target="tpu_custom_call" | custom-call | flops 1048576 | bytes 1048576 | tf_op jit(solution)/shard_map/pallas_call | solution.py:534
  (1 shorter events, 0.0 us)
Async XLA Ops:
  0.6 1.0 %copy-start.8 = (bf16[2,64,8,128]{3,2,1,0:T(8,128)(2,1)S(1)}, bf16[2,64,8,128]{3,2,1,0:T(8,128)(2,1)}, u32[]{:S(2)}) copy-start(bf16[2,64,8,128]{3,2,1,0:T(8,128)(2,1)} %pre_ref.1) | copy-start | bytes 786436
  1.6 0.9 %copy-start.9 = (bf16[2,12,16,256]{3,2,1,0:T(8,128)(2,1)S(1)}, bf16[2,12,16,256]{3,2,1,0:T(8,128)(2,1)}, u32[]{:S(2)}) copy-start(bf16[2,12,16,256]{3,2,1,0:T(8,128)(2,1)} %cot_ref.1) | copy-start | bytes 589828
  2.5 4.0 %copy-start = (bf16[1,1,2,64,768]{4,3,2,1,0:T(8,128)(2,1)S(1)}, bf16[1,1,2,64,768]{4,3,2,1,0:T(8,128)(2,1)}, u32[]{:S(2)}) copy-start(bf16[1,1,2,64,768]{4,3,2,1,0:T(8,128)(2,1)} %param.10) | copy-start | bytes 589828
  2.5 4.0 %copy-start.1 = (bf16[768,64]{0,1:T(8,128)(2,1)S(1)}, bf16[768,64]{0,1:T(8,128)(2,1)}, u32[]{:S(2)}) copy-start(bf16[768,64]{0,1:T(8,128)(2,1)} %param.15) | copy-start | bytes 294916
  2.5 4.1 %copy-start.2 = (bf16[4,4,64,64]{3,2,1,0:T(8,128)(2,1)S(1)}, bf16[4,4,64,64]{3,2,1,0:T(8,128)(2,1)}, u32[]{:S(2)}) copy-start(bf16[4,4,64,64]{3,2,1,0:T(8,128)(2,1)} %first_ref.1) | copy-start | bytes 393220
  2.5 4.1 %copy-start.3 = (bf16[4,4,12,64]{3,1,2,0:T(4,128)(2,1)S(1)}, bf16[4,4,12,64]{3,1,2,0:T(4,128)(2,1)}, u32[]{:S(2)}) copy-start(bf16[4,4,12,64]{3,1,2,0:T(4,128)(2,1)} %param.17) | copy-start | bytes 73732
  2.5 4.1 %copy-start.6 = (s32[1,1,2,64,1]{3,4,2,1,0:T(1,128)S(1)}, s32[1,1,2,64,1]{3,4,2,1,0:T(1,128)}, u32[]{:S(2)}) copy-start(s32[1,1,2,64,1]{3,4,2,1,0:T(1,128)} %param.13) | copy-start | bytes 1540
  2.9 6.0 %collective-permute-start = (bf16[8,1024]{1,0:T(8,128)(2,1)S(1)}, bf16[8,1024]{1,0:T(8,128)(2,1)S(1)}, u32[]{:S(2)}, u32[]{:S(2)}) collective-permute-start(bf16[8,1024]{1,0:T(8,128)(2,1)S(1)} %get-tuple-element.41), channel_id=1, source_target_pairs={{0,8},{8,0},{16,24},{24,16},{1,9},{9,1},{17,25},{25,17},{2,10},{10... | collective-permute-start | bytes 49160 | tf_op jit(solution)/shard_map/ppermute | solution.py:530
  5.9 3.1 %collective-permute-start.1 = (bf16[8,1024]{1,0:T(8,128)(2,1)S(1)}, bf16[8,1024]{1,0:T(8,128)(2,1)S(1)}, u32[]{:S(2)}, u32[]{:S(2)}) collective-permute-start(bf16[8,1024]{1,0:T(8,128)(2,1)S(1)} %get-tuple-element.41), channel_id=1, source_target_pairs={{8,16},{16,8},{9,17},{17,9},{10,18},{18,10},{11,19},{19,11},{12,20... | collective-permute-start | bytes 49160 | tf_op jit(solution)/shard_map/ppermute | solution.py:530
  6.5 0.7 %copy-start.4 = (bf16[768]{0:T(1024)(128)(2,1)S(1)}, bf16[768]{0:T(1024)(128)(2,1)}, u32[]{:S(2)}) copy-start(bf16[768]{0:T(1024)(128)(2,1)} %mask_ref.3) | copy-start | bytes 4612
  6.5 0.7 %copy-start.5 = (s32[1,1,2,64]{3,2,1,0:T(2,128)S(1)}, s32[1,1,2,64]{3,2,1,0:T(2,128)}, u32[]{:S(2)}) copy-start(s32[1,1,2,64]{3,2,1,0:T(2,128)} %param.11) | copy-start | bytes 1540
  6.5 0.7 %copy-start.7 = (s32[1,1,2]{2,1,0:T(1,128)S(1)}, s32[1,1,2]{2,1,0:T(1,128)}, u32[]{:S(2)}) copy-start(s32[1,1,2]{2,1,0:T(1,128)} %param.12) | copy-start | bytes 28
  9.0 2.7 %collective-permute-start.2 = (bf16[64,768]{1,0:T(8,128)(2,1)S(1)}, bf16[64,768]{1,0:T(8,128)(2,1)S(1)}, u32[]{:S(2)}, u32[]{:S(2)}) collective-permute-start(bf16[64,768]{1,0:T(8,128)(2,1)S(1)} %get-tuple-element.42), channel_id=1, source_target_pairs={{0,1},{1,0},{2,3},{3,2},{4,5},{5,4},{6,7},{7,6},{8,9},{9,8},{10,11... | collective-permute-start | bytes 294920 | tf_op jit(solution)/shard_map/ppermute | solution.py:530
  9.0 2.6 %collective-permute-start.3 = (bf16[64,768]{1,0:T(8,128)(2,1)S(1)}, bf16[64,768]{1,0:T(8,128)(2,1)S(1)}, u32[]{:S(2)}, u32[]{:S(2)}) collective-permute-start(bf16[64,768]{1,0:T(8,128)(2,1)S(1)} %get-tuple-element.43), channel_id=1, source_target_pairs={{1,2},{2,1},{3,4},{4,3},{5,6},{6,5},{9,10},{10,9},{11,12},{12,11},... | collective-permute-start | bytes 294920 | tf_op jit(solution)/shard_map/ppermute | solution.py:530

commit v4 on v3

--- a/solution.py
+++ b/solution.py
@@ -141,8 +141,8 @@
     frames, slots, patches = pick_ref.shape
     chans = proj_ref.shape[0]
     bands = second_ref.shape[1]
-    owners = route_ref.shape[0] // GROUP
-    half = capacity // 2
+    slot_rows = -(-capacity // 8) * 8
+    owners = route_ref.shape[0] // slot_rows
     eye = (iota((chans, chans), 0) == iota((chans, chans), 1)).astype(BF)
     pad = jnp.zeros((GROUP - bands, chans), F32)
     taps = []
@@ -199,12 +199,9 @@
     before = (iota(square, 0) < iota(square, 1)).astype(BF)
     earlier = nn(hit.astype(BF), before)
     place = jnp.sum(earlier * hit, axis=0, keepdims=True).astype(jnp.int32)
-    for h in range(2):
-        inside = (live > 0) & (place >= h * half) & (place < (h + 1) * half)
-        target = jnp.where(inside, owner * GROUP + place - h * half, -1)
-        route_ref[:, h * slots_all : (h + 1) * slots_all] = (
-            iota((owners * GROUP, slots_all), 0) == target
-        ).astype(F32).astype(BF)
+    block = lax.rem(owner, 2) * (owners // 2) + owner // 2
+    target = jnp.where(live > 0, block * slot_rows + place, -1)
+    route_ref[...] = (iota((owners * slot_rows, slots_all), 0) == target).astype(F32).astype(BF)
 
 
 def side_columns(ea_ref, eb_ref, even_ew):
@@ -322,10 +319,10 @@
 
 
 def outer_kernel(
-    n_ew, rows_each, ra_ref, rb_ref, pix_ref, cell_ref,
+    n_ew, n_ns, ra_ref, rb_ref, pix_ref, cell_ref,
     delta_ref, second_ref, first_ref, turn_ref, edge_ref, pre_ref,
     grid_ref, pick_ref, hidden_ref, route_ref, wab_ref, w2_ref, tokens_ref, mask_ref,
-    out_ref, ext, wide, wins, pres, routed,
+    keep_ref, give_ref, ext, wide, wins, pres,
 ):
     frames, slots, patches = pick_ref.shape
     chans = w2_ref.shape[0]
@@ -333,7 +330,6 @@
     cols = pre_ref.shape[3] // 2
     pcol = 2 * cols
     deep = 3 * GROUP
-    n_ns = route_ref.shape[0] // GROUP
     ns = lax.axis_index("ns")
     ew = lax.axis_index("ew")
     even_ns = lax.rem(ns, 2) == 0
@@ -408,11 +404,11 @@
         grids.append(jnp.concatenate(parts, axis=1).astype(BF))
     none = jnp.zeros((chans, patches), BF)
     mask_sum = nt(hidden_ref[...], jnp.concatenate(grids, axis=1))
-    lower = [nt(pick_ref[f], jnp.concatenate([grids[f], none], axis=0)) for f in range(frames)]
-    upper = [nt(pick_ref[f], jnp.concatenate([none, grids[f]], axis=0)) for f in range(frames)]
-    chosen = jnp.concatenate(lower + upper, axis=0).astype(BF)
-    routed[...] = nn(route_ref[...], chosen).astype(BF)
-    features = tokens_ref.shape[1]
+    chosen = [nt(pick_ref[f], jnp.concatenate([grids[f], none], axis=0)) for f in range(frames)]
+    chosen = jnp.concatenate(chosen, axis=0)
+    placed = jnp.where(even_ns, chosen, pltpu.roll(chosen, chans, 1)).astype(BF)
+    chosen = chosen.astype(BF)
+    routed = nn(route_ref[...], placed)
     hi = mask_sum.astype(BF).astype(F32)
     lo = mask_sum - hi
     line = iota(hi.shape, 0)
@@ -420,31 +416,48 @@
     line = iota((16, features), 0)
     mask_row = mask_ref[...].astype(F32).reshape(1, features)
     spread_row = jnp.where(line < 2, mask_row, 0.0).astype(BF)
-    slots_all = tokens_ref.shape[0]
-    grad_proj = tn(chosen[:slots_all, :chans], tokens_ref[...]) + tn(mask_rows, spread_row)
+    grad_proj = tn(chosen[:, :chans], tokens_ref[...]) + tn(mask_rows, spread_row)
     grad_proj = [grad_proj[:, k * 128 : (k + 1) * 128] for k in range(features // 128)]
     both = jnp.concatenate([hi[0:1], lo[0:1]], axis=1)
     mark = iota(grad_second.shape, 0) == MASK_ROW - SECOND_AT
     grad_second = jnp.where(mark, both, grad_second)
-    total = jnp.concatenate([grad_first, *grad_proj, grad_second], axis=0).astype(BF)
+    halves = (grad_first, jnp.concatenate([*grad_proj, grad_second], axis=0))
+    part = routed.shape[0] // 2
+
+    def split(mine):
+        keep_ref[: GRAD_ROWS // 2, :] = halves[mine]
+        keep_ref[GRAD_ROWS // 2 :, :] = routed[mine * part : (mine + 1) * part]
+        give_ref[: GRAD_ROWS // 2, :] = halves[1 - mine].astype(BF)
+        give_ref[GRAD_ROWS // 2 :, :] = routed[(1 - mine) * part : (2 - mine) * part].astype(BF)
+
+    @pl.when(even_ns)
+    def _():
+        split(0)
+
+    @pl.when(jnp.logical_not(even_ns))
+    def _():
+        split(1)
+
+
+def chip_kernel(rows_each, keep_ref, got_ref, out_ref):
     count = out_ref.shape[0]
-    for d in range(GRAD_ROWS // rows_each):
+    slot_rows = out_ref.shape[1] - rows_each
+    grads = GRAD_ROWS // 2
+    chips = (keep_ref.shape[0] - grads) // slot_rows
+    total = (keep_ref[...] + got_ref[...].astype(F32)).astype(BF)
+    full = min(count, grads // rows_each)
+    for d in range(full):
         out_ref[d, :rows_each, :] = total[d * rows_each : (d + 1) * rows_each]
-    if count * rows_each > GRAD_ROWS:
-
-        @pl.loop(GRAD_ROWS // rows_each, count)
+    if full < count:
+
+        @pl.loop(full, count)
         def _(d):
-            out_ref[d, :rows_each, :] = jnp.zeros((rows_each, 2 * chans), BF)
-
-    def place(d):
-        source = pl.multiple_of(lax.rem(d, n_ns) * GROUP, GROUP)
-        out_ref[d, rows_each:, :] = routed[pl.ds(source, GROUP), :]
-
-    if count <= 64:
-        for d in range(count):
-            out_ref[d, rows_each:, :] = routed[pl.ds((d % n_ns) * GROUP, GROUP), :]
-    else:
-        pl.loop(0, count)(place)
+            out_ref[d, :rows_each, :] = jnp.zeros((rows_each, total.shape[1]), BF)
+
+    for z in range(chips):
+        rows = total[grads + z * slot_rows : grads + (z + 1) * slot_rows]
+        for e in range(count // chips):
+            out_ref[e * chips + z, rows_each:, :] = rows
 
 
 def sum_kernel(rows_each, got_ref, sum_ref):
@@ -471,32 +484,32 @@
             sum_ref[d] = share
 
 
-def owner_rows(n_ns, capacity, rows_each, arrived_ref, proj_ref, token_ref):
+def owner_kernel(capacity, rows_each, arrived_ref, proj_ref, token_ref):
     chans = proj_ref.shape[0]
-    half = capacity // 2
+    slot_rows = arrived_ref.shape[1] - rows_each
+    chips = token_ref.shape[0] // (2 * capacity)
     ew = lax.axis_index("ew")
-    arrived = jnp.concatenate(
-        [arrived_ref[ew * n_ns + s, rows_each:, :] for s in range(n_ns)], axis=0
-    )
-    shape = (n_ns * capacity, n_ns * GROUP)
+    arrived = [arrived_ref[ew * chips + z, rows_each:, :].astype(F32) for z in range(chips)]
+    arrived = jnp.concatenate(arrived, axis=0).astype(BF)
+    shape = (token_ref.shape[0], chips * slot_rows)
     row, col = iota(shape, 0), iota(shape, 1)
-    slot = lax.rem(row, capacity)
-    source = (row // capacity) * GROUP + lax.rem(slot, half)
+    source = (row // (2 * capacity)) * slot_rows + lax.rem(row, capacity)
     picked = nn((source == col).astype(F32).astype(BF), arrived)
-    second = lax.rem(iota(picked.shape, 0), capacity) >= half
+    second = lax.rem(iota(picked.shape, 0) // capacity, 2) == 1
     picked = jnp.where(second, pltpu.roll(picked, chans, 1), picked)[:, :chans].astype(BF)
     token_ref[...] = nn(picked, proj_ref[...]).astype(BF)
 
 
-def finish_kernel(
-    n_ns, capacity, arrived_ref, got_ref, proj_ref, token_out, proj_out, first_out, second_out, mask_out
-):
-    owner_rows(n_ns, capacity, got_ref.shape[1], arrived_ref, proj_ref, token_out)
+def finish_kernel(mine_ref, other_ref, proj_ref, proj_out, first_out, second_out, mask_out):
     chans, features = proj_ref.shape
     bands = second_out.shape[1]
-    rows_each = got_ref.shape[1]
-    parts = [got_ref[d] for d in range(GRAD_ROWS // rows_each)]
-    total = jnp.concatenate(parts, axis=0).astype(F32)
+    rows_each = mine_ref.shape[1]
+    blocks = range(GRAD_ROWS // 2 // rows_each)
+    mine = jnp.concatenate([mine_ref[d] for d in blocks], axis=0)
+    other = jnp.concatenate([other_ref[d] for d in blocks], axis=0)
+    even = lax.rem(lax.axis_index("ns"), 2) == 0
+    total = [jnp.where(even, mine, other), jnp.where(even, other, mine)]
+    total = jnp.concatenate(total, axis=0).astype(F32)
     for arrangement, taps in enumerate(((1, 2), (3, 0))):
         rows = total[arrangement * 4 * chans : (arrangement + 1) * 4 * chans]
         turned = pltpu.roll(rows, chans, 1)
@@ -553,6 +566,8 @@
     capacity = 3 * frames * slots // (2 * n_ns)
     rows_each = -(-GRAD_ROWS // count)
     rows_each = -(-rows_each // 16) * 16
+    slot_rows = -(-capacity // 8) * 8
+    groups = [[e * n_ns + z * 2 + c for e in range(n_ew) for z in range(n_ns // 2)] for c in range(2)]
     slots_all = frames * slots
     shape = jax.ShapeDtypeStruct
 
@@ -588,7 +603,7 @@
             shape((frames, 2, 2 * chans, 2 * cols), BF),
             shape((frames, slots, patches), BF),
             shape((16, frames * patches), BF),
-            shape((n_ns * GROUP, 2 * slots_all), BF),
+            shape((n_ns * slot_rows, slots_all), BF),
             shape((2 * chans, 8 * chans), BF),
             shape((chans, 16 * GROUP), BF),
             shape((pcol + 128, 4 * pcol), BF),
@@ -640,9 +655,10 @@
         limit=16 << 20,
     )
     beyond = frames * 2 * 3 * GROUP
-    outgoing = call(
-        functools.partial(outer_kernel, n_ew, rows_each),
-        shape((count, rows_each + GROUP, 2 * chans), BF),
+    half_rows = GRAD_ROWS // 2 + n_ns // 2 * slot_rows
+    keep, give = call(
+        functools.partial(outer_kernel, n_ew, n_ns),
+        (shape((half_rows, 2 * chans), F32), shape((half_rows, 2 * chans), BF)),
         (
             got_a, got_b, pixels, cells, delta_mid, second_mid, first_mid, turn_mid, edge_wins, edge_pre,
             grid, picks, hidden, route, wab, w2, tile_tokens, mask_token,
@@ -652,33 +668,45 @@
             pltpu.VMEM((frames * 2 * chans, 2 * cols), BF),
             pltpu.VMEM((beyond, 8 * cols), BF),
             pltpu.VMEM((frames * 2 * chans, 2 * cols), F32),
-            pltpu.VMEM((n_ns * GROUP, 2 * chans), BF),
         ],
         flops=1 << 27,
         limit=24 << 20,
     )
-    arrived = lax.all_to_all(outgoing, ("ew", "ns"), 0, 0, tiled=True)
+
+    def exchange(blocks):
+        return lax.all_to_all(blocks, ("ew", "ns"), 0, 0, axis_index_groups=groups, tiled=True)
+
+    outgoing = call(
+        functools.partial(chip_kernel, rows_each),
+        shape((count // 2, rows_each + slot_rows, 2 * chans), BF),
+        (keep, swap(give, "ns", 0)),
+        flops=1 << 20,
+    )
+    arrived = exchange(outgoing)
     shares = call(
         functools.partial(sum_kernel, rows_each),
-        shape((count, rows_each, 2 * chans), BF),
+        shape((count // 2, rows_each, 2 * chans), BF),
         (arrived,),
-        flops=1 << 24,
-        limit=16 << 20,
-    )
-    summed = lax.all_to_all(shares, ("ew", "ns"), 0, 0, tiled=True)
-    summed = summed[: GRAD_ROWS // rows_each]
-    token_grad, grad_proj, grad_first, grad_second, grad_mask = call(
-        functools.partial(finish_kernel, n_ns, capacity),
+        flops=1 << 20,
+    )
+    summed = exchange(shares)[: GRAD_ROWS // 2 // rows_each]
+    other = swap(summed, "ns", 0)
+    token_grad = call(
+        functools.partial(owner_kernel, capacity, rows_each),
+        shape((n_ns * capacity, features), BF),
+        (arrived, proj),
+        flops=1 << 27,
+    )
+    grad_proj, grad_first, grad_second, grad_mask = call(
+        finish_kernel,
         (
-            shape((n_ns * capacity, features), BF),
             shape((chans, features), F32),
             shape((4, 4, chans, chans), F32),
             shape((4, bands, 4, chans), F32),
             shape((features,), F32),
         ),
-        (arrived, summed, proj),
+        (summed, other, proj),
         flops=1 << 20,
-        limit=16 << 20,
     )
     return (token_grad[None, None], grad_proj.T, grad_first, grad_second.transpose(0, 2, 1, 3), grad_mask)
 

time: 52.6 us -> 50.5 us (0.960)
  blocking collectives: 37.4 us -> 29.5 us
  starting transfers between devices: 4.33 us -> 8.22 us
  waiting for transfers between devices: 0.01 us -> 1.23 us
  Pallas kernels: 7.48 us -> 8.24 us
    all_to_all x2, blocking collectives: 37.4 us -> 29.5 us  [exchange(): lax.all_to_all(blocks, ('ew', 'ns'), 0, 0, axis_index_groups=groups, tile...]
    ppermute x4 -> x6, starting transfers between devices: 4.33 us -> 8.22 us  [swap(): lax.ppermute(block, axis, [(i, j) for i, j in pairs if 0 <= j < count])]
    ppermute x4 -> x6, waiting for transfers between devices: 0.01 us -> 1.23 us  [swap(): lax.ppermute(block, axis, [(i, j) for i, j in pairs if 0 <= j < count])]
    pallas_call x8 -> x10, Pallas kernels: 7.48 us -> 8.24 us  [call(): pl.pallas_call(kernel, out_shape=outs, in_specs=specs or [VMEM] * len(arg...]
  transfers between devices with their start and end apart: 4 -> 6, of which waited for: 0 -> 2; matrix products, arithmetic and copies ran while one was open for 0% -> 0% of each run, Pallas kernels for 7% -> 9%
where the time goes in v4:
time: 50.5 us; the launch traced here: 50.2 us
  blocking collectives  29.5 us (58%)
  Pallas kernels  8.24 us (16%)
  starting transfers between devices  8.22 us (16%)
  local copies, waits for them, and re-layouts  2.24 us (4%)
  waiting for transfers between devices  1.23 us (2%)
  between operations  0.82 us (2%)
    all_to_all x2, blocking collectives, exchange(): lax.all_to_all(blocks, ('ew', 'ns'), 0, 0, axis_index_groups=groups, tile...  29.5 us
    pallas_call x10, Pallas kernels, call(): pl.pallas_call(kernel, out_shape=outs, in_specs=specs or [VMEM] * len(arg...  8.24 us
    ppermute x6, starting transfers between devices, swap(): lax.ppermute(block, axis, [(i, j) for i, j in pairs if 0 <= j < count])  8.22 us
    unnamed x20, local copies, waits for them, and re-layouts  2.24 us
    ppermute x6, waiting for transfers between devices, swap(): lax.ppermute(block, axis, [(i, j) for i, j in pairs if 0 <= j < count])  1.23 us
  transfers between devices with their start and end apart: 6, of which 2 were waited for; matrix products, arithmetic and copies ran while one was open for 0% of the time, Pallas kernels for 9%

profile of v4, /device:TPU:0, one launch (start us, length us, event | category | flops | bytes accessed | tf_op | source)
XLA Modules:
  0.0 50.2 jit_solution(955024728431398523)
XLA Ops:
  0.6 0.0 copy-start.8
  0.6 0.9 %copy-done.8 = bf16[2,64,8,128]{3,2,1,0:T(8,128)(2,1)S(1)} copy-done((bf16[2,64,8,128]{3,2,1,0:T(8,128)(2,1)S(1)}, bf16[2,64,8,128]{3,2,1,0:T(8,128)(2,1)}, u32[]{:S(2)}) %copy-start.8) | copy-done | bytes 262168
  1.6 0.0 copy-start.9
  1.6 0.3 shard_map.137
  1.9 0.6 %copy-done.9 = bf16[2,12,16,256]{3,2,1,0:T(8,128)(2,1)S(1)} copy-done((bf16[2,12,16,256]{3,2,1,0:T(8,128)(2,1)S(1)}, bf16[2,12,16,256]{3,2,1,0:T(8,128)(2,1)}, u32[]{:S(2)}) %copy-start.9) | copy-done | bytes 196632
  2.5 0.0 copy-start
  2.5 0.0 copy-start.1
  2.5 0.0 copy-start.2
  2.5 0.0 copy-start.3
  2.5 0.0 copy-start.6
  2.5 0.4 shard_map.138
  2.9 2.9 %collective-permute-start = (bf16[8,1024]{1,0:T(8,128)(2,1)S(1)}, bf16[8,1024]{1,0:T(8,128)(2,1)S(1)}, u32[]{:S(2)}, u32[]{:S(2)}) collective-permute-start(bf16[8,1024]{1,0:T(8,128)(2,1)S(1)} %get-tuple-element.42), channel_id=1, source_target_pairs={{0,8},{8,0},{16,24},{24,16},{1,9},{9,1},{17,25},{25,17},{2,10},{10... | collective-permute-start | bytes 49160 | tf_op jit(solution)/shard_map/ppermute | solution.py:543
  5.9 0.7 %collective-permute-start.1 = (bf16[8,1024]{1,0:T(8,128)(2,1)S(1)}, bf16[8,1024]{1,0:T(8,128)(2,1)S(1)}, u32[]{:S(2)}, u32[]{:S(2)}) collective-permute-start(bf16[8,1024]{1,0:T(8,128)(2,1)S(1)} %get-tuple-element.42), channel_id=1, source_target_pairs={{8,16},{16,8},{9,17},{17,9},{10,18},{18,10},{11,19},{19,11},{12,20... | collective-permute-start | bytes 49160 | tf_op jit(solution)/shard_map/ppermute | solution.py:543
  6.5 0.0 copy-start.4
  6.5 0.0 copy-start.5
  6.5 0.0 copy-start.7
  6.6 0.0 copy-done
  6.6 0.0 copy-done.1
  6.6 0.0 copy-done.2
  6.6 0.0 copy-done.3
  6.6 0.0 copy-done.6
  6.6 0.6 %copy-done.4 = bf16[768]{0:T(1024)(128)(2,1)S(1)} copy-done((bf16[768]{0:T(1024)(128)(2,1)S(1)}, bf16[768]{0:T(1024)(128)(2,1)}, u32[]{:S(2)}) %copy-start.4) | copy-done | bytes 1560
  7.2 0.0 copy-done.5
  7.2 0.0 copy-done.7
  7.2 1.7 %shard_map.139 = (bf16[48,512]{1,0:T(8,128)(2,1)S(1)}, bf16[64,256]{1,0:T(8,128)(2,1)S(1)}, bf16[48,512]{1,0:T(8,128)(2,1)S(1)}, bf16[64,256]{1,0:T(8,128)(2,1)S...) custom-call(s32[1,2]{1,0:T(1,128)S(1)} %bitcast.19, ...), custom_call_target="tpu_custom_call" | custom-call | flops 16777216 | bytes 1048576 | tf_op jit(solution)/shard_map/pallas_call | solution.py:547
  8.9 0.0 collective-permute-done.sa_ref.ea_ref
  8.9 0.0 collective-permute-done.1.sb_ref.eb_ref
  9.0 0.1 collective-permute-start.2
  9.1 0.7 %collective-permute-start.3 = (bf16[64,768]{1,0:T(8,128)(2,1)S(1)}, bf16[64,768]{1,0:T(8,128)(2,1)S(1)}, u32[]{:S(2)}, u32[]{:S(2)}) collective-permute-start(bf16[64,768]{1,0:T(8,128)(2,1)S(1)} %get-tuple-element.44), channel_id=1, source_target_pairs={{1,2},{2,1},{3,4},{4,3},{5,6},{6,5},{9,10},{10,9},{11,12},{12,11},... | collective-permute-start | bytes 294920 | tf_op jit(solution)/shard_map/ppermute | solution.py:543
  9.7 1.9 %shard_map.141 = (bf16[512,256]{1,0:T(8,128)(2,1)S(1)}, f32[128,128]{1,0:T(8,128)S(1)}, f32[512,128]{1,0:T(8,128)S(1)}, f32[2,128,256]{2,1,0:T(8,128)S(1)}, bf16...) custom-call(bf16[512,256]{1,0:T(8,128)(2,1)S(1)} %get-tuple-element.36.g_ref, ...), custom_call_target="tpu_custom_call" | custom-call | flops 134217728 | bytes 1048576 | tf_op jit(solution)/shard_map/pallas_call | solution.py:547
  11.6 0.0 collective-permute-done.2.ra_ref
  11.6 0.0 collective-permute-done.3.rb_ref
  11.7 1.8 %shard_map.142 = (f32[608,128]{1,0:T(8,128)S(1)}, bf16[608,128]{1,0:T(8,128)(2,1)S(1)}) custom-call(bf16[64,768]{1,0:T(8,128)(2,1)S(1)} %collective-permute-done.2.ra_ref, bf16[64,768]{1,0:T(8,128)(2,1)S(1)} %collective-permute-done.3.rb_ref, bf16[384,1024]{1,0:T(8,128)(2,1)S(1)} %get-tuple-element.45.pix_ref, ...), custom_call_target="tpu_custom_call" | custom-call | flops 134217728 | bytes 1048576 | tf_op jit(solution)/shard_map/pallas_call | solution.py:547
  13.5 3.9 %collective-permute-start.4 = (bf16[608,128]{1,0:T(8,128)(2,1)S(1)}, bf16[608,128]{1,0:T(8,128)(2,1)S(1)}, u32[]{:S(2)}, u32[]{:S(2)}) collective-permute-start(bf16[608,128]{1,0:T(8,128)(2,1)S(1)} %get-tuple-element.60), channel_id=1, source_target_pairs={{0,1},{1,0},{2,3},{3,2},{4,5},{5,4},{6,7},{7,6},{8,9},{9,8},{10,11... | collective-permute-start | bytes 466952 | tf_op jit(solution)/shard_map/ppermute | solution.py:543
  17.3 1.0 %collective-permute-done.4.got_ref = bf16[608,128]{1,0:T(8,128)(2,1)S(1)} collective-permute-done((bf16[608,128]{1,0:T(8,128)(2,1)S(1)}, bf16[608,128]{1,0:T(8,128)(2,1)S(1)}, u32[]{:S(2)}, u32[]{:S(2)}) %collective-permute-start.4) | collective-permute-done | bytes 155680 | tf_op jit(solution)/shard_map/ppermute | solution.py:543
  18.4 19.2 %all_to_all.10.arrived_ref.got_ref = bf16[16,56,128]{2,1,0:T(8,128)(2,1)S(1)} all-to-all(bf16[16,56,128]{2,1,0:T(8,128)(2,1)S(1)} %shard_map.143), channel_id=1, replica_groups={{0,2,4,6,8,10,12,14,16,18,20,22,24,26,28,30},{1,3,5,7,9,11,13,15,17,19,..., dimensions={0} | all-to-all | bytes 458752 | tf_op jit(solution)/shard_map/all_to_all | solution.py:677
  37.6 10.3 %all_to_all.11.mine_ref = bf16[16,32,128]{2,1,0:T(8,128)(2,1)S(1)} all-to-all(bf16[16,32,128]{2,1,0:T(8,128)(2,1)S(1)} %shard_map.145), channel_id=1, replica_groups={{0,2,4,6,8,10,12,14,16,18,20,22,24,26,28,30},{1,3,5,7,9,11,13,15,17,19,..., dimensions={0} | all-to-all | bytes 262144 | tf_op jit(solution)/shard_map/all_to_all | solution.py:677
  47.9 0.0 collective-permute-start.5
  47.9 1.1 %shard_map.144 = bf16[192,768]{1,0:T(8,128)(2,1)} custom-call(bf16[16,56,128]{2,1,0:T(8,128)(2,1)S(1)} %all_to_all.10.arrived_ref.got_ref, bf16[64,768]{1,0:T(8,128)(2,1)S(1)} %bitcast.12), custom_call_target="tpu_custom_call" | custom-call | flops 134217728 | bytes 1048576 | tf_op jit(solution)/shard_map/pallas_call | solution.py:547
  49.1 0.2 collective-permute-done.5.other_ref
  49.3 1.0 %shard_map.146 = (f32[64,768]{1,0:T(8,128)}, f32[4,4,64,64]{3,2,1,0:T(8,128)}, f32[4,12,4,64]{3,2,1,0:T(4,128)}, f32[768]{0:T(1024)}) custom-call(bf16[16,32,128]{2,1,0:T(8,128)(2,1)S(1)} %all_to_all.11.mine_ref, bf16[16,32,128]{2,1,0:T(8,128)(2,1)S(1)} %collective-permute-done.5.other_ref, bf16[64,768]{1,0:T(8,128)(2,1)S(1)} %bitcast.13), custom_call_target="tpu_custom_call" | custom-call | flops 1048576 | bytes 1048576 | tf_op jit(solution)/shard_map/pallas_call | solution.py:547
  (3 shorter events, 0.1 us)
Async XLA Ops:
  0.6 1.0 %copy-start.8 = (bf16[2,64,8,128]{3,2,1,0:T(8,128)(2,1)S(1)}, bf16[2,64,8,128]{3,2,1,0:T(8,128)(2,1)}, u32[]{:S(2)}) copy-start(bf16[2,64,8,128]{3,2,1,0:T(8,128)(2,1)} %pre_ref.1) | copy-start | bytes 786436
  1.6 0.9 %copy-start.9 = (bf16[2,12,16,256]{3,2,1,0:T(8,128)(2,1)S(1)}, bf16[2,12,16,256]{3,2,1,0:T(8,128)(2,1)}, u32[]{:S(2)}) copy-start(bf16[2,12,16,256]{3,2,1,0:T(8,128)(2,1)} %cot_ref.1) | copy-start | bytes 589828
  2.5 4.0 %copy-start = (bf16[768,64]{0,1:T(8,128)(2,1)S(1)}, bf16[768,64]{0,1:T(8,128)(2,1)}, u32[]{:S(2)}) copy-start(bf16[768,64]{0,1:T(8,128)(2,1)} %param.15) | copy-start | bytes 294916
  2.5 4.1 %copy-start.1 = (bf16[1,1,2,64,768]{4,3,2,1,0:T(8,128)(2,1)S(1)}, bf16[1,1,2,64,768]{4,3,2,1,0:T(8,128)(2,1)}, u32[]{:S(2)}) copy-start(bf16[1,1,2,64,768]{4,3,2,1,0:T(8,128)(2,1)} %param.10) | copy-start | bytes 589828
  2.5 4.1 %copy-start.2 = (bf16[4,4,64,64]{3,2,1,0:T(8,128)(2,1)S(1)}, bf16[4,4,64,64]{3,2,1,0:T(8,128)(2,1)}, u32[]{:S(2)}) copy-start(bf16[4,4,64,64]{3,2,1,0:T(8,128)(2,1)} %first_ref.1) | copy-start | bytes 393220
  2.5 4.1 %copy-start.3 = (bf16[4,4,12,64]{3,1,2,0:T(4,128)(2,1)S(1)}, bf16[4,4,12,64]{3,1,2,0:T(4,128)(2,1)}, u32[]{:S(2)}) copy-start(bf16[4,4,12,64]{3,1,2,0:T(4,128)(2,1)} %param.17) | copy-start | bytes 73732
  2.5 4.1 %copy-start.6 = (s32[1,1,2,64,1]{3,4,2,1,0:T(1,128)S(1)}, s32[1,1,2,64,1]{3,4,2,1,0:T(1,128)}, u32[]{:S(2)}) copy-start(s32[1,1,2,64,1]{3,4,2,1,0:T(1,128)} %param.13) | copy-start | bytes 1540
  2.9 6.0 %collective-permute-start = (bf16[8,1024]{1,0:T(8,128)(2,1)S(1)}, bf16[8,1024]{1,0:T(8,128)(2,1)S(1)}, u32[]{:S(2)}, u32[]{:S(2)}) collective-permute-start(bf16[8,1024]{1,0:T(8,128)(2,1)S(1)} %get-tuple-element.42), channel_id=1, source_target_pairs={{0,8},{8,0},{16,24},{24,16},{1,9},{9,1},{17,25},{25,17},{2,10},{10... | collective-permute-start | bytes 49160 | tf_op jit(solution)/shard_map/ppermute | solution.py:543
  5.9 3.1 %collective-permute-start.1 = (bf16[8,1024]{1,0:T(8,128)(2,1)S(1)}, bf16[8,1024]{1,0:T(8,128)(2,1)S(1)}, u32[]{:S(2)}, u32[]{:S(2)}) collective-permute-start(bf16[8,1024]{1,0:T(8,128)(2,1)S(1)} %get-tuple-element.42), channel_id=1, source_target_pairs={{8,16},{16,8},{9,17},{17,9},{10,18},{18,10},{11,19},{19,11},{12,20... | collective-permute-start | bytes 49160 | tf_op jit(solution)/shard_map/ppermute | solution.py:543
  6.5 0.7 %copy-start.4 = (bf16[768]{0:T(1024)(128)(2,1)S(1)}, bf16[768]{0:T(1024)(128)(2,1)}, u32[]{:S(2)}) copy-start(bf16[768]{0:T(1024)(128)(2,1)} %mask_ref.3) | copy-start | bytes 4612
  6.5 0.7 %copy-start.5 = (s32[1,1,2,64]{3,2,1,0:T(2,128)S(1)}, s32[1,1,2,64]{3,2,1,0:T(2,128)}, u32[]{:S(2)}) copy-start(s32[1,1,2,64]{3,2,1,0:T(2,128)} %param.11) | copy-start | bytes 1540
  6.5 0.7 %copy-start.7 = (s32[1,1,2]{2,1,0:T(1,128)S(1)}, s32[1,1,2]{2,1,0:T(1,128)}, u32[]{:S(2)}) copy-start(s32[1,1,2]{2,1,0:T(1,128)} %param.12) | copy-start | bytes 28
  9.0 2.7 %collective-permute-start.2 = (bf16[64,768]{1,0:T(8,128)(2,1)S(1)}, bf16[64,768]{1,0:T(8,128)(2,1)S(1)}, u32[]{:S(2)}, u32[]{:S(2)}) collective-permute-start(bf16[64,768]{1,0:T(8,128)(2,1)S(1)} %get-tuple-element.43), channel_id=1, source_target_pairs={{0,1},{1,0},{2,3},{3,2},{4,5},{5,4},{6,7},{7,6},{8,9},{9,8},{10,11... | collective-permute-start | bytes 294920 | tf_op jit(solution)/shard_map/ppermute | solution.py:543
  9.1 2.6 %collective-permute-start.3 = (bf16[64,768]{1,0:T(8,128)(2,1)S(1)}, bf16[64,768]{1,0:T(8,128)(2,1)S(1)}, u32[]{:S(2)}, u32[]{:S(2)}) collective-permute-start(bf16[64,768]{1,0:T(8,128)(2,1)S(1)} %get-tuple-element.44), channel_id=1, source_target_pairs={{1,2},{2,1},{3,4},{4,3},{5,6},{6,5},{9,10},{10,9},{11,12},{12,11},... | collective-permute-start | bytes 294920 | tf_op jit(solution)/shard_map/ppermute | solution.py:543
  13.5 4.9 %collective-permute-start.4 = (bf16[608,128]{1,0:T(8,128)(2,1)S(1)}, bf16[608,128]{1,0:T(8,128)(2,1)S(1)}, u32[]{:S(2)}, u32[]{:S(2)}) collective-permute-start(bf16[608,128]{1,0:T(8,128)(2,1)S(1)} %get-tuple-element.60), channel_id=1, source_target_pairs={{0,1},{1,0},{2,3},{3,2},{4,5},{5,4},{6,7},{7,6},{8,9},{9,8},{10,11... | collective-permute-start | bytes 466952 | tf_op jit(solution)/shard_map/ppermute | solution.py:543
  47.9 1.3 %collective-permute-start.5 = (bf16[16,32,128]{2,1,0:T(8,128)(2,1)S(1)}, bf16[16,32,128]{2,1,0:T(8,128)(2,1)S(1)}, u32[]{:S(2)}, u32[]{:S(2)}) collective-permute-start(bf16[16,32,128]{2,1,0:T(8,128)(2,1)S(1)} %all_to_all.11.mine_ref), channel_id=1, source_target_pairs={{0,1},{1,0},{2,3},{3,2},{4,5},{5,4},{6,7},{7,6},{8,9},{9,8},{10,11... | collective-permute-start | bytes 393224 | tf_op jit(solution)/shard_map/ppermute | solution.py:543

commit v5 on v4

--- a/solution.py
+++ b/solution.py
@@ -249,7 +249,7 @@
     return [wins[pl.ds(at, 4 * GROUP), b * 2 * cols : (b + 1) * 2 * cols] for b in range(4)]
 
 
-def message_kernel(ga_ref, pa_ref, gb_ref, pb_ref, sa_ref, sb_ref, a_ref, b_ref):
+def message_kernel(sb_ref, sa_ref, ga_ref, pa_ref, gb_ref, pb_ref, a_ref, b_ref):
     deep, span = ga_ref.shape
     corners = jnp.concatenate([sa_ref[:, :span].astype(F32), sb_ref[:, :span].astype(F32)], axis=0).astype(BF)
     for out, g, p in ((a_ref, ga_ref, pa_ref), (b_ref, gb_ref, pb_ref)):
@@ -259,7 +259,7 @@
 
 
 def inner_kernel(
-    n_ew, g_ref, p_ref, ea_ref, eb_ref, pix_ref, cell_ref, grid_ref, wab_ref, w2_ref,
+    n_ew, eb_ref, ea_ref, g_ref, p_ref, pix_ref, cell_ref, grid_ref, wab_ref, w2_ref,
     delta_ref, second_ref, first_ref, turn_ref, edge_ref, pre_ref, ext, wide, wins, pres,
 ):
     frames = grid_ref.shape[0]
@@ -319,7 +319,7 @@
 
 
 def outer_kernel(
-    n_ew, n_ns, ra_ref, rb_ref, pix_ref, cell_ref,
+    n_ew, n_ns, rb_ref, ra_ref, pix_ref, cell_ref,
     delta_ref, second_ref, first_ref, turn_ref, edge_ref, pre_ref,
     grid_ref, pick_ref, hidden_ref, route_ref, wab_ref, w2_ref, tokens_ref, mask_ref,
     keep_ref, give_ref, ext, wide, wins, pres,
@@ -628,7 +628,7 @@
     send_a, send_b = call(
         message_kernel,
         (message_shape, message_shape),
-        (g_a, p_a, g_b, p_b, side_a, side_b),
+        (side_b, side_a, g_a, p_a, g_b, p_b),
         flops=1 << 20,
     )
     got_b = swap(send_b, "ns", 1)
@@ -644,7 +644,7 @@
             shape((frames, 2, 3 * GROUP, 8 * cols), BF),
             shape((frames, 2, chans, 2 * cols), F32),
         ),
-        (own_g, own_p, side_a, side_b, pixels, cells, grid, wab, w2),
+        (side_b, side_a, own_g, own_p, pixels, cells, grid, wab, w2),
         [
             pltpu.VMEM((frames * tall, pcol + 128), BF),
             pltpu.VMEM((rows * frames * chans, 2 * cols), BF),
@@ -660,7 +660,7 @@
         functools.partial(outer_kernel, n_ew, n_ns),
         (shape((half_rows, 2 * chans), F32), shape((half_rows, 2 * chans), BF)),
         (
-            got_a, got_b, pixels, cells, delta_mid, second_mid, first_mid, turn_mid, edge_wins, edge_pre,
+            got_b, got_a, pixels, cells, delta_mid, second_mid, first_mid, turn_mid, edge_wins, edge_pre,
             grid, picks, hidden, route, wab, w2, tile_tokens, mask_token,
         ),
         [

time: 50.5 us -> 49.7 us (0.984)
  blocking collectives: 29.5 us -> 26.4 us
  starting transfers between devices: 8.22 us -> 10.4 us
    all_to_all x2, blocking collectives: 29.5 us -> 26.4 us  [exchange(): lax.all_to_all(blocks, ('ew', 'ns'), 0, 0, axis_index_groups=groups, tile...]
    ppermute x6, starting transfers between devices: 8.22 us -> 10.4 us  [swap(): lax.ppermute(block, axis, [(i, j) for i, j in pairs if 0 <= j < count])]
  transfers between devices with their start and end apart: 6 -> 6, of which waited for: 2 -> 2; matrix products, arithmetic and copies ran while one was open for 0% -> 0% of each run, Pallas kernels for 9% -> 10%
where the time goes in v5:
time: 49.7 us; the launch traced here: 49.4 us
  blocking collectives  26.4 us (53%)
  starting transfers between devices  10.4 us (21%)
  Pallas kernels  8.24 us (17%)
  local copies, waits for them, and re-layouts  2.26 us (5%)
  waiting for transfers between devices  1.29 us (3%)
  between operations  0.78 us (2%)
    all_to_all x2, blocking collectives, exchange(): lax.all_to_all(blocks, ('ew', 'ns'), 0, 0, axis_index_groups=groups, tile...  26.4 us
    ppermute x6, starting transfers between devices, swap(): lax.ppermute(block, axis, [(i, j) for i, j in pairs if 0 <= j < count])  10.4 us
    pallas_call x10, Pallas kernels, call(): pl.pallas_call(kernel, out_shape=outs, in_specs=specs or [VMEM] * len(arg...  8.24 us
    unnamed x20, local copies, waits for them, and re-layouts  2.26 us
    ppermute x6, waiting for transfers between devices, swap(): lax.ppermute(block, axis, [(i, j) for i, j in pairs if 0 <= j < count])  1.29 us
  transfers between devices with their start and end apart: 6, of which 2 were waited for; matrix products, arithmetic and copies ran while one was open for 0% of the time, Pallas kernels for 10%

profile of v5, /device:TPU:0, one launch (start us, length us, event | category | flops | bytes accessed | tf_op | source)
XLA Modules:
  0.0 49.4 jit_solution(17593148232476395580)
XLA Ops:
  0.6 0.0 copy-start.8
  0.6 0.9 %copy-done.8 = bf16[2,64,8,128]{3,2,1,0:T(8,128)(2,1)S(1)} copy-done((bf16[2,64,8,128]{3,2,1,0:T(8,128)(2,1)S(1)}, bf16[2,64,8,128]{3,2,1,0:T(8,128)(2,1)}, u32[]{:S(2)}) %copy-start.8) | copy-done | bytes 262168
  1.6 0.0 copy-start.9
  1.6 0.3 shard_map.137
  1.9 0.6 %copy-done.9 = bf16[2,12,16,256]{3,2,1,0:T(8,128)(2,1)S(1)} copy-done((bf16[2,12,16,256]{3,2,1,0:T(8,128)(2,1)S(1)}, bf16[2,12,16,256]{3,2,1,0:T(8,128)(2,1)}, u32[]{:S(2)}) %copy-start.9) | copy-done | bytes 196632
  2.5 0.0 copy-start
  2.5 0.0 copy-start.1
  2.5 0.0 copy-start.2
  2.5 0.0 copy-start.3
  2.5 0.0 copy-start.6
  2.5 0.4 shard_map.138
  2.9 0.7 %collective-permute-start = (bf16[8,1024]{1,0:T(8,128)(2,1)S(1)}, bf16[8,1024]{1,0:T(8,128)(2,1)S(1)}, u32[]{:S(2)}, u32[]{:S(2)}) collective-permute-start(bf16[8,1024]{1,0:T(8,128)(2,1)S(1)} %get-tuple-element.36), channel_id=1, source_target_pairs={{8,16},{16,8},{9,17},{17,9},{10,18},{18,10},{11,19},{19,11},{12,20... | collective-permute-start | bytes 49160 | tf_op jit(solution)/shard_map/ppermute | solution.py:543
  3.6 5.7 %collective-permute-start.1 = (bf16[8,1024]{1,0:T(8,128)(2,1)S(1)}, bf16[8,1024]{1,0:T(8,128)(2,1)S(1)}, u32[]{:S(2)}, u32[]{:S(2)}) collective-permute-start(bf16[8,1024]{1,0:T(8,128)(2,1)S(1)} %get-tuple-element.36), channel_id=1, source_target_pairs={{0,8},{8,0},{16,24},{24,16},{1,9},{9,1},{17,25},{25,17},{2,10},{10... | collective-permute-start | bytes 49160 | tf_op jit(solution)/shard_map/ppermute | solution.py:543
  9.3 0.0 copy-start.4
  9.3 0.0 copy-start.5
  9.3 0.0 copy-start.7
  9.3 0.0 copy-done
  9.3 0.0 copy-done.1
  9.3 0.0 copy-done.2
  9.4 0.0 copy-done.3
  9.4 0.0 copy-done.6
  9.4 0.6 %copy-done.4 = bf16[768]{0:T(1024)(128)(2,1)S(1)} copy-done((bf16[768]{0:T(1024)(128)(2,1)S(1)}, bf16[768]{0:T(1024)(128)(2,1)}, u32[]{:S(2)}) %copy-start.4) | copy-done | bytes 1560
  10.0 0.0 copy-done.5
  10.0 0.0 copy-done.7
  10.0 1.7 %shard_map.139 = (bf16[48,512]{1,0:T(8,128)(2,1)S(1)}, bf16[64,256]{1,0:T(8,128)(2,1)S(1)}, bf16[48,512]{1,0:T(8,128)(2,1)S(1)}, bf16[64,256]{1,0:T(8,128)(2,1)S...) custom-call(s32[1,2]{1,0:T(1,128)S(1)} %bitcast.19, ...), custom_call_target="tpu_custom_call" | custom-call | flops 16777216 | bytes 1048576 | tf_op jit(solution)/shard_map/pallas_call | solution.py:547
  11.7 0.0 collective-permute-done.sb_ref.eb_ref
  11.7 0.0 collective-permute-done.1.sa_ref.ea_ref
  11.8 0.7 %collective-permute-start.2 = (bf16[64,768]{1,0:T(8,128)(2,1)S(1)}, bf16[64,768]{1,0:T(8,128)(2,1)S(1)}, u32[]{:S(2)}, u32[]{:S(2)}) collective-permute-start(bf16[64,768]{1,0:T(8,128)(2,1)S(1)} %get-tuple-element.43), channel_id=1, source_target_pairs={{1,2},{2,1},{3,4},{4,3},{5,6},{6,5},{9,10},{10,9},{11,12},{12,11},... | collective-permute-start | bytes 294920 | tf_op jit(solution)/shard_map/ppermute | solution.py:543
  12.4 3.0 %collective-permute-start.3 = (bf16[64,768]{1,0:T(8,128)(2,1)S(1)}, bf16[64,768]{1,0:T(8,128)(2,1)S(1)}, u32[]{:S(2)}, u32[]{:S(2)}) collective-permute-start(bf16[64,768]{1,0:T(8,128)(2,1)S(1)} %get-tuple-element.44), channel_id=1, source_target_pairs={{0,1},{1,0},{2,3},{3,2},{4,5},{5,4},{6,7},{7,6},{8,9},{9,8},{10,11... | collective-permute-start | bytes 294920 | tf_op jit(solution)/shard_map/ppermute | solution.py:543
  15.4 1.9 %shard_map.141 = (bf16[512,256]{1,0:T(8,128)(2,1)S(1)}, f32[128,128]{1,0:T(8,128)S(1)}, f32[512,128]{1,0:T(8,128)S(1)}, f32[2,128,256]{2,1,0:T(8,128)S(1)}, bf16...) custom-call(bf16[8,1024]{1,0:T(8,128)(2,1)S(1)} %collective-permute-done.sb_ref.eb_ref, ...), custom_call_target="tpu_custom_call" | custom-call | flops 134217728 | bytes 1048576 | tf_op jit(solution)/shard_map/pallas_call | solution.py:547
  17.3 0.0 collective-permute-done.2.rb_ref
  17.4 0.0 collective-permute-done.3.ra_ref
  17.4 1.8 %shard_map.142 = (f32[608,128]{1,0:T(8,128)S(1)}, bf16[608,128]{1,0:T(8,128)(2,1)S(1)}) custom-call(bf16[64,768]{1,0:T(8,128)(2,1)S(1)} %collective-permute-done.2.rb_ref, bf16[64,768]{1,0:T(8,128)(2,1)S(1)} %collective-permute-done.3.ra_ref, bf16[384,1024]{1,0:T(8,128)(2,1)S(1)} %get-tuple-element.45.pix_ref, ...), custom_call_target="tpu_custom_call" | custom-call | flops 134217728 | bytes 1048576 | tf_op jit(solution)/shard_map/pallas_call | solution.py:547
  19.2 0.4 collective-permute-start.4
  19.5 1.1 %collective-permute-done.4.got_ref = bf16[608,128]{1,0:T(8,128)(2,1)S(1)} collective-permute-done((bf16[608,128]{1,0:T(8,128)(2,1)S(1)}, bf16[608,128]{1,0:T(8,128)(2,1)S(1)}, u32[]{:S(2)}, u32[]{:S(2)}) %collective-permute-start.4) | collective-permute-done | bytes 155680 | tf_op jit(solution)/shard_map/ppermute | solution.py:543
  20.7 16.2 %all_to_all.10.arrived_ref.got_ref = bf16[16,56,128]{2,1,0:T(8,128)(2,1)S(1)} all-to-all(bf16[16,56,128]{2,1,0:T(8,128)(2,1)S(1)} %shard_map.143), channel_id=1, replica_groups={{0,2,4,6,8,10,12,14,16,18,20,22,24,26,28,30},{1,3,5,7,9,11,13,15,17,19,..., dimensions={0} | all-to-all | bytes 458752 | tf_op jit(solution)/shard_map/all_to_all | solution.py:677
  36.9 10.3 %all_to_all.11.mine_ref = bf16[16,32,128]{2,1,0:T(8,128)(2,1)S(1)} all-to-all(bf16[16,32,128]{2,1,0:T(8,128)(2,1)S(1)} %shard_map.145), channel_id=1, replica_groups={{0,2,4,6,8,10,12,14,16,18,20,22,24,26,28,30},{1,3,5,7,9,11,13,15,17,19,..., dimensions={0} | all-to-all | bytes 262144 | tf_op jit(solution)/shard_map/all_to_all | solution.py:677
  47.1 0.0 collective-permute-start.5
  47.1 1.1 %shard_map.144 = bf16[192,768]{1,0:T(8,128)(2,1)} custom-call(bf16[16,56,128]{2,1,0:T(8,128)(2,1)S(1)} %all_to_all.10.arrived_ref.got_ref, bf16[64,768]{1,0:T(8,128)(2,1)S(1)} %bitcast.12), custom_call_target="tpu_custom_call" | custom-call | flops 134217728 | bytes 1048576 | tf_op jit(solution)/shard_map/pallas_call | solution.py:547
  48.3 0.2 collective-permute-done.5.other_ref
  48.5 1.0 %shard_map.146 = (f32[64,768]{1,0:T(8,128)}, f32[4,4,64,64]{3,2,1,0:T(8,128)}, f32[4,12,4,64]{3,2,1,0:T(4,128)}, f32[768]{0:T(1024)}) custom-call(bf16[16,32,128]{2,1,0:T(8,128)(2,1)S(1)} %all_to_all.11.mine_ref, bf16[16,32,128]{2,1,0:T(8,128)(2,1)S(1)} %collective-permute-done.5.other_ref, bf16[64,768]{1,0:T(8,128)(2,1)S(1)} %bitcast.13), custom_call_target="tpu_custom_call" | custom-call | flops 1048576 | bytes 1048576 | tf_op jit(solution)/shard_map/pallas_call | solution.py:547
  (3 shorter events, 0.1 us)
Async XLA Ops:
  0.6 1.0 %copy-start.8 = (bf16[2,64,8,128]{3,2,1,0:T(8,128)(2,1)S(1)}, bf16[2,64,8,128]{3,2,1,0:T(8,128)(2,1)}, u32[]{:S(2)}) copy-start(bf16[2,64,8,128]{3,2,1,0:T(8,128)(2,1)} %pre_ref.1) | copy-start | bytes 786436
  1.6 0.9 %copy-start.9 = (bf16[2,12,16,256]{3,2,1,0:T(8,128)(2,1)S(1)}, bf16[2,12,16,256]{3,2,1,0:T(8,128)(2,1)}, u32[]{:S(2)}) copy-start(bf16[2,12,16,256]{3,2,1,0:T(8,128)(2,1)} %cot_ref.1) | copy-start | bytes 589828
  2.5 6.8 %copy-start = (bf16[768,64]{0,1:T(8,128)(2,1)S(1)}, bf16[768,64]{0,1:T(8,128)(2,1)}, u32[]{:S(2)}) copy-start(bf16[768,64]{0,1:T(8,128)(2,1)} %param.15) | copy-start | bytes 294916
  2.5 6.8 %copy-start.1 = (bf16[1,1,2,64,768]{4,3,2,1,0:T(8,128)(2,1)S(1)}, bf16[1,1,2,64,768]{4,3,2,1,0:T(8,128)(2,1)}, u32[]{:S(2)}) copy-start(bf16[1,1,2,64,768]{4,3,2,1,0:T(8,128)(2,1)} %param.10) | copy-start | bytes 589828
  2.5 6.8 %copy-start.2 = (bf16[4,4,64,64]{3,2,1,0:T(8,128)(2,1)S(1)}, bf16[4,4,64,64]{3,2,1,0:T(8,128)(2,1)}, u32[]{:S(2)}) copy-start(bf16[4,4,64,64]{3,2,1,0:T(8,128)(2,1)} %first_ref.1) | copy-start | bytes 393220
  2.5 6.8 %copy-start.3 = (bf16[4,4,12,64]{3,1,2,0:T(4,128)(2,1)S(1)}, bf16[4,4,12,64]{3,1,2,0:T(4,128)(2,1)}, u32[]{:S(2)}) copy-start(bf16[4,4,12,64]{3,1,2,0:T(4,128)(2,1)} %param.17) | copy-start | bytes 73732
  2.5 6.8 %copy-start.6 = (s32[1,1,2,64,1]{3,4,2,1,0:T(1,128)S(1)}, s32[1,1,2,64,1]{3,4,2,1,0:T(1,128)}, u32[]{:S(2)}) copy-start(s32[1,1,2,64,1]{3,4,2,1,0:T(1,128)} %param.13) | copy-start | bytes 1540
  2.9 8.8 %collective-permute-start = (bf16[8,1024]{1,0:T(8,128)(2,1)S(1)}, bf16[8,1024]{1,0:T(8,128)(2,1)S(1)}, u32[]{:S(2)}, u32[]{:S(2)}) collective-permute-start(bf16[8,1024]{1,0:T(8,128)(2,1)S(1)} %get-tuple-element.36), channel_id=1, source_target_pairs={{8,16},{16,8},{9,17},{17,9},{10,18},{18,10},{11,19},{19,11},{12,20... | collective-permute-start | bytes 49160 | tf_op jit(solution)/shard_map/ppermute | solution.py:543
  3.6 8.2 %collective-permute-start.1 = (bf16[8,1024]{1,0:T(8,128)(2,1)S(1)}, bf16[8,1024]{1,0:T(8,128)(2,1)S(1)}, u32[]{:S(2)}, u32[]{:S(2)}) collective-permute-start(bf16[8,1024]{1,0:T(8,128)(2,1)S(1)} %get-tuple-element.36), channel_id=1, source_target_pairs={{0,8},{8,0},{16,24},{24,16},{1,9},{9,1},{17,25},{25,17},{2,10},{10... | collective-permute-start | bytes 49160 | tf_op jit(solution)/shard_map/ppermute | solution.py:543
  9.3 0.7 %copy-start.4 = (bf16[768]{0:T(1024)(128)(2,1)S(1)}, bf16[768]{0:T(1024)(128)(2,1)}, u32[]{:S(2)}) copy-start(bf16[768]{0:T(1024)(128)(2,1)} %mask_ref.3) | copy-start | bytes 4612
  9.3 0.7 %copy-start.5 = (s32[1,1,2,64]{3,2,1,0:T(2,128)S(1)}, s32[1,1,2,64]{3,2,1,0:T(2,128)}, u32[]{:S(2)}) copy-start(s32[1,1,2,64]{3,2,1,0:T(2,128)} %param.11) | copy-start | bytes 1540
  9.3 0.7 %copy-start.7 = (s32[1,1,2]{2,1,0:T(1,128)S(1)}, s32[1,1,2]{2,1,0:T(1,128)}, u32[]{:S(2)}) copy-start(s32[1,1,2]{2,1,0:T(1,128)} %param.12) | copy-start | bytes 28
  11.8 5.6 %collective-permute-start.2 = (bf16[64,768]{1,0:T(8,128)(2,1)S(1)}, bf16[64,768]{1,0:T(8,128)(2,1)S(1)}, u32[]{:S(2)}, u32[]{:S(2)}) collective-permute-start(bf16[64,768]{1,0:T(8,128)(2,1)S(1)} %get-tuple-element.43), channel_id=1, source_target_pairs={{1,2},{2,1},{3,4},{4,3},{5,6},{6,5},{9,10},{10,9},{11,12},{12,11},... | collective-permute-start | bytes 294920 | tf_op jit(solution)/shard_map/ppermute | solution.py:543
  12.4 4.9 %collective-permute-start.3 = (bf16[64,768]{1,0:T(8,128)(2,1)S(1)}, bf16[64,768]{1,0:T(8,128)(2,1)S(1)}, u32[]{:S(2)}, u32[]{:S(2)}) collective-permute-start(bf16[64,768]{1,0:T(8,128)(2,1)S(1)} %get-tuple-element.44), channel_id=1, source_target_pairs={{0,1},{1,0},{2,3},{3,2},{4,5},{5,4},{6,7},{7,6},{8,9},{9,8},{10,11... | collective-permute-start | bytes 294920 | tf_op jit(solution)/shard_map/ppermute | solution.py:543
  19.2 1.4 %collective-permute-start.4 = (bf16[608,128]{1,0:T(8,128)(2,1)S(1)}, bf16[608,128]{1,0:T(8,128)(2,1)S(1)}, u32[]{:S(2)}, u32[]{:S(2)}) collective-permute-start(bf16[608,128]{1,0:T(8,128)(2,1)S(1)} %get-tuple-element.60), channel_id=1, source_target_pairs={{0,1},{1,0},{2,3},{3,2},{4,5},{5,4},{6,7},{7,6},{8,9},{9,8},{10,11... | collective-permute-start | bytes 466952 | tf_op jit(solution)/shard_map/ppermute | solution.py:543
  47.1 1.3 %collective-permute-start.5 = (bf16[16,32,128]{2,1,0:T(8,128)(2,1)S(1)}, bf16[16,32,128]{2,1,0:T(8,128)(2,1)S(1)}, u32[]{:S(2)}, u32[]{:S(2)}) collective-permute-start(bf16[16,32,128]{2,1,0:T(8,128)(2,1)S(1)} %all_to_all.11.mine_ref), channel_id=1, source_target_pairs={{0,1},{1,0},{2,3},{3,2},{4,5},{5,4},{6,7},{7,6},{8,9},{9,8},{10,11... | collective-permute-start | bytes 393224 | tf_op jit(solution)/shard_map/ppermute | solution.py:543

commit v6 on v5

--- a/solution.py
+++ b/solution.py
@@ -41,6 +41,14 @@
     own = 2 * jnp.where(right, lane - cols // 2, lane) + jnp.where(right, 1, 0)
     shifted = own + jnp.where(right, -2, 2)
     return jnp.where(lax.rem(lanes // cols, 2) == 0, own, shifted)
+
+
+def table_kernel(pix_ref, cell_ref, pick_ref):
+    cols = cell_ref.shape[0] // 2
+    column_tables(cols, pix_ref, cell_ref)
+    pick_g, pick_p = edge_tables(2 * cols, cols)
+    pick_ref[:, : 2 * cols] = pick_g
+    pick_ref[:, 2 * cols :] = pick_p
 
 
 def column_tables(cols, pix_ref, cell_ref):
@@ -77,19 +85,19 @@
     return pick_g.astype(F32).astype(BF), pick_p.astype(F32).astype(BF)
 
 
-def cell_layout_kernel(pre_ref, p_ref, edge_ref, pre_wide):
+def cell_layout_kernel(pick_ref, pre_ref, p_ref, edge_ref, pre_wide):
     frames, chans, rows, cols = pre_ref.shape
     spread(pre_ref, pre_wide, chans)
     for r in range(rows):
         for f in range(frames):
             p_ref[pl.ds((r * frames + f) * chans, chans), :] = gathered(pre_wide, 0, frames, chans, rows, f, r)
-    edges = nt(edge_tables(2 * cols, cols)[1], p_ref[...])[:8]
+    edges = nt(pick_ref[:, 2 * cols :], p_ref[...])[:8]
     line = frames * chans
     last = (rows - 1) * line
     edge_ref[...] = jnp.concatenate([edges[:, :line], edges[:, last:], edges[:, line:last]], axis=1)
 
 
-def pixel_layout_kernel(cot_ref, edge_ref, g_ref, own_ref, cot_wide):
+def pixel_layout_kernel(pick_ref, cot_ref, edge_ref, g_ref, own_ref, cot_wide):
     frames, bands, prow, pcol = cot_ref.shape
     spread(cot_ref, cot_wide, GROUP)
     for f in range(frames):
@@ -98,7 +106,7 @@
                 g_ref[pl.ds((f * prow + y) * GROUP, GROUP), h * 128 : (h + 1) * 128] = gathered(
                     cot_wide, h, frames, GROUP, prow, f, y
                 )
-    edges = nt(edge_tables(pcol, pcol // 2)[0], g_ref[...])[:8]
+    edges = nt(pick_ref[:, :pcol], g_ref[...])[:8]
     width = edges.shape[1]
     below = edge_ref[...]
     own_ref[...] = jnp.concatenate([edges + below[:, :width], below[:, width:]], axis=1).astype(BF)
@@ -133,10 +141,9 @@
 
 def local_kernel(
     capacity, counts_ref, g_ref, p_ref, vis_ref, owners_ref, tokens_ref, mask_ref, proj_ref, first_ref, second_ref,
-    ga_ref, pa_ref, gb_ref, pb_ref, grid_ref, pick_ref, hidden_ref, route_ref, wab_ref, w2_ref, pix_ref, cell_ref,
+    ga_ref, pa_ref, gb_ref, pb_ref, grid_ref, pick_ref, hidden_ref, route_ref, wab_ref, w2_ref,
 ):
     row_messages(g_ref, p_ref, ga_ref, pa_ref, gb_ref, pb_ref)
-    column_tables(p_ref.shape[1], pix_ref, cell_ref)
     slots_all = tokens_ref.shape[0]
     frames, slots, patches = pick_ref.shape
     chans = proj_ref.shape[0]
@@ -551,7 +558,7 @@
         out_specs=jax.tree.map(lambda _: VMEM, outs),
         scratch_shapes=list(scratch),
         compiler_params=pltpu.CompilerParams(vmem_limit_bytes=limit),
-        cost_estimate=pl.CostEstimate(flops=flops, bytes_accessed=1 << 20, transcendentals=0),
+        cost_estimate=pl.CostEstimate(flops=flops, bytes_accessed=1 << 10, transcendentals=0),
     )(*args)
 
 
@@ -572,19 +579,25 @@
     shape = jax.ShapeDtypeStruct
 
     tall = prow * GROUP
+    pixels, cells, edge_picks = call(
+        table_kernel,
+        (shape((pcol + 128, 4 * pcol), BF), shape((pcol, pcol), BF), shape((16, pcol + cols), BF)),
+        (),
+        flops=1 << 33,
+    )
     own_p, p_edges = call(
         cell_layout_kernel,
         (shape((frames * rows * chans, cols), BF), shape((8, frames * rows * chans), F32)),
-        (saved_pre,),
+        (edge_picks, saved_pre),
         [pltpu.VMEM((frames * chans * rows, cols), F32)],
-        flops=1 << 31,
+        flops=1 << 10,
     )
     own_g, own_edges = call(
         pixel_layout_kernel,
         (shape((frames * tall, pcol), BF), shape((8, frames * rows * chans), BF)),
-        (cotangent, p_edges),
+        (edge_picks, cotangent, p_edges),
         [pltpu.VMEM((frames * tall * pcol // 128, 128), F32)],
-        flops=1 << 31,
+        flops=1 << 33,
     )
     side_b = swap(own_edges, "ew", 1)
     side_a = swap(own_edges, "ew", 0)
@@ -593,7 +606,7 @@
     proj = proj_weight.T
     g_message = shape((3 * GROUP, frames * pcol), BF)
     p_message = shape((chans, frames * cols), BF)
-    g_a, p_a, g_b, p_b, grid, picks, hidden, route, wab, w2, pixels, cells = call(
+    g_a, p_a, g_b, p_b, grid, picks, hidden, route, wab, w2 = call(
         functools.partial(local_kernel, capacity),
         (
             g_message,
@@ -606,8 +619,6 @@
             shape((n_ns * slot_rows, slots_all), BF),
             shape((2 * chans, 8 * chans), BF),
             shape((chans, 16 * GROUP), BF),
-            shape((pcol + 128, 4 * pcol), BF),
-            shape((pcol, pcol), BF),
         ),
         (
             counts.reshape(1, frames),

time: 49.7 us -> 49 us (0.986)
  local copies, waits for them, and re-layouts: 2.26 us -> 1.44 us
    unnamed x20, local copies, waits for them, and re-layouts: 2.26 us -> 1.44 us
    pallas_call x10 -> x11, Pallas kernels: 8.24 us -> 8.11 us  [call(): pl.pallas_call(kernel, out_shape=outs, in_specs=specs or [VMEM] * len(arg...]
  transfers between devices with their start and end apart: 6 -> 6, of which waited for: 2 -> 2; matrix products, arithmetic and copies ran while one was open for 0% -> 0% of each run, Pallas kernels for 10% -> 9%
where the time goes in v6:
time: 49 us; the launch traced here: 48.7 us
  blocking collectives  26.6 us (54%)
  starting transfers between devices  10.4 us (21%)
  Pallas kernels  8.11 us (17%)
  local copies, waits for them, and re-layouts  1.44 us (3%)
  waiting for transfers between devices  1.29 us (3%)
  between operations  0.82 us (2%)
    all_to_all x2, blocking collectives, exchange(): lax.all_to_all(blocks, ('ew', 'ns'), 0, 0, axis_index_groups=groups, tile...  26.6 us
    ppermute x6, starting transfers between devices, swap(): lax.ppermute(block, axis, [(i, j) for i, j in pairs if 0 <= j < count])  10.4 us
    pallas_call x11, Pallas kernels, call(): pl.pallas_call(kernel, out_shape=outs, in_specs=specs or [VMEM] * len(arg...  8.11 us
    unnamed x20, local copies, waits for them, and re-layouts  1.44 us
    ppermute x6, waiting for transfers between devices, swap(): lax.ppermute(block, axis, [(i, j) for i, j in pairs if 0 <= j < count])  1.29 us
  transfers between devices with their start and end apart: 6, of which 2 were waited for; matrix products, arithmetic and copies ran while one was open for 0% of the time, Pallas kernels for 9%

profile of v6, /device:TPU:0, one launch (start us, length us, event | category | flops | bytes accessed | tf_op | source)
XLA Modules:
  0.0 48.7 jit_solution(6143700043876888989)
XLA Ops:
  0.6 0.0 copy-start.2
  0.6 0.2 shard_map.137
  0.8 0.0 copy-start.9
  0.8 0.7 %copy-done.2 = bf16[2,64,8,128]{3,2,1,0:T(8,128)(2,1)S(1)} copy-done((bf16[2,64,8,128]{3,2,1,0:T(8,128)(2,1)S(1)}, bf16[2,64,8,128]{3,2,1,0:T(8,128)(2,1)}, u32[]{:S(2)}) %copy-start.2) | copy-done | bytes 262168
  1.6 0.3 shard_map.138
  1.9 0.0 copy-done.9
  1.9 0.0 copy-start
  1.9 0.0 copy-start.1
  1.9 0.0 copy-start.3
  1.9 0.0 copy-start.4
  1.9 0.0 copy-start.7
  1.9 0.4 shard_map.139
  2.3 0.7 %collective-permute-start = (bf16[8,1024]{1,0:T(8,128)(2,1)S(1)}, bf16[8,1024]{1,0:T(8,128)(2,1)S(1)}, u32[]{:S(2)}, u32[]{:S(2)}) collective-permute-start(bf16[8,1024]{1,0:T(8,128)(2,1)S(1)} %get-tuple-element.38), channel_id=1, source_target_pairs={{8,16},{16,8},{9,17},{17,9},{10,18},{18,10},{11,19},{19,11},{12,20... | collective-permute-start | bytes 49160 | tf_op jit(solution)/shard_map/ppermute | solution.py:550
  3.0 5.7 %collective-permute-start.1 = (bf16[8,1024]{1,0:T(8,128)(2,1)S(1)}, bf16[8,1024]{1,0:T(8,128)(2,1)S(1)}, u32[]{:S(2)}, u32[]{:S(2)}) collective-permute-start(bf16[8,1024]{1,0:T(8,128)(2,1)S(1)} %get-tuple-element.38), channel_id=1, source_target_pairs={{0,8},{8,0},{16,24},{24,16},{1,9},{9,1},{17,25},{25,17},{2,10},{10... | collective-permute-start | bytes 49160 | tf_op jit(solution)/shard_map/ppermute | solution.py:550
  8.7 0.0 copy-start.5
  8.7 0.0 copy-start.6
  8.7 0.0 copy-start.8
  8.7 0.0 copy-done
  8.7 0.0 copy-done.1
  8.7 0.0 copy-done.3
  8.7 0.0 copy-done.4
  8.7 0.0 copy-done.7
  8.8 0.6 %copy-done.5 = bf16[768]{0:T(1024)(128)(2,1)S(1)} copy-done((bf16[768]{0:T(1024)(128)(2,1)S(1)}, bf16[768]{0:T(1024)(128)(2,1)}, u32[]{:S(2)}) %copy-start.5) | copy-done | bytes 1560
  9.4 0.0 copy-done.6
  9.4 0.0 copy-done.8
  9.4 1.4 %shard_map.140 = (bf16[48,512]{1,0:T(8,128)(2,1)S(1)}, bf16[64,256]{1,0:T(8,128)(2,1)S(1)}, bf16[48,512]{1,0:T(8,128)(2,1)S(1)}, bf16[64,256]{1,0:T(8,128)(2,1)S...) custom-call(s32[1,2]{1,0:T(1,128)S(1)} %bitcast.19, ...), custom_call_target="tpu_custom_call" | custom-call | flops 16777216 | bytes 1024 | tf_op jit(solution)/shard_map/pallas_call | solution.py:554
  10.8 0.0 collective-permute-done.sb_ref.eb_ref
  10.8 0.0 collective-permute-done.1.sa_ref.ea_ref
  10.9 0.7 %collective-permute-start.2 = (bf16[64,768]{1,0:T(8,128)(2,1)S(1)}, bf16[64,768]{1,0:T(8,128)(2,1)S(1)}, u32[]{:S(2)}, u32[]{:S(2)}) collective-permute-start(bf16[64,768]{1,0:T(8,128)(2,1)S(1)} %get-tuple-element.45), channel_id=1, source_target_pairs={{1,2},{2,1},{3,4},{4,3},{5,6},{6,5},{9,10},{10,9},{11,12},{12,11},... | collective-permute-start | bytes 294920 | tf_op jit(solution)/shard_map/ppermute | solution.py:550
  11.5 3.0 %collective-permute-start.3 = (bf16[64,768]{1,0:T(8,128)(2,1)S(1)}, bf16[64,768]{1,0:T(8,128)(2,1)S(1)}, u32[]{:S(2)}, u32[]{:S(2)}) collective-permute-start(bf16[64,768]{1,0:T(8,128)(2,1)S(1)} %get-tuple-element.46), channel_id=1, source_target_pairs={{0,1},{1,0},{2,3},{3,2},{4,5},{5,4},{6,7},{7,6},{8,9},{9,8},{10,11... | collective-permute-start | bytes 294920 | tf_op jit(solution)/shard_map/ppermute | solution.py:550
  14.5 1.9 %shard_map.142 = (bf16[512,256]{1,0:T(8,128)(2,1)S(1)}, f32[128,128]{1,0:T(8,128)S(1)}, f32[512,128]{1,0:T(8,128)S(1)}, f32[2,128,256]{2,1,0:T(8,128)S(1)}, bf16...) custom-call(bf16[8,1024]{1,0:T(8,128)(2,1)S(1)} %collective-permute-done.sb_ref.eb_ref, ...), custom_call_target="tpu_custom_call" | custom-call | flops 134217728 | bytes 1024 | tf_op jit(solution)/shard_map/pallas_call | solution.py:554
  16.4 0.0 collective-permute-done.2.rb_ref
  16.4 0.0 collective-permute-done.3.ra_ref
  16.4 1.8 %shard_map.143 = (f32[608,128]{1,0:T(8,128)S(1)}, bf16[608,128]{1,0:T(8,128)(2,1)S(1)}) custom-call(bf16[64,768]{1,0:T(8,128)(2,1)S(1)} %collective-permute-done.2.rb_ref, bf16[64,768]{1,0:T(8,128)(2,1)S(1)} %collective-permute-done.3.ra_ref, bf16[384,1024]{1,0:T(8,128)(2,1)S(1)} %get-tuple-element.47.pix_ref, ...), custom_call_target="tpu_custom_call" | custom-call | flops 134217728 | bytes 1024 | tf_op jit(solution)/shard_map/pallas_call | solution.py:554
  18.3 0.4 collective-permute-start.4
  18.6 1.1 %collective-permute-done.4.got_ref = bf16[608,128]{1,0:T(8,128)(2,1)S(1)} collective-permute-done((bf16[608,128]{1,0:T(8,128)(2,1)S(1)}, bf16[608,128]{1,0:T(8,128)(2,1)S(1)}, u32[]{:S(2)}, u32[]{:S(2)}) %collective-permute-start.4) | collective-permute-done | bytes 155680 | tf_op jit(solution)/shard_map/ppermute | solution.py:550
  19.7 16.3 %all_to_all.10.arrived_ref.got_ref = bf16[16,56,128]{2,1,0:T(8,128)(2,1)S(1)} all-to-all(bf16[16,56,128]{2,1,0:T(8,128)(2,1)S(1)} %shard_map.144), channel_id=1, replica_groups={{0,2,4,6,8,10,12,14,16,18,20,22,24,26,28,30},{1,3,5,7,9,11,13,15,17,19,..., dimensions={0} | all-to-all | bytes 458752 | tf_op jit(solution)/shard_map/all_to_all | solution.py:688
  36.1 10.3 %all_to_all.11.mine_ref = bf16[16,32,128]{2,1,0:T(8,128)(2,1)S(1)} all-to-all(bf16[16,32,128]{2,1,0:T(8,128)(2,1)S(1)} %shard_map.146), channel_id=1, replica_groups={{0,2,4,6,8,10,12,14,16,18,20,22,24,26,28,30},{1,3,5,7,9,11,13,15,17,19,..., dimensions={0} | all-to-all | bytes 262144 | tf_op jit(solution)/shard_map/all_to_all | solution.py:688
  46.4 0.0 collective-permute-start.5
  46.4 1.1 %shard_map.145 = bf16[192,768]{1,0:T(8,128)(2,1)} custom-call(bf16[16,56,128]{2,1,0:T(8,128)(2,1)S(1)} %all_to_all.10.arrived_ref.got_ref, bf16[64,768]{1,0:T(8,128)(2,1)S(1)} %bitcast.12), custom_call_target="tpu_custom_call" | custom-call | flops 134217728 | bytes 1024 | tf_op jit(solution)/shard_map/pallas_call | solution.py:554
  47.5 0.2 collective-permute-done.5.other_ref
  47.7 1.0 %shard_map.147 = (f32[64,768]{1,0:T(8,128)}, f32[4,4,64,64]{3,2,1,0:T(8,128)}, f32[4,12,4,64]{3,2,1,0:T(4,128)}, f32[768]{0:T(1024)}) custom-call(bf16[16,32,128]{2,1,0:T(8,128)(2,1)S(1)} %all_to_all.11.mine_ref, bf16[16,32,128]{2,1,0:T(8,128)(2,1)S(1)} %collective-permute-done.5.other_ref, bf16[64,768]{1,0:T(8,128)(2,1)S(1)} %bitcast.13), custom_call_target="tpu_custom_call" | custom-call | flops 1048576 | bytes 1024 | tf_op jit(solution)/shard_map/pallas_call | solution.py:554
  (3 shorter events, 0.1 us)
Async XLA Ops:
  0.6 1.0 %copy-start.2 = (bf16[2,64,8,128]{3,2,1,0:T(8,128)(2,1)S(1)}, bf16[2,64,8,128]{3,2,1,0:T(8,128)(2,1)}, u32[]{:S(2)}) copy-start(bf16[2,64,8,128]{3,2,1,0:T(8,128)(2,1)} %pre_ref.1) | copy-start | bytes 786436
  0.8 1.0 %copy-start.9 = (bf16[2,12,16,256]{3,2,1,0:T(8,128)(2,1)S(1)}, bf16[2,12,16,256]{3,2,1,0:T(8,128)(2,1)}, u32[]{:S(2)}) copy-start(bf16[2,12,16,256]{3,2,1,0:T(8,128)(2,1)} %cot_ref.1) | copy-start | bytes 589828
  1.9 6.9 %copy-start = (bf16[768,64]{0,1:T(8,128)(2,1)S(1)}, bf16[768,64]{0,1:T(8,128)(2,1)}, u32[]{:S(2)}) copy-start(bf16[768,64]{0,1:T(8,128)(2,1)} %param.15) | copy-start | bytes 294916
  1.9 6.9 %copy-start.1 = (bf16[1,1,2,64,768]{4,3,2,1,0:T(8,128)(2,1)S(1)}, bf16[1,1,2,64,768]{4,3,2,1,0:T(8,128)(2,1)}, u32[]{:S(2)}) copy-start(bf16[1,1,2,64,768]{4,3,2,1,0:T(8,128)(2,1)} %param.10) | copy-start | bytes 589828
  1.9 6.8 %copy-start.3 = (bf16[4,4,64,64]{3,2,1,0:T(8,128)(2,1)S(1)}, bf16[4,4,64,64]{3,2,1,0:T(8,128)(2,1)}, u32[]{:S(2)}) copy-start(bf16[4,4,64,64]{3,2,1,0:T(8,128)(2,1)} %first_ref.1) | copy-start | bytes 393220
  1.9 6.8 %copy-start.4 = (bf16[4,4,12,64]{3,1,2,0:T(4,128)(2,1)S(1)}, bf16[4,4,12,64]{3,1,2,0:T(4,128)(2,1)}, u32[]{:S(2)}) copy-start(bf16[4,4,12,64]{3,1,2,0:T(4,128)(2,1)} %param.17) | copy-start | bytes 73732
  1.9 6.8 %copy-start.7 = (s32[1,1,2,64,1]{3,4,2,1,0:T(1,128)S(1)}, s32[1,1,2,64,1]{3,4,2,1,0:T(1,128)}, u32[]{:S(2)}) copy-start(s32[1,1,2,64,1]{3,4,2,1,0:T(1,128)} %param.13) | copy-start | bytes 1540
  2.3 8.5 %collective-permute-start = (bf16[8,1024]{1,0:T(8,128)(2,1)S(1)}, bf16[8,1024]{1,0:T(8,128)(2,1)S(1)}, u32[]{:S(2)}, u32[]{:S(2)}) collective-permute-start(bf16[8,1024]{1,0:T(8,128)(2,1)S(1)} %get-tuple-element.38), channel_id=1, source_target_pairs={{8,16},{16,8},{9,17},{17,9},{10,18},{18,10},{11,19},{19,11},{12,20... | collective-permute-start | bytes 49160 | tf_op jit(solution)/shard_map/ppermute | solution.py:550
  3.0 7.9 %collective-permute-start.1 = (bf16[8,1024]{1,0:T(8,128)(2,1)S(1)}, bf16[8,1024]{1,0:T(8,128)(2,1)S(1)}, u32[]{:S(2)}, u32[]{:S(2)}) collective-permute-start(bf16[8,1024]{1,0:T(8,128)(2,1)S(1)} %get-tuple-element.38), channel_id=1, source_target_pairs={{0,8},{8,0},{16,24},{24,16},{1,9},{9,1},{17,25},{25,17},{2,10},{10... | collective-permute-start | bytes 49160 | tf_op jit(solution)/shard_map/ppermute | solution.py:550
  8.7 0.7 %copy-start.5 = (bf16[768]{0:T(1024)(128)(2,1)S(1)}, bf16[768]{0:T(1024)(128)(2,1)}, u32[]{:S(2)}) copy-start(bf16[768]{0:T(1024)(128)(2,1)} %mask_ref.3) | copy-start | bytes 4612
  8.7 0.7 %copy-start.6 = (s32[1,1,2,64]{3,2,1,0:T(2,128)S(1)}, s32[1,1,2,64]{3,2,1,0:T(2,128)}, u32[]{:S(2)}) copy-start(s32[1,1,2,64]{3,2,1,0:T(2,128)} %param.11) | copy-start | bytes 1540
  8.7 0.7 %copy-start.8 = (s32[1,1,2]{2,1,0:T(1,128)S(1)}, s32[1,1,2]{2,1,0:T(1,128)}, u32[]{:S(2)}) copy-start(s32[1,1,2]{2,1,0:T(1,128)} %param.12) | copy-start | bytes 28
  10.9 5.6 %collective-permute-start.2 = (bf16[64,768]{1,0:T(8,128)(2,1)S(1)}, bf16[64,768]{1,0:T(8,128)(2,1)S(1)}, u32[]{:S(2)}, u32[]{:S(2)}) collective-permute-start(bf16[64,768]{1,0:T(8,128)(2,1)S(1)} %get-tuple-element.45), channel_id=1, source_target_pairs={{1,2},{2,1},{3,4},{4,3},{5,6},{6,5},{9,10},{10,9},{11,12},{12,11},... | collective-permute-start | bytes 294920 | tf_op jit(solution)/shard_map/ppermute | solution.py:550
  11.5 4.9 %collective-permute-start.3 = (bf16[64,768]{1,0:T(8,128)(2,1)S(1)}, bf16[64,768]{1,0:T(8,128)(2,1)S(1)}, u32[]{:S(2)}, u32[]{:S(2)}) collective-permute-start(bf16[64,768]{1,0:T(8,128)(2,1)S(1)} %get-tuple-element.46), channel_id=1, source_target_pairs={{0,1},{1,0},{2,3},{3,2},{4,5},{5,4},{6,7},{7,6},{8,9},{9,8},{10,11... | collective-permute-start | bytes 294920 | tf_op jit(solution)/shard_map/ppermute | solution.py:550
  18.3 1.4 %collective-permute-start.4 = (bf16[608,128]{1,0:T(8,128)(2,1)S(1)}, bf16[608,128]{1,0:T(8,128)(2,1)S(1)}, u32[]{:S(2)}, u32[]{:S(2)}) collective-permute-start(bf16[608,128]{1,0:T(8,128)(2,1)S(1)} %get-tuple-element.62), channel_id=1, source_target_pairs={{0,1},{1,0},{2,3},{3,2},{4,5},{5,4},{6,7},{7,6},{8,9},{9,8},{10,11... | collective-permute-start | bytes 466952 | tf_op jit(solution)/shard_map/ppermute | solution.py:550
  46.4 1.3 %collective-permute-start.5 = (bf16[16,32,128]{2,1,0:T(8,128)(2,1)S(1)}, bf16[16,32,128]{2,1,0:T(8,128)(2,1)S(1)}, u32[]{:S(2)}, u32[]{:S(2)}) collective-permute-start(bf16[16,32,128]{2,1,0:T(8,128)(2,1)S(1)} %all_to_all.11.mine_ref), channel_id=1, source_target_pairs={{0,1},{1,0},{2,3},{3,2},{4,5},{5,4},{6,7},{7,6},{8,9},{9,8},{10,11... | collective-permute-start | bytes 393224 | tf_op jit(solution)/shard_map/ppermute | solution.py:550

commit v7 on v6

--- a/solution.py
+++ b/solution.py
@@ -11,7 +11,6 @@
 BF = jnp.bfloat16
 F32 = jnp.float32
 VMEM = pl.BlockSpec(memory_space=pltpu.VMEM)
-SMEM = pl.BlockSpec(memory_space=pltpu.SMEM)
 GROUP = 16
 GRAD_ROWS = 1024
 PROJ_AT = 512
@@ -85,20 +84,13 @@
     return pick_g.astype(F32).astype(BF), pick_p.astype(F32).astype(BF)
 
 
-def cell_layout_kernel(pick_ref, pre_ref, p_ref, edge_ref, pre_wide):
+def layout_kernel(pick_ref, pre_ref, cot_ref, p_ref, g_ref, own_ref, pre_wide, cot_wide):
     frames, chans, rows, cols = pre_ref.shape
+    prow, pcol = cot_ref.shape[2:]
     spread(pre_ref, pre_wide, chans)
     for r in range(rows):
         for f in range(frames):
             p_ref[pl.ds((r * frames + f) * chans, chans), :] = gathered(pre_wide, 0, frames, chans, rows, f, r)
-    edges = nt(pick_ref[:, 2 * cols :], p_ref[...])[:8]
-    line = frames * chans
-    last = (rows - 1) * line
-    edge_ref[...] = jnp.concatenate([edges[:, :line], edges[:, last:], edges[:, line:last]], axis=1)
-
-
-def pixel_layout_kernel(pick_ref, cot_ref, edge_ref, g_ref, own_ref, cot_wide):
-    frames, bands, prow, pcol = cot_ref.shape
     spread(cot_ref, cot_wide, GROUP)
     for f in range(frames):
         for y in range(prow):
@@ -106,9 +98,12 @@
                 g_ref[pl.ds((f * prow + y) * GROUP, GROUP), h * 128 : (h + 1) * 128] = gathered(
                     cot_wide, h, frames, GROUP, prow, f, y
                 )
+    below = nt(pick_ref[:, pcol:], p_ref[...])[:8]
+    line = frames * chans
+    last = (rows - 1) * line
+    below = jnp.concatenate([below[:, :line], below[:, last:], below[:, line:last]], axis=1)
     edges = nt(pick_ref[:, :pcol], g_ref[...])[:8]
     width = edges.shape[1]
-    below = edge_ref[...]
     own_ref[...] = jnp.concatenate([edges + below[:, :width], below[:, width:]], axis=1).astype(BF)
 
 
@@ -172,7 +167,7 @@
     slot = iota((1, slots_all), 1)
     live = jnp.zeros((1, slots_all), jnp.int32)
     for f in range(frames):
-        inside = (slot >= f * slots) & (slot < f * slots + counts_ref[0, f])
+        inside = (slot >= f * slots) & (slot < f * slots + counts_ref[:, f : f + 1])
         live = jnp.where(inside, 1, live)
     wanted = jnp.where(live > 0, vis, patches)
     square = (slots_all, slots_all)
@@ -585,18 +580,18 @@
         (),
         flops=1 << 33,
     )
-    own_p, p_edges = call(
-        cell_layout_kernel,
-        (shape((frames * rows * chans, cols), BF), shape((8, frames * rows * chans), F32)),
-        (edge_picks, saved_pre),
-        [pltpu.VMEM((frames * chans * rows, cols), F32)],
-        flops=1 << 10,
-    )
-    own_g, own_edges = call(
-        pixel_layout_kernel,
-        (shape((frames * tall, pcol), BF), shape((8, frames * rows * chans), BF)),
-        (edge_picks, cotangent, p_edges),
-        [pltpu.VMEM((frames * tall * pcol // 128, 128), F32)],
+    own_p, own_g, own_edges = call(
+        layout_kernel,
+        (
+            shape((frames * rows * chans, cols), BF),
+            shape((frames * tall, pcol), BF),
+            shape((8, frames * rows * chans), BF),
+        ),
+        (edge_picks, saved_pre, cotangent),
+        [
+            pltpu.VMEM((frames * chans * rows, cols), F32),
+            pltpu.VMEM((frames * tall * pcol // 128, 128), F32),
+        ],
         flops=1 << 33,
     )
     side_b = swap(own_edges, "ew", 1)
@@ -633,7 +628,6 @@
             up_second.transpose(0, 2, 1, 3),
         ),
         flops=1 << 24,
-        specs=[SMEM] + [VMEM] * 9,
     )
     message_shape = shape((3 * GROUP + 16, frames * (pcol + cols)), BF)
     send_a, send_b = call(

time: 49 us -> 48.9 us (level)
  Pallas kernels: 8.11 us -> 7.43 us
    pallas_call x11 -> x10, Pallas kernels: 8.11 us -> 7.43 us  [call(): pl.pallas_call(kernel, out_shape=outs, in_specs=specs or [VMEM] * len(arg...]
  transfers between devices with their start and end apart: 6 -> 6, of which waited for: 2 -> 3; matrix products, arithmetic and copies ran while one was open for 0% -> 0% of each run, Pallas kernels for 9% -> 8%
where the time goes in v7:
time: 48.9 us; the launch traced here: 48.6 us
  blocking collectives  26.9 us (55%)
  starting transfers between devices  10.4 us (21%)
  Pallas kernels  7.43 us (15%)
  waiting for transfers between devices  1.53 us (3%)
  local copies, waits for them, and re-layouts  1.48 us (3%)
  between operations  0.78 us (2%)
    all_to_all x2, blocking collectives, exchange(): lax.all_to_all(blocks, ('ew', 'ns'), 0, 0, axis_index_groups=groups, tile...  26.9 us
    ppermute x6, starting transfers between devices, swap(): lax.ppermute(block, axis, [(i, j) for i, j in pairs if 0 <= j < count])  10.4 us
    pallas_call x10, Pallas kernels, call(): pl.pallas_call(kernel, out_shape=outs, in_specs=specs or [VMEM] * len(arg...  7.43 us
    ppermute x6, waiting for transfers between devices, swap(): lax.ppermute(block, axis, [(i, j) for i, j in pairs if 0 <= j < count])  1.53 us
    unnamed x20, local copies, waits for them, and re-layouts  1.48 us
  transfers between devices with their start and end apart: 6, of which 3 were waited for; matrix products, arithmetic and copies ran while one was open for 0% of the time, Pallas kernels for 8%

profile of v7, /device:TPU:0, one launch (start us, length us, event | category | flops | bytes accessed | tf_op | source)
XLA Modules:
  0.0 48.6 jit_solution(10069574172448052358)
XLA Ops:
  0.6 0.0 copy-start.8
  0.6 0.0 copy-start.9
  0.7 0.2 shard_map.137
  0.8 0.7 %copy-done.8 = bf16[2,64,8,128]{3,2,1,0:T(8,128)(2,1)S(1)} copy-done((bf16[2,64,8,128]{3,2,1,0:T(8,128)(2,1)S(1)}, bf16[2,64,8,128]{3,2,1,0:T(8,128)(2,1)}, u32[]{:S(2)}) %copy-start.8) | copy-done | bytes 262168
  1.6 0.1 copy-done.9
  1.6 0.0 copy-start
  1.6 0.0 copy-start.1
  1.6 0.0 copy-start.2
  1.6 0.0 copy-start.3
  1.6 0.0 copy-start.6
  1.7 0.5 %shard_map.138 = (bf16[1024,128]{1,0:T(8,128)(2,1)S(1)}, bf16[512,256]{1,0:T(8,128)(2,1)S(1)}, bf16[8,1024]{1,0:T(8,128)(2,1)S(1)}) custom-call(bf16[16,384]{1,0:T(8,128)(2,1)S(1)} %get-tuple-element.35.pick_ref, bf16[2,64,8,128]{3,2,1,0:T(8,128)(2,1)S(1)} %copy-done.8, bf16[2,12,16,256]{3,2,1,0:T(8,128)(2,1)S(1)} %copy-done.9), custom_call_target="tpu_custom_call" | custom-call | flops 8589934592 | bytes 1024 | tf_op jit(solution)/shard_map/pallas_call | solution.py:549
  2.2 0.7 %collective-permute-start = (bf16[8,1024]{1,0:T(8,128)(2,1)S(1)}, bf16[8,1024]{1,0:T(8,128)(2,1)S(1)}, u32[]{:S(2)}, u32[]{:S(2)}) collective-permute-start(bf16[8,1024]{1,0:T(8,128)(2,1)S(1)} %get-tuple-element.36), channel_id=1, source_target_pairs={{8,16},{16,8},{9,17},{17,9},{10,18},{18,10},{11,19},{19,11},{12,20... | collective-permute-start | bytes 49160 | tf_op jit(solution)/shard_map/ppermute | solution.py:545
  2.9 5.7 %collective-permute-start.1 = (bf16[8,1024]{1,0:T(8,128)(2,1)S(1)}, bf16[8,1024]{1,0:T(8,128)(2,1)S(1)}, u32[]{:S(2)}, u32[]{:S(2)}) collective-permute-start(bf16[8,1024]{1,0:T(8,128)(2,1)S(1)} %get-tuple-element.36), channel_id=1, source_target_pairs={{0,8},{8,0},{16,24},{24,16},{1,9},{9,1},{17,25},{25,17},{2,10},{10... | collective-permute-start | bytes 49160 | tf_op jit(solution)/shard_map/ppermute | solution.py:545
  8.6 0.0 copy-start.4
  8.6 0.0 copy-start.5
  8.6 0.0 copy-start.7
  8.6 0.0 copy-done
  8.6 0.0 copy-done.1
  8.6 0.0 copy-done.2
  8.6 0.0 copy-done.3
  8.6 0.0 copy-done.6
  8.7 0.6 %copy-done.4 = bf16[768]{0:T(1024)(128)(2,1)S(1)} copy-done((bf16[768]{0:T(1024)(128)(2,1)S(1)}, bf16[768]{0:T(1024)(128)(2,1)}, u32[]{:S(2)}) %copy-start.4) | copy-done | bytes 1560
  9.3 0.0 copy-done.5
  9.3 0.0 copy-done.7
  9.3 0.8 %shard_map.139 = (bf16[48,512]{1,0:T(8,128)(2,1)S(1)}, bf16[64,256]{1,0:T(8,128)(2,1)S(1)}, bf16[48,512]{1,0:T(8,128)(2,1)S(1)}, bf16[64,256]{1,0:T(8,128)(2,1)S...) custom-call(s32[1,2]{1,0:T(1,128)S(1)} %bitcast.19, ...), custom_call_target="tpu_custom_call" | custom-call | flops 16777216 | bytes 1024 | tf_op jit(solution)/shard_map/pallas_call | solution.py:549
  10.2 0.0 collective-permute-done.sb_ref.eb_ref
  10.2 0.2 collective-permute-done.1.sa_ref.ea_ref
  10.4 0.7 %collective-permute-start.2 = (bf16[64,768]{1,0:T(8,128)(2,1)S(1)}, bf16[64,768]{1,0:T(8,128)(2,1)S(1)}, u32[]{:S(2)}, u32[]{:S(2)}) collective-permute-start(bf16[64,768]{1,0:T(8,128)(2,1)S(1)} %get-tuple-element.43), channel_id=1, source_target_pairs={{1,2},{2,1},{3,4},{4,3},{5,6},{6,5},{9,10},{10,9},{11,12},{12,11},... | collective-permute-start | bytes 294920 | tf_op jit(solution)/shard_map/ppermute | solution.py:545
  11.1 3.0 %collective-permute-start.3 = (bf16[64,768]{1,0:T(8,128)(2,1)S(1)}, bf16[64,768]{1,0:T(8,128)(2,1)S(1)}, u32[]{:S(2)}, u32[]{:S(2)}) collective-permute-start(bf16[64,768]{1,0:T(8,128)(2,1)S(1)} %get-tuple-element.44), channel_id=1, source_target_pairs={{0,1},{1,0},{2,3},{3,2},{4,5},{5,4},{6,7},{7,6},{8,9},{9,8},{10,11... | collective-permute-start | bytes 294920 | tf_op jit(solution)/shard_map/ppermute | solution.py:545
  14.1 1.9 %shard_map.141 = (bf16[512,256]{1,0:T(8,128)(2,1)S(1)}, f32[128,128]{1,0:T(8,128)S(1)}, f32[512,128]{1,0:T(8,128)S(1)}, f32[2,128,256]{2,1,0:T(8,128)S(1)}, bf16...) custom-call(bf16[8,1024]{1,0:T(8,128)(2,1)S(1)} %collective-permute-done.sb_ref.eb_ref, ...), custom_call_target="tpu_custom_call" | custom-call | flops 134217728 | bytes 1024 | tf_op jit(solution)/shard_map/pallas_call | solution.py:549
  16.0 0.0 collective-permute-done.2.rb_ref
  16.0 0.0 collective-permute-done.3.ra_ref
  16.0 1.8 %shard_map.142 = (f32[608,128]{1,0:T(8,128)S(1)}, bf16[608,128]{1,0:T(8,128)(2,1)S(1)}) custom-call(bf16[64,768]{1,0:T(8,128)(2,1)S(1)} %collective-permute-done.2.rb_ref, bf16[64,768]{1,0:T(8,128)(2,1)S(1)} %collective-permute-done.3.ra_ref, bf16[384,1024]{1,0:T(8,128)(2,1)S(1)} %get-tuple-element.45.pix_ref, ...), custom_call_target="tpu_custom_call" | custom-call | flops 134217728 | bytes 1024 | tf_op jit(solution)/shard_map/pallas_call | solution.py:549
  17.8 0.4 collective-permute-start.4
  18.2 1.1 %collective-permute-done.4.got_ref = bf16[608,128]{1,0:T(8,128)(2,1)S(1)} collective-permute-done((bf16[608,128]{1,0:T(8,128)(2,1)S(1)}, bf16[608,128]{1,0:T(8,128)(2,1)S(1)}, u32[]{:S(2)}, u32[]{:S(2)}) %collective-permute-start.4) | collective-permute-done | bytes 155680 | tf_op jit(solution)/shard_map/ppermute | solution.py:545
  19.3 16.7 %all_to_all.10.arrived_ref.got_ref = bf16[16,56,128]{2,1,0:T(8,128)(2,1)S(1)} all-to-all(bf16[16,56,128]{2,1,0:T(8,128)(2,1)S(1)} %shard_map.143), channel_id=1, replica_groups={{0,2,4,6,8,10,12,14,16,18,20,22,24,26,28,30},{1,3,5,7,9,11,13,15,17,19,..., dimensions={0} | all-to-all | bytes 458752 | tf_op jit(solution)/shard_map/all_to_all | solution.py:682
  36.0 10.3 %all_to_all.11.mine_ref = bf16[16,32,128]{2,1,0:T(8,128)(2,1)S(1)} all-to-all(bf16[16,32,128]{2,1,0:T(8,128)(2,1)S(1)} %shard_map.145), channel_id=1, replica_groups={{0,2,4,6,8,10,12,14,16,18,20,22,24,26,28,30},{1,3,5,7,9,11,13,15,17,19,..., dimensions={0} | all-to-all | bytes 262144 | tf_op jit(solution)/shard_map/all_to_all | solution.py:682
  46.3 0.0 collective-permute-start.5
  46.3 1.1 %shard_map.144 = bf16[192,768]{1,0:T(8,128)(2,1)} custom-call(bf16[16,56,128]{2,1,0:T(8,128)(2,1)S(1)} %all_to_all.10.arrived_ref.got_ref, bf16[64,768]{1,0:T(8,128)(2,1)S(1)} %bitcast.12), custom_call_target="tpu_custom_call" | custom-call | flops 134217728 | bytes 1024 | tf_op jit(solution)/shard_map/pallas_call | solution.py:549
  47.4 0.2 collective-permute-done.5.other_ref
  47.6 1.0 %shard_map.146 = (f32[64,768]{1,0:T(8,128)}, f32[4,4,64,64]{3,2,1,0:T(8,128)}, f32[4,12,4,64]{3,2,1,0:T(4,128)}, f32[768]{0:T(1024)}) custom-call(bf16[16,32,128]{2,1,0:T(8,128)(2,1)S(1)} %all_to_all.11.mine_ref, bf16[16,32,128]{2,1,0:T(8,128)(2,1)S(1)} %collective-permute-done.5.other_ref, bf16[64,768]{1,0:T(8,128)(2,1)S(1)} %bitcast.13), custom_call_target="tpu_custom_call" | custom-call | flops 1048576 | bytes 1024 | tf_op jit(solution)/shard_map/pallas_call | solution.py:549
  (3 shorter events, 0.1 us)
Async XLA Ops:
  0.6 1.0 %copy-start.8 = (bf16[2,64,8,128]{3,2,1,0:T(8,128)(2,1)S(1)}, bf16[2,64,8,128]{3,2,1,0:T(8,128)(2,1)}, u32[]{:S(2)}) copy-start(bf16[2,64,8,128]{3,2,1,0:T(8,128)(2,1)} %pre_ref.1) | copy-start | bytes 786436
  0.6 1.0 %copy-start.9 = (bf16[2,12,16,256]{3,2,1,0:T(8,128)(2,1)S(1)}, bf16[2,12,16,256]{3,2,1,0:T(8,128)(2,1)}, u32[]{:S(2)}) copy-start(bf16[2,12,16,256]{3,2,1,0:T(8,128)(2,1)} %cot_ref.1) | copy-start | bytes 589828
  1.6 7.0 %copy-start = (bf16[768,64]{0,1:T(8,128)(2,1)S(1)}, bf16[768,64]{0,1:T(8,128)(2,1)}, u32[]{:S(2)}) copy-start(bf16[768,64]{0,1:T(8,128)(2,1)} %param.15) | copy-start | bytes 294916
  1.6 7.0 %copy-start.1 = (bf16[1,1,2,64,768]{4,3,2,1,0:T(8,128)(2,1)S(1)}, bf16[1,1,2,64,768]{4,3,2,1,0:T(8,128)(2,1)}, u32[]{:S(2)}) copy-start(bf16[1,1,2,64,768]{4,3,2,1,0:T(8,128)(2,1)} %param.10) | copy-start | bytes 589828
  1.6 7.0 %copy-start.2 = (bf16[4,4,64,64]{3,2,1,0:T(8,128)(2,1)S(1)}, bf16[4,4,64,64]{3,2,1,0:T(8,128)(2,1)}, u32[]{:S(2)}) copy-start(bf16[4,4,64,64]{3,2,1,0:T(8,128)(2,1)} %first_ref.1) | copy-start | bytes 393220
  1.6 7.0 %copy-start.3 = (bf16[4,4,12,64]{3,1,2,0:T(4,128)(2,1)S(1)}, bf16[4,4,12,64]{3,1,2,0:T(4,128)(2,1)}, u32[]{:S(2)}) copy-start(bf16[4,4,12,64]{3,1,2,0:T(4,128)(2,1)} %param.17) | copy-start | bytes 73732
  1.6 7.0 %copy-start.6 = (s32[1,1,2,64,1]{3,4,2,1,0:T(1,128)S(1)}, s32[1,1,2,64,1]{3,4,2,1,0:T(1,128)}, u32[]{:S(2)}) copy-start(s32[1,1,2,64,1]{3,4,2,1,0:T(1,128)} %param.13) | copy-start | bytes 1540
  2.2 8.0 %collective-permute-start = (bf16[8,1024]{1,0:T(8,128)(2,1)S(1)}, bf16[8,1024]{1,0:T(8,128)(2,1)S(1)}, u32[]{:S(2)}, u32[]{:S(2)}) collective-permute-start(bf16[8,1024]{1,0:T(8,128)(2,1)S(1)} %get-tuple-element.36), channel_id=1, source_target_pairs={{8,16},{16,8},{9,17},{17,9},{10,18},{18,10},{11,19},{19,11},{12,20... | collective-permute-start | bytes 49160 | tf_op jit(solution)/shard_map/ppermute | solution.py:545
  2.9 7.5 %collective-permute-start.1 = (bf16[8,1024]{1,0:T(8,128)(2,1)S(1)}, bf16[8,1024]{1,0:T(8,128)(2,1)S(1)}, u32[]{:S(2)}, u32[]{:S(2)}) collective-permute-start(bf16[8,1024]{1,0:T(8,128)(2,1)S(1)} %get-tuple-element.36), channel_id=1, source_target_pairs={{0,8},{8,0},{16,24},{24,16},{1,9},{9,1},{17,25},{25,17},{2,10},{10... | collective-permute-start | bytes 49160 | tf_op jit(solution)/shard_map/ppermute | solution.py:545
  8.6 0.7 %copy-start.4 = (bf16[768]{0:T(1024)(128)(2,1)S(1)}, bf16[768]{0:T(1024)(128)(2,1)}, u32[]{:S(2)}) copy-start(bf16[768]{0:T(1024)(128)(2,1)} %mask_ref.3) | copy-start | bytes 4612
  8.6 0.7 %copy-start.5 = (s32[1,1,2,64]{3,2,1,0:T(2,128)S(1)}, s32[1,1,2,64]{3,2,1,0:T(2,128)}, u32[]{:S(2)}) copy-start(s32[1,1,2,64]{3,2,1,0:T(2,128)} %param.11) | copy-start | bytes 1540
  8.6 0.7 %copy-start.7 = (s32[1,1,2]{2,1,0:T(1,128)S(1)}, s32[1,1,2]{2,1,0:T(1,128)}, u32[]{:S(2)}) copy-start(s32[1,1,2]{2,1,0:T(1,128)} %param.12) | copy-start | bytes 28
  10.4 5.6 %collective-permute-start.2 = (bf16[64,768]{1,0:T(8,128)(2,1)S(1)}, bf16[64,768]{1,0:T(8,128)(2,1)S(1)}, u32[]{:S(2)}, u32[]{:S(2)}) collective-permute-start(bf16[64,768]{1,0:T(8,128)(2,1)S(1)} %get-tuple-element.43), channel_id=1, source_target_pairs={{1,2},{2,1},{3,4},{4,3},{5,6},{6,5},{9,10},{10,9},{11,12},{12,11},... | collective-permute-start | bytes 294920 | tf_op jit(solution)/shard_map/ppermute | solution.py:545
  11.1 4.9 %collective-permute-start.3 = (bf16[64,768]{1,0:T(8,128)(2,1)S(1)}, bf16[64,768]{1,0:T(8,128)(2,1)S(1)}, u32[]{:S(2)}, u32[]{:S(2)}) collective-permute-start(bf16[64,768]{1,0:T(8,128)(2,1)S(1)} %get-tuple-element.44), channel_id=1, source_target_pairs={{0,1},{1,0},{2,3},{3,2},{4,5},{5,4},{6,7},{7,6},{8,9},{9,8},{10,11... | collective-permute-start | bytes 294920 | tf_op jit(solution)/shard_map/ppermute | solution.py:545
  17.8 1.4 %collective-permute-start.4 = (bf16[608,128]{1,0:T(8,128)(2,1)S(1)}, bf16[608,128]{1,0:T(8,128)(2,1)S(1)}, u32[]{:S(2)}, u32[]{:S(2)}) collective-permute-start(bf16[608,128]{1,0:T(8,128)(2,1)S(1)} %get-tuple-element.60), channel_id=1, source_target_pairs={{0,1},{1,0},{2,3},{3,2},{4,5},{5,4},{6,7},{7,6},{8,9},{9,8},{10,11... | collective-permute-start | bytes 466952 | tf_op jit(solution)/shard_map/ppermute | solution.py:545
  46.3 1.3 %collective-permute-start.5 = (bf16[16,32,128]{2,1,0:T(8,128)(2,1)S(1)}, bf16[16,32,128]{2,1,0:T(8,128)(2,1)S(1)}, u32[]{:S(2)}, u32[]{:S(2)}) collective-permute-start(bf16[16,32,128]{2,1,0:T(8,128)(2,1)S(1)} %all_to_all.11.mine_ref), channel_id=1, source_target_pairs={{0,1},{1,0},{2,3},{3,2},{4,5},{5,4},{6,7},{7,6},{8,9},{9,8},{10,11... | collective-permute-start | bytes 393224 | tf_op jit(solution)/shard_map/ppermute | solution.py:545

commit v8 on v7

--- a/solution.py
+++ b/solution.py
@@ -545,11 +545,11 @@
     return lax.ppermute(block, axis, [(i, j) for i, j in pairs if 0 <= j < count])
 
 
-def call(kernel, outs, args, scratch=(), flops=0, limit=8 << 20, specs=None):
+def call(kernel, outs, args, scratch=(), flops=0, limit=8 << 20):
     return pl.pallas_call(
         kernel,
         out_shape=outs,
-        in_specs=specs or [VMEM] * len(args),
+        in_specs=[VMEM] * len(args),
         out_specs=jax.tree.map(lambda _: VMEM, outs),
         scratch_shapes=list(scratch),
         compiler_params=pltpu.CompilerParams(vmem_limit_bytes=limit),
@@ -589,8 +589,8 @@
         ),
         (edge_picks, saved_pre, cotangent),
         [
-            pltpu.VMEM((frames * chans * rows, cols), F32),
-            pltpu.VMEM((frames * tall * pcol // 128, 128), F32),
+            pltpu.VMEM((frames * chans * rows + rows, cols), F32),
+            pltpu.VMEM((frames * tall * pcol // 128 + prow, 128), F32),
         ],
         flops=1 << 33,
     )

time: 48.9 us -> 48.9 us (level)
  no operation moved by 1% of the time
where the time goes in v8:
time: 48.9 us; the launch traced here: 48.6 us
  blocking collectives  26.9 us (55%)
  starting transfers between devices  10.5 us (21%)
  Pallas kernels  7.43 us (15%)
  waiting for transfers between devices  1.52 us (3%)
  local copies, waits for them, and re-layouts  1.48 us (3%)
  between operations  0.78 us (2%)
    all_to_all x2, blocking collectives, exchange(): lax.all_to_all(blocks, ('ew', 'ns'), 0, 0, axis_index_groups=groups, tile...  26.9 us
    ppermute x6, starting transfers between devices, swap(): lax.ppermute(block, axis, [(i, j) for i, j in pairs if 0 <= j < count])  10.5 us
    pallas_call x10, Pallas kernels, call(): pl.pallas_call(kernel, out_shape=outs, in_specs=[VMEM] * len(args), out_s...  7.43 us
    ppermute x6, waiting for transfers between devices, swap(): lax.ppermute(block, axis, [(i, j) for i, j in pairs if 0 <= j < count])  1.52 us
    unnamed x20, local copies, waits for them, and re-layouts  1.48 us
  transfers between devices with their start and end apart: 6, of which 3 were waited for; matrix products, arithmetic and copies ran while one was open for 0% of the time, Pallas kernels for 8%

profile of v8, /device:TPU:0, one launch (start us, length us, event | category | flops | bytes accessed | tf_op | source)
XLA Modules:
  0.0 48.6 jit_solution(5251437964269066095)
XLA Ops:
  0.6 0.0 copy-start.8
  0.6 0.0 copy-start.9
  0.7 0.2 shard_map.137
  0.8 0.7 %copy-done.8 = bf16[2,64,8,128]{3,2,1,0:T(8,128)(2,1)S(1)} copy-done((bf16[2,64,8,128]{3,2,1,0:T(8,128)(2,1)S(1)}, bf16[2,64,8,128]{3,2,1,0:T(8,128)(2,1)}, u32[]{:S(2)}) %copy-start.8) | copy-done | bytes 262168
  1.6 0.1 copy-done.9
  1.6 0.0 copy-start
  1.6 0.0 copy-start.1
  1.6 0.0 copy-start.2
  1.6 0.0 copy-start.3
  1.6 0.0 copy-start.6
  1.7 0.5 %shard_map.138 = (bf16[1024,128]{1,0:T(8,128)(2,1)S(1)}, bf16[512,256]{1,0:T(8,128)(2,1)S(1)}, bf16[8,1024]{1,0:T(8,128)(2,1)S(1)}) custom-call(bf16[16,384]{1,0:T(8,128)(2,1)S(1)} %get-tuple-element.35.pick_ref, bf16[2,64,8,128]{3,2,1,0:T(8,128)(2,1)S(1)} %copy-done.8, bf16[2,12,16,256]{3,2,1,0:T(8,128)(2,1)S(1)} %copy-done.9), custom_call_target="tpu_custom_call" | custom-call | flops 8589934592 | bytes 1024 | tf_op jit(solution)/shard_map/pallas_call | solution.py:549
  2.2 0.7 %collective-permute-start = (bf16[8,1024]{1,0:T(8,128)(2,1)S(1)}, bf16[8,1024]{1,0:T(8,128)(2,1)S(1)}, u32[]{:S(2)}, u32[]{:S(2)}) collective-permute-start(bf16[8,1024]{1,0:T(8,128)(2,1)S(1)} %get-tuple-element.36), channel_id=1, source_target_pairs={{8,16},{16,8},{9,17},{17,9},{10,18},{18,10},{11,19},{19,11},{12,20... | collective-permute-start | bytes 49160 | tf_op jit(solution)/shard_map/ppermute | solution.py:545
  2.9 5.7 %collective-permute-start.1 = (bf16[8,1024]{1,0:T(8,128)(2,1)S(1)}, bf16[8,1024]{1,0:T(8,128)(2,1)S(1)}, u32[]{:S(2)}, u32[]{:S(2)}) collective-permute-start(bf16[8,1024]{1,0:T(8,128)(2,1)S(1)} %get-tuple-element.36), channel_id=1, source_target_pairs={{0,8},{8,0},{16,24},{24,16},{1,9},{9,1},{17,25},{25,17},{2,10},{10... | collective-permute-start | bytes 49160 | tf_op jit(solution)/shard_map/ppermute | solution.py:545
  8.6 0.0 copy-start.4
  8.6 0.0 copy-start.5
  8.6 0.0 copy-start.7
  8.6 0.0 copy-done
  8.6 0.0 copy-done.1
  8.6 0.0 copy-done.2
  8.6 0.0 copy-done.3
  8.6 0.0 copy-done.6
  8.7 0.6 %copy-done.4 = bf16[768]{0:T(1024)(128)(2,1)S(1)} copy-done((bf16[768]{0:T(1024)(128)(2,1)S(1)}, bf16[768]{0:T(1024)(128)(2,1)}, u32[]{:S(2)}) %copy-start.4) | copy-done | bytes 1560
  9.3 0.0 copy-done.5
  9.3 0.0 copy-done.7
  9.3 0.8 %shard_map.139 = (bf16[48,512]{1,0:T(8,128)(2,1)S(1)}, bf16[64,256]{1,0:T(8,128)(2,1)S(1)}, bf16[48,512]{1,0:T(8,128)(2,1)S(1)}, bf16[64,256]{1,0:T(8,128)(2,1)S...) custom-call(s32[1,2]{1,0:T(1,128)S(1)} %bitcast.19, ...), custom_call_target="tpu_custom_call" | custom-call | flops 16777216 | bytes 1024 | tf_op jit(solution)/shard_map/pallas_call | solution.py:549
  10.2 0.0 collective-permute-done.sb_ref.eb_ref
  10.2 0.2 collective-permute-done.1.sa_ref.ea_ref
  10.4 0.7 %collective-permute-start.2 = (bf16[64,768]{1,0:T(8,128)(2,1)S(1)}, bf16[64,768]{1,0:T(8,128)(2,1)S(1)}, u32[]{:S(2)}, u32[]{:S(2)}) collective-permute-start(bf16[64,768]{1,0:T(8,128)(2,1)S(1)} %get-tuple-element.43), channel_id=1, source_target_pairs={{1,2},{2,1},{3,4},{4,3},{5,6},{6,5},{9,10},{10,9},{11,12},{12,11},... | collective-permute-start | bytes 294920 | tf_op jit(solution)/shard_map/ppermute | solution.py:545
  11.1 3.0 %collective-permute-start.3 = (bf16[64,768]{1,0:T(8,128)(2,1)S(1)}, bf16[64,768]{1,0:T(8,128)(2,1)S(1)}, u32[]{:S(2)}, u32[]{:S(2)}) collective-permute-start(bf16[64,768]{1,0:T(8,128)(2,1)S(1)} %get-tuple-element.44), channel_id=1, source_target_pairs={{0,1},{1,0},{2,3},{3,2},{4,5},{5,4},{6,7},{7,6},{8,9},{9,8},{10,11... | collective-permute-start | bytes 294920 | tf_op jit(solution)/shard_map/ppermute | solution.py:545
  14.1 1.9 %shard_map.141 = (bf16[512,256]{1,0:T(8,128)(2,1)S(1)}, f32[128,128]{1,0:T(8,128)S(1)}, f32[512,128]{1,0:T(8,128)S(1)}, f32[2,128,256]{2,1,0:T(8,128)S(1)}, bf16...) custom-call(bf16[8,1024]{1,0:T(8,128)(2,1)S(1)} %collective-permute-done.sb_ref.eb_ref, ...), custom_call_target="tpu_custom_call" | custom-call | flops 134217728 | bytes 1024 | tf_op jit(solution)/shard_map/pallas_call | solution.py:549
  16.0 0.0 collective-permute-done.2.rb_ref
  16.0 0.0 collective-permute-done.3.ra_ref
  16.0 1.8 %shard_map.142 = (f32[608,128]{1,0:T(8,128)S(1)}, bf16[608,128]{1,0:T(8,128)(2,1)S(1)}) custom-call(bf16[64,768]{1,0:T(8,128)(2,1)S(1)} %collective-permute-done.2.rb_ref, bf16[64,768]{1,0:T(8,128)(2,1)S(1)} %collective-permute-done.3.ra_ref, bf16[384,1024]{1,0:T(8,128)(2,1)S(1)} %get-tuple-element.45.pix_ref, ...), custom_call_target="tpu_custom_call" | custom-call | flops 134217728 | bytes 1024 | tf_op jit(solution)/shard_map/pallas_call | solution.py:549
  17.8 0.4 collective-permute-start.4
  18.2 1.1 %collective-permute-done.4.got_ref = bf16[608,128]{1,0:T(8,128)(2,1)S(1)} collective-permute-done((bf16[608,128]{1,0:T(8,128)(2,1)S(1)}, bf16[608,128]{1,0:T(8,128)(2,1)S(1)}, u32[]{:S(2)}, u32[]{:S(2)}) %collective-permute-start.4) | collective-permute-done | bytes 155680 | tf_op jit(solution)/shard_map/ppermute | solution.py:545
  19.3 16.7 %all_to_all.10.arrived_ref.got_ref = bf16[16,56,128]{2,1,0:T(8,128)(2,1)S(1)} all-to-all(bf16[16,56,128]{2,1,0:T(8,128)(2,1)S(1)} %shard_map.143), channel_id=1, replica_groups={{0,2,4,6,8,10,12,14,16,18,20,22,24,26,28,30},{1,3,5,7,9,11,13,15,17,19,..., dimensions={0} | all-to-all | bytes 458752 | tf_op jit(solution)/shard_map/all_to_all | solution.py:682
  36.0 10.3 %all_to_all.11.mine_ref = bf16[16,32,128]{2,1,0:T(8,128)(2,1)S(1)} all-to-all(bf16[16,32,128]{2,1,0:T(8,128)(2,1)S(1)} %shard_map.145), channel_id=1, replica_groups={{0,2,4,6,8,10,12,14,16,18,20,22,24,26,28,30},{1,3,5,7,9,11,13,15,17,19,..., dimensions={0} | all-to-all | bytes 262144 | tf_op jit(solution)/shard_map/all_to_all | solution.py:682
  46.3 0.0 collective-permute-start.5
  46.3 1.1 %shard_map.144 = bf16[192,768]{1,0:T(8,128)(2,1)} custom-call(bf16[16,56,128]{2,1,0:T(8,128)(2,1)S(1)} %all_to_all.10.arrived_ref.got_ref, bf16[64,768]{1,0:T(8,128)(2,1)S(1)} %bitcast.12), custom_call_target="tpu_custom_call" | custom-call | flops 134217728 | bytes 1024 | tf_op jit(solution)/shard_map/pallas_call | solution.py:549
  47.4 0.2 collective-permute-done.5.other_ref
  47.6 1.0 %shard_map.146 = (f32[64,768]{1,0:T(8,128)}, f32[4,4,64,64]{3,2,1,0:T(8,128)}, f32[4,12,4,64]{3,2,1,0:T(4,128)}, f32[768]{0:T(1024)}) custom-call(bf16[16,32,128]{2,1,0:T(8,128)(2,1)S(1)} %all_to_all.11.mine_ref, bf16[16,32,128]{2,1,0:T(8,128)(2,1)S(1)} %collective-permute-done.5.other_ref, bf16[64,768]{1,0:T(8,128)(2,1)S(1)} %bitcast.13), custom_call_target="tpu_custom_call" | custom-call | flops 1048576 | bytes 1024 | tf_op jit(solution)/shard_map/pallas_call | solution.py:549
  (3 shorter events, 0.1 us)
Async XLA Ops:
  0.6 1.0 %copy-start.8 = (bf16[2,64,8,128]{3,2,1,0:T(8,128)(2,1)S(1)}, bf16[2,64,8,128]{3,2,1,0:T(8,128)(2,1)}, u32[]{:S(2)}) copy-start(bf16[2,64,8,128]{3,2,1,0:T(8,128)(2,1)} %pre_ref.1) | copy-start | bytes 786436
  0.6 1.0 %copy-start.9 = (bf16[2,12,16,256]{3,2,1,0:T(8,128)(2,1)S(1)}, bf16[2,12,16,256]{3,2,1,0:T(8,128)(2,1)}, u32[]{:S(2)}) copy-start(bf16[2,12,16,256]{3,2,1,0:T(8,128)(2,1)} %cot_ref.1) | copy-start | bytes 589828
  1.6 7.0 %copy-start = (bf16[768,64]{0,1:T(8,128)(2,1)S(1)}, bf16[768,64]{0,1:T(8,128)(2,1)}, u32[]{:S(2)}) copy-start(bf16[768,64]{0,1:T(8,128)(2,1)} %param.15) | copy-start | bytes 294916
  1.6 7.0 %copy-start.1 = (bf16[1,1,2,64,768]{4,3,2,1,0:T(8,128)(2,1)S(1)}, bf16[1,1,2,64,768]{4,3,2,1,0:T(8,128)(2,1)}, u32[]{:S(2)}) copy-start(bf16[1,1,2,64,768]{4,3,2,1,0:T(8,128)(2,1)} %param.10) | copy-start | bytes 589828
  1.6 7.0 %copy-start.2 = (bf16[4,4,64,64]{3,2,1,0:T(8,128)(2,1)S(1)}, bf16[4,4,64,64]{3,2,1,0:T(8,128)(2,1)}, u32[]{:S(2)}) copy-start(bf16[4,4,64,64]{3,2,1,0:T(8,128)(2,1)} %first_ref.1) | copy-start | bytes 393220
  1.6 7.0 %copy-start.3 = (bf16[4,4,12,64]{3,1,2,0:T(4,128)(2,1)S(1)}, bf16[4,4,12,64]{3,1,2,0:T(4,128)(2,1)}, u32[]{:S(2)}) copy-start(bf16[4,4,12,64]{3,1,2,0:T(4,128)(2,1)} %param.17) | copy-start | bytes 73732
  1.6 7.0 %copy-start.6 = (s32[1,1,2,64,1]{3,4,2,1,0:T(1,128)S(1)}, s32[1,1,2,64,1]{3,4,2,1,0:T(1,128)}, u32[]{:S(2)}) copy-start(s32[1,1,2,64,1]{3,4,2,1,0:T(1,128)} %param.13) | copy-start | bytes 1540
  2.2 8.0 %collective-permute-start = (bf16[8,1024]{1,0:T(8,128)(2,1)S(1)}, bf16[8,1024]{1,0:T(8,128)(2,1)S(1)}, u32[]{:S(2)}, u32[]{:S(2)}) collective-permute-start(bf16[8,1024]{1,0:T(8,128)(2,1)S(1)} %get-tuple-element.36), channel_id=1, source_target_pairs={{8,16},{16,8},{9,17},{17,9},{10,18},{18,10},{11,19},{19,11},{12,20... | collective-permute-start | bytes 49160 | tf_op jit(solution)/shard_map/ppermute | solution.py:545
  2.9 7.5 %collective-permute-start.1 = (bf16[8,1024]{1,0:T(8,128)(2,1)S(1)}, bf16[8,1024]{1,0:T(8,128)(2,1)S(1)}, u32[]{:S(2)}, u32[]{:S(2)}) collective-permute-start(bf16[8,1024]{1,0:T(8,128)(2,1)S(1)} %get-tuple-element.36), channel_id=1, source_target_pairs={{0,8},{8,0},{16,24},{24,16},{1,9},{9,1},{17,25},{25,17},{2,10},{10... | collective-permute-start | bytes 49160 | tf_op jit(solution)/shard_map/ppermute | solution.py:545
  8.6 0.7 %copy-start.4 = (bf16[768]{0:T(1024)(128)(2,1)S(1)}, bf16[768]{0:T(1024)(128)(2,1)}, u32[]{:S(2)}) copy-start(bf16[768]{0:T(1024)(128)(2,1)} %mask_ref.3) | copy-start | bytes 4612
  8.6 0.7 %copy-start.5 = (s32[1,1,2,64]{3,2,1,0:T(2,128)S(1)}, s32[1,1,2,64]{3,2,1,0:T(2,128)}, u32[]{:S(2)}) copy-start(s32[1,1,2,64]{3,2,1,0:T(2,128)} %param.11) | copy-start | bytes 1540
  8.6 0.7 %copy-start.7 = (s32[1,1,2]{2,1,0:T(1,128)S(1)}, s32[1,1,2]{2,1,0:T(1,128)}, u32[]{:S(2)}) copy-start(s32[1,1,2]{2,1,0:T(1,128)} %param.12) | copy-start | bytes 28
  10.4 5.6 %collective-permute-start.2 = (bf16[64,768]{1,0:T(8,128)(2,1)S(1)}, bf16[64,768]{1,0:T(8,128)(2,1)S(1)}, u32[]{:S(2)}, u32[]{:S(2)}) collective-permute-start(bf16[64,768]{1,0:T(8,128)(2,1)S(1)} %get-tuple-element.43), channel_id=1, source_target_pairs={{1,2},{2,1},{3,4},{4,3},{5,6},{6,5},{9,10},{10,9},{11,12},{12,11},... | collective-permute-start | bytes 294920 | tf_op jit(solution)/shard_map/ppermute | solution.py:545
  11.1 4.9 %collective-permute-start.3 = (bf16[64,768]{1,0:T(8,128)(2,1)S(1)}, bf16[64,768]{1,0:T(8,128)(2,1)S(1)}, u32[]{:S(2)}, u32[]{:S(2)}) collective-permute-start(bf16[64,768]{1,0:T(8,128)(2,1)S(1)} %get-tuple-element.44), channel_id=1, source_target_pairs={{0,1},{1,0},{2,3},{3,2},{4,5},{5,4},{6,7},{7,6},{8,9},{9,8},{10,11... | collective-permute-start | bytes 294920 | tf_op jit(solution)/shard_map/ppermute | solution.py:545
  17.8 1.4 %collective-permute-start.4 = (bf16[608,128]{1,0:T(8,128)(2,1)S(1)}, bf16[608,128]{1,0:T(8,128)(2,1)S(1)}, u32[]{:S(2)}, u32[]{:S(2)}) collective-permute-start(bf16[608,128]{1,0:T(8,128)(2,1)S(1)} %get-tuple-element.60), channel_id=1, source_target_pairs={{0,1},{1,0},{2,3},{3,2},{4,5},{5,4},{6,7},{7,6},{8,9},{9,8},{10,11... | collective-permute-start | bytes 466952 | tf_op jit(solution)/shard_map/ppermute | solution.py:545
  46.3 1.3 %collective-permute-start.5 = (bf16[16,32,128]{2,1,0:T(8,128)(2,1)S(1)}, bf16[16,32,128]{2,1,0:T(8,128)(2,1)S(1)}, u32[]{:S(2)}, u32[]{:S(2)}) collective-permute-start(bf16[16,32,128]{2,1,0:T(8,128)(2,1)S(1)} %all_to_all.11.mine_ref), channel_id=1, source_target_pairs={{0,1},{1,0},{2,3},{3,2},{4,5},{5,4},{6,7},{7,6},{8,9},{9,8},{10,11... | collective-permute-start | bytes 393224 | tf_op jit(solution)/shard_map/ppermute | solution.py:545

commit v9 on v8

--- a/solution.py
+++ b/solution.py
@@ -203,7 +203,11 @@
     place = jnp.sum(earlier * hit, axis=0, keepdims=True).astype(jnp.int32)
     block = lax.rem(owner, 2) * (owners // 2) + owner // 2
     target = jnp.where(live > 0, block * slot_rows + place, -1)
-    route_ref[...] = (iota((owners * slot_rows, slots_all), 0) == target).astype(F32).astype(BF)
+    route = (iota((owners * slot_rows, slots_all), 0) == target).astype(F32).astype(BF)
+    for f in range(frames):
+        route_ref[:, f * patches : (f + 1) * patches] = nn(
+            route[:, f * slots : (f + 1) * slots], pick_ref[f]
+        ).astype(BF)
 
 
 def side_columns(ea_ref, eb_ref, even_ew):
@@ -408,9 +412,11 @@
     mask_sum = nt(hidden_ref[...], jnp.concatenate(grids, axis=1))
     chosen = [nt(pick_ref[f], jnp.concatenate([grids[f], none], axis=0)) for f in range(frames)]
     chosen = jnp.concatenate(chosen, axis=0)
-    placed = jnp.where(even_ns, chosen, pltpu.roll(chosen, chans, 1)).astype(BF)
     chosen = chosen.astype(BF)
-    routed = nn(route_ref[...], placed)
+    grid = jnp.concatenate(grids, axis=1)
+    blank = jnp.zeros_like(grid)
+    placed = [jnp.where(even_ns, grid, blank), jnp.where(even_ns, blank, grid)]
+    routed = nt(route_ref[...], jnp.concatenate(placed, axis=0))
     hi = mask_sum.astype(BF).astype(F32)
     lo = mask_sum - hi
     line = iota(hi.shape, 0)
@@ -611,7 +617,7 @@
             shape((frames, 2, 2 * chans, 2 * cols), BF),
             shape((frames, slots, patches), BF),
             shape((16, frames * patches), BF),
-            shape((n_ns * slot_rows, slots_all), BF),
+            shape((n_ns * slot_rows, frames * patches), BF),
             shape((2 * chans, 8 * chans), BF),
             shape((chans, 16 * GROUP), BF),
         ),

time: 48.9 us -> 48.8 us (level)
  no operation moved by 1% of the time
where the time goes in v9:
time: 48.8 us; the launch traced here: 48.6 us
  blocking collectives  26.9 us (55%)
  starting transfers between devices  10.4 us (21%)
  Pallas kernels  7.55 us (15%)
  local copies, waits for them, and re-layouts  1.48 us (3%)
  waiting for transfers between devices  1.39 us (3%)
  between operations  0.78 us (2%)
    all_to_all x2, blocking collectives, exchange(): lax.all_to_all(blocks, ('ew', 'ns'), 0, 0, axis_index_groups=groups, tile...  26.9 us
    ppermute x6, starting transfers between devices, swap(): lax.ppermute(block, axis, [(i, j) for i, j in pairs if 0 <= j < count])  10.4 us
    pallas_call x10, Pallas kernels, call(): pl.pallas_call(kernel, out_shape=outs, in_specs=[VMEM] * len(args), out_s...  7.55 us
    unnamed x20, local copies, waits for them, and re-layouts  1.48 us
    ppermute x6, waiting for transfers between devices, swap(): lax.ppermute(block, axis, [(i, j) for i, j in pairs if 0 <= j < count])  1.39 us
  transfers between devices with their start and end apart: 6, of which 3 were waited for; matrix products, arithmetic and copies ran while one was open for 0% of the time, Pallas kernels for 8%

profile of v9, /device:TPU:0, one launch (start us, length us, event | category | flops | bytes accessed | tf_op | source)
XLA Modules:
  0.0 48.6 jit_solution(17217930181326094733)
XLA Ops:
  0.6 0.0 copy-start.8
  0.6 0.0 copy-start.9
  0.7 0.2 shard_map.137
  0.8 0.7 %copy-done.8 = bf16[2,64,8,128]{3,2,1,0:T(8,128)(2,1)S(1)} copy-done((bf16[2,64,8,128]{3,2,1,0:T(8,128)(2,1)S(1)}, bf16[2,64,8,128]{3,2,1,0:T(8,128)(2,1)}, u32[]{:S(2)}) %copy-start.8) | copy-done | bytes 262168
  1.6 0.1 copy-done.9
  1.6 0.0 copy-start
  1.6 0.0 copy-start.1
  1.6 0.0 copy-start.2
  1.6 0.0 copy-start.3
  1.6 0.0 copy-start.6
  1.7 0.5 %shard_map.138 = (bf16[1024,128]{1,0:T(8,128)(2,1)S(1)}, bf16[512,256]{1,0:T(8,128)(2,1)S(1)}, bf16[8,1024]{1,0:T(8,128)(2,1)S(1)}) custom-call(bf16[16,384]{1,0:T(8,128)(2,1)S(1)} %get-tuple-element.35.pick_ref, bf16[2,64,8,128]{3,2,1,0:T(8,128)(2,1)S(1)} %copy-done.8, bf16[2,12,16,256]{3,2,1,0:T(8,128)(2,1)S(1)} %copy-done.9), custom_call_target="tpu_custom_call" | custom-call | flops 8589934592 | bytes 1024 | tf_op jit(solution)/shard_map/pallas_call | solution.py:555
  2.2 0.7 %collective-permute-start = (bf16[8,1024]{1,0:T(8,128)(2,1)S(1)}, bf16[8,1024]{1,0:T(8,128)(2,1)S(1)}, u32[]{:S(2)}, u32[]{:S(2)}) collective-permute-start(bf16[8,1024]{1,0:T(8,128)(2,1)S(1)} %get-tuple-element.36), channel_id=1, source_target_pairs={{8,16},{16,8},{9,17},{17,9},{10,18},{18,10},{11,19},{19,11},{12,20... | collective-permute-start | bytes 49160 | tf_op jit(solution)/shard_map/ppermute | solution.py:551
  2.9 5.7 %collective-permute-start.1 = (bf16[8,1024]{1,0:T(8,128)(2,1)S(1)}, bf16[8,1024]{1,0:T(8,128)(2,1)S(1)}, u32[]{:S(2)}, u32[]{:S(2)}) collective-permute-start(bf16[8,1024]{1,0:T(8,128)(2,1)S(1)} %get-tuple-element.36), channel_id=1, source_target_pairs={{0,8},{8,0},{16,24},{24,16},{1,9},{9,1},{17,25},{25,17},{2,10},{10... | collective-permute-start | bytes 49160 | tf_op jit(solution)/shard_map/ppermute | solution.py:551
  8.6 0.0 copy-start.4
  8.6 0.0 copy-start.5
  8.6 0.0 copy-start.7
  8.6 0.0 copy-done
  8.6 0.0 copy-done.1
  8.6 0.0 copy-done.2
  8.6 0.0 copy-done.3
  8.6 0.0 copy-done.6
  8.7 0.6 %copy-done.4 = bf16[768]{0:T(1024)(128)(2,1)S(1)} copy-done((bf16[768]{0:T(1024)(128)(2,1)S(1)}, bf16[768]{0:T(1024)(128)(2,1)}, u32[]{:S(2)}) %copy-start.4) | copy-done | bytes 1560
  9.3 0.0 copy-done.5
  9.3 0.0 copy-done.7
  9.3 1.0 %shard_map.139 = (bf16[48,512]{1,0:T(8,128)(2,1)S(1)}, bf16[64,256]{1,0:T(8,128)(2,1)S(1)}, bf16[48,512]{1,0:T(8,128)(2,1)S(1)}, bf16[64,256]{1,0:T(8,128)(2,1)S...) custom-call(s32[1,2]{1,0:T(1,128)S(1)} %bitcast.19, ...), custom_call_target="tpu_custom_call" | custom-call | flops 16777216 | bytes 1024 | tf_op jit(solution)/shard_map/pallas_call | solution.py:555
  10.3 0.0 collective-permute-done.sb_ref.eb_ref
  10.3 0.1 collective-permute-done.1.sa_ref.ea_ref
  10.4 0.7 %collective-permute-start.2 = (bf16[64,768]{1,0:T(8,128)(2,1)S(1)}, bf16[64,768]{1,0:T(8,128)(2,1)S(1)}, u32[]{:S(2)}, u32[]{:S(2)}) collective-permute-start(bf16[64,768]{1,0:T(8,128)(2,1)S(1)} %get-tuple-element.43), channel_id=1, source_target_pairs={{1,2},{2,1},{3,4},{4,3},{5,6},{6,5},{9,10},{10,9},{11,12},{12,11},... | collective-permute-start | bytes 294920 | tf_op jit(solution)/shard_map/ppermute | solution.py:551
  11.1 3.0 %collective-permute-start.3 = (bf16[64,768]{1,0:T(8,128)(2,1)S(1)}, bf16[64,768]{1,0:T(8,128)(2,1)S(1)}, u32[]{:S(2)}, u32[]{:S(2)}) collective-permute-start(bf16[64,768]{1,0:T(8,128)(2,1)S(1)} %get-tuple-element.44), channel_id=1, source_target_pairs={{0,1},{1,0},{2,3},{3,2},{4,5},{5,4},{6,7},{7,6},{8,9},{9,8},{10,11... | collective-permute-start | bytes 294920 | tf_op jit(solution)/shard_map/ppermute | solution.py:551
  14.1 1.9 %shard_map.141 = (bf16[512,256]{1,0:T(8,128)(2,1)S(1)}, f32[128,128]{1,0:T(8,128)S(1)}, f32[512,128]{1,0:T(8,128)S(1)}, f32[2,128,256]{2,1,0:T(8,128)S(1)}, bf16...) custom-call(bf16[8,1024]{1,0:T(8,128)(2,1)S(1)} %collective-permute-done.sb_ref.eb_ref, ...), custom_call_target="tpu_custom_call" | custom-call | flops 134217728 | bytes 1024 | tf_op jit(solution)/shard_map/pallas_call | solution.py:555
  16.0 0.0 collective-permute-done.2.rb_ref
  16.0 0.0 collective-permute-done.3.ra_ref
  16.0 1.8 %shard_map.142 = (f32[608,128]{1,0:T(8,128)S(1)}, bf16[608,128]{1,0:T(8,128)(2,1)S(1)}) custom-call(bf16[64,768]{1,0:T(8,128)(2,1)S(1)} %collective-permute-done.2.rb_ref, bf16[64,768]{1,0:T(8,128)(2,1)S(1)} %collective-permute-done.3.ra_ref, bf16[384,1024]{1,0:T(8,128)(2,1)S(1)} %get-tuple-element.45.pix_ref, ...), custom_call_target="tpu_custom_call" | custom-call | flops 134217728 | bytes 1024 | tf_op jit(solution)/shard_map/pallas_call | solution.py:555
  17.8 0.4 collective-permute-start.4
  18.2 1.1 %collective-permute-done.4.got_ref = bf16[608,128]{1,0:T(8,128)(2,1)S(1)} collective-permute-done((bf16[608,128]{1,0:T(8,128)(2,1)S(1)}, bf16[608,128]{1,0:T(8,128)(2,1)S(1)}, u32[]{:S(2)}, u32[]{:S(2)}) %collective-permute-start.4) | collective-permute-done | bytes 155680 | tf_op jit(solution)/shard_map/ppermute | solution.py:551
  19.3 16.7 %all_to_all.10.arrived_ref.got_ref = bf16[16,56,128]{2,1,0:T(8,128)(2,1)S(1)} all-to-all(bf16[16,56,128]{2,1,0:T(8,128)(2,1)S(1)} %shard_map.143), channel_id=1, replica_groups={{0,2,4,6,8,10,12,14,16,18,20,22,24,26,28,30},{1,3,5,7,9,11,13,15,17,19,..., dimensions={0} | all-to-all | bytes 458752 | tf_op jit(solution)/shard_map/all_to_all | solution.py:688
  36.0 10.3 %all_to_all.11.mine_ref = bf16[16,32,128]{2,1,0:T(8,128)(2,1)S(1)} all-to-all(bf16[16,32,128]{2,1,0:T(8,128)(2,1)S(1)} %shard_map.145), channel_id=1, replica_groups={{0,2,4,6,8,10,12,14,16,18,20,22,24,26,28,30},{1,3,5,7,9,11,13,15,17,19,..., dimensions={0} | all-to-all | bytes 262144 | tf_op jit(solution)/shard_map/all_to_all | solution.py:688
  46.3 0.0 collective-permute-start.5
  46.3 1.1 %shard_map.144 = bf16[192,768]{1,0:T(8,128)(2,1)} custom-call(bf16[16,56,128]{2,1,0:T(8,128)(2,1)S(1)} %all_to_all.10.arrived_ref.got_ref, bf16[64,768]{1,0:T(8,128)(2,1)S(1)} %bitcast.12), custom_call_target="tpu_custom_call" | custom-call | flops 134217728 | bytes 1024 | tf_op jit(solution)/shard_map/pallas_call | solution.py:555
  47.4 0.2 collective-permute-done.5.other_ref
  47.6 1.0 %shard_map.146 = (f32[64,768]{1,0:T(8,128)}, f32[4,4,64,64]{3,2,1,0:T(8,128)}, f32[4,12,4,64]{3,2,1,0:T(4,128)}, f32[768]{0:T(1024)}) custom-call(bf16[16,32,128]{2,1,0:T(8,128)(2,1)S(1)} %all_to_all.11.mine_ref, bf16[16,32,128]{2,1,0:T(8,128)(2,1)S(1)} %collective-permute-done.5.other_ref, bf16[64,768]{1,0:T(8,128)(2,1)S(1)} %bitcast.13), custom_call_target="tpu_custom_call" | custom-call | flops 1048576 | bytes 1024 | tf_op jit(solution)/shard_map/pallas_call | solution.py:555
  (3 shorter events, 0.1 us)
Async XLA Ops:
  0.6 1.0 %copy-start.8 = (bf16[2,64,8,128]{3,2,1,0:T(8,128)(2,1)S(1)}, bf16[2,64,8,128]{3,2,1,0:T(8,128)(2,1)}, u32[]{:S(2)}) copy-start(bf16[2,64,8,128]{3,2,1,0:T(8,128)(2,1)} %pre_ref.1) | copy-start | bytes 786436
  0.6 1.0 %copy-start.9 = (bf16[2,12,16,256]{3,2,1,0:T(8,128)(2,1)S(1)}, bf16[2,12,16,256]{3,2,1,0:T(8,128)(2,1)}, u32[]{:S(2)}) copy-start(bf16[2,12,16,256]{3,2,1,0:T(8,128)(2,1)} %cot_ref.1) | copy-start | bytes 589828
  1.6 7.0 %copy-start = (bf16[768,64]{0,1:T(8,128)(2,1)S(1)}, bf16[768,64]{0,1:T(8,128)(2,1)}, u32[]{:S(2)}) copy-start(bf16[768,64]{0,1:T(8,128)(2,1)} %param.15) | copy-start | bytes 294916
  1.6 7.0 %copy-start.1 = (bf16[1,1,2,64,768]{4,3,2,1,0:T(8,128)(2,1)S(1)}, bf16[1,1,2,64,768]{4,3,2,1,0:T(8,128)(2,1)}, u32[]{:S(2)}) copy-start(bf16[1,1,2,64,768]{4,3,2,1,0:T(8,128)(2,1)} %param.10) | copy-start | bytes 589828
  1.6 7.0 %copy-start.2 = (bf16[4,4,64,64]{3,2,1,0:T(8,128)(2,1)S(1)}, bf16[4,4,64,64]{3,2,1,0:T(8,128)(2,1)}, u32[]{:S(2)}) copy-start(bf16[4,4,64,64]{3,2,1,0:T(8,128)(2,1)} %first_ref.1) | copy-start | bytes 393220
  1.6 7.0 %copy-start.3 = (bf16[4,4,12,64]{3,1,2,0:T(4,128)(2,1)S(1)}, bf16[4,4,12,64]{3,1,2,0:T(4,128)(2,1)}, u32[]{:S(2)}) copy-start(bf16[4,4,12,64]{3,1,2,0:T(4,128)(2,1)} %param.17) | copy-start | bytes 73732
  1.6 7.0 %copy-start.6 = (s32[1,1,2,64,1]{3,4,2,1,0:T(1,128)S(1)}, s32[1,1,2,64,1]{3,4,2,1,0:T(1,128)}, u32[]{:S(2)}) copy-start(s32[1,1,2,64,1]{3,4,2,1,0:T(1,128)} %param.13) | copy-start | bytes 1540
  2.2 8.1 %collective-permute-start = (bf16[8,1024]{1,0:T(8,128)(2,1)S(1)}, bf16[8,1024]{1,0:T(8,128)(2,1)S(1)}, u32[]{:S(2)}, u32[]{:S(2)}) collective-permute-start(bf16[8,1024]{1,0:T(8,128)(2,1)S(1)} %get-tuple-element.36), channel_id=1, source_target_pairs={{8,16},{16,8},{9,17},{17,9},{10,18},{18,10},{11,19},{19,11},{12,20... | collective-permute-start | bytes 49160 | tf_op jit(solution)/shard_map/ppermute | solution.py:551
  2.9 7.5 %collective-permute-start.1 = (bf16[8,1024]{1,0:T(8,128)(2,1)S(1)}, bf16[8,1024]{1,0:T(8,128)(2,1)S(1)}, u32[]{:S(2)}, u32[]{:S(2)}) collective-permute-start(bf16[8,1024]{1,0:T(8,128)(2,1)S(1)} %get-tuple-element.36), channel_id=1, source_target_pairs={{0,8},{8,0},{16,24},{24,16},{1,9},{9,1},{17,25},{25,17},{2,10},{10... | collective-permute-start | bytes 49160 | tf_op jit(solution)/shard_map/ppermute | solution.py:551
  8.6 0.7 %copy-start.4 = (bf16[768]{0:T(1024)(128)(2,1)S(1)}, bf16[768]{0:T(1024)(128)(2,1)}, u32[]{:S(2)}) copy-start(bf16[768]{0:T(1024)(128)(2,1)} %mask_ref.3) | copy-start | bytes 4612
  8.6 0.7 %copy-start.5 = (s32[1,1,2,64]{3,2,1,0:T(2,128)S(1)}, s32[1,1,2,64]{3,2,1,0:T(2,128)}, u32[]{:S(2)}) copy-start(s32[1,1,2,64]{3,2,1,0:T(2,128)} %param.11) | copy-start | bytes 1540
  8.6 0.7 %copy-start.7 = (s32[1,1,2]{2,1,0:T(1,128)S(1)}, s32[1,1,2]{2,1,0:T(1,128)}, u32[]{:S(2)}) copy-start(s32[1,1,2]{2,1,0:T(1,128)} %param.12) | copy-start | bytes 28
  10.4 5.6 %collective-permute-start.2 = (bf16[64,768]{1,0:T(8,128)(2,1)S(1)}, bf16[64,768]{1,0:T(8,128)(2,1)S(1)}, u32[]{:S(2)}, u32[]{:S(2)}) collective-permute-start(bf16[64,768]{1,0:T(8,128)(2,1)S(1)} %get-tuple-element.43), channel_id=1, source_target_pairs={{1,2},{2,1},{3,4},{4,3},{5,6},{6,5},{9,10},{10,9},{11,12},{12,11},... | collective-permute-start | bytes 294920 | tf_op jit(solution)/shard_map/ppermute | solution.py:551
  11.1 4.9 %collective-permute-start.3 = (bf16[64,768]{1,0:T(8,128)(2,1)S(1)}, bf16[64,768]{1,0:T(8,128)(2,1)S(1)}, u32[]{:S(2)}, u32[]{:S(2)}) collective-permute-start(bf16[64,768]{1,0:T(8,128)(2,1)S(1)} %get-tuple-element.44), channel_id=1, source_target_pairs={{0,1},{1,0},{2,3},{3,2},{4,5},{5,4},{6,7},{7,6},{8,9},{9,8},{10,11... | collective-permute-start | bytes 294920 | tf_op jit(solution)/shard_map/ppermute | solution.py:551
  17.8 1.4 %collective-permute-start.4 = (bf16[608,128]{1,0:T(8,128)(2,1)S(1)}, bf16[608,128]{1,0:T(8,128)(2,1)S(1)}, u32[]{:S(2)}, u32[]{:S(2)}) collective-permute-start(bf16[608,128]{1,0:T(8,128)(2,1)S(1)} %get-tuple-element.60), channel_id=1, source_target_pairs={{0,1},{1,0},{2,3},{3,2},{4,5},{5,4},{6,7},{7,6},{8,9},{9,8},{10,11... | collective-permute-start | bytes 466952 | tf_op jit(solution)/shard_map/ppermute | solution.py:551
  46.3 1.3 %collective-permute-start.5 = (bf16[16,32,128]{2,1,0:T(8,128)(2,1)S(1)}, bf16[16,32,128]{2,1,0:T(8,128)(2,1)S(1)}, u32[]{:S(2)}, u32[]{:S(2)}) collective-permute-start(bf16[16,32,128]{2,1,0:T(8,128)(2,1)S(1)} %all_to_all.11.mine_ref), channel_id=1, source_target_pairs={{0,1},{1,0},{2,3},{3,2},{4,5},{5,4},{6,7},{7,6},{8,9},{9,8},{10,11... | collective-permute-start | bytes 393224 | tf_op jit(solution)/shard_map/ppermute | solution.py:551

commit v10 on v8

--- a/solution.py
+++ b/solution.py
@@ -206,8 +206,13 @@
     route_ref[...] = (iota((owners * slot_rows, slots_all), 0) == target).astype(F32).astype(BF)
 
 
-def side_columns(ea_ref, eb_ref, even_ew):
-    ea, eb = ea_ref[...].astype(F32), eb_ref[...].astype(F32)
+def scene_side(ref, n_ew):
+    ew = lax.axis_index("ew")
+    return jnp.where((ew == 0) | (ew == n_ew - 1), 0.0, ref[...].astype(F32))
+
+
+def side_columns(ea_ref, eb_ref, even_ew, n_ew):
+    ea, eb = ea_ref[...].astype(F32), scene_side(eb_ref, n_ew)
     return jnp.concatenate([jnp.where(even_ew, ea, eb), jnp.where(even_ew, eb, ea)], axis=0).astype(BF)
 
 
@@ -251,9 +256,9 @@
     return [wins[pl.ds(at, 4 * GROUP), b * 2 * cols : (b + 1) * 2 * cols] for b in range(4)]
 
 
-def message_kernel(sb_ref, sa_ref, ga_ref, pa_ref, gb_ref, pb_ref, a_ref, b_ref):
+def message_kernel(n_ew, sb_ref, sa_ref, ga_ref, pa_ref, gb_ref, pb_ref, a_ref, b_ref):
     deep, span = ga_ref.shape
-    corners = jnp.concatenate([sa_ref[:, :span].astype(F32), sb_ref[:, :span].astype(F32)], axis=0).astype(BF)
+    corners = jnp.concatenate([sa_ref[:, :span].astype(F32), scene_side(sb_ref, n_ew)[:, :span]], axis=0).astype(BF)
     for out, g, p in ((a_ref, ga_ref, pa_ref), (b_ref, gb_ref, pb_ref)):
         out[:deep, :span] = g[...]
         out[deep:, :span] = corners
@@ -270,7 +275,7 @@
     tall = g_ref.shape[0] // frames
     rows = p_ref.shape[0] // (frames * chans)
     ew = lax.axis_index("ew")
-    sides = side_columns(ea_ref, eb_ref, lax.rem(ew, 2) == 0)
+    sides = side_columns(ea_ref, eb_ref, lax.rem(ew, 2) == 0, n_ew)
     pick_g, pick_p = halo_tables()
     line = frames * chans
     ext[:, :pcol] = g_ref[...]
@@ -539,9 +544,11 @@
     mask_out[...] = grad_mask.reshape(features)
 
 
-def swap(block, axis, offset):
+def swap(block, axis, offset, ring=False):
     count = lax.axis_size(axis)
     pairs = [(i, ((i + offset) ^ 1) - offset) for i in range(count)]
+    if ring and count % 2 == 0:
+        pairs = [(i, j % count) for i, j in pairs]
     return lax.ppermute(block, axis, [(i, j) for i, j in pairs if 0 <= j < count])
 
 
@@ -594,7 +601,7 @@
         ],
         flops=1 << 33,
     )
-    side_b = swap(own_edges, "ew", 1)
+    side_b = swap(own_edges, "ew", 1, ring=True)
     side_a = swap(own_edges, "ew", 0)
 
     tile_tokens = tokens.reshape(slots_all, features)
@@ -631,7 +638,7 @@
     )
     message_shape = shape((3 * GROUP + 16, frames * (pcol + cols)), BF)
     send_a, send_b = call(
-        message_kernel,
+        functools.partial(message_kernel, n_ew),
         (message_shape, message_shape),
         (side_b, side_a, g_a, p_a, g_b, p_b),
         flops=1 << 20,

time: 48.9 us -> 47.2 us (0.965)
  starting transfers between devices: 10.5 us -> 8.49 us
  waiting for transfers between devices: 1.52 us -> 2.93 us
  blocking collectives: 26.9 us -> 25.9 us
    ppermute x6, starting transfers between devices: 10.5 us -> 8.49 us  [swap(): lax.ppermute(block, axis, [(i, j) for i, j in pairs if 0 <= j < count])]
    ppermute x6, waiting for transfers between devices: 1.52 us -> 2.93 us  [swap(): lax.ppermute(block, axis, [(i, j) for i, j in pairs if 0 <= j < count])]
    all_to_all x2, blocking collectives: 26.9 us -> 25.9 us  [exchange(): lax.all_to_all(blocks, ('ew', 'ns'), 0, 0, axis_index_groups=groups, tile...]
where the time goes in v10:
time: 47.2 us; the launch traced here: 47 us
  blocking collectives  25.9 us (55%)
  starting transfers between devices  8.49 us (18%)
  Pallas kernels  7.43 us (16%)
  waiting for transfers between devices  2.93 us (6%)
  local copies, waits for them, and re-layouts  1.48 us (3%)
  between operations  0.78 us (2%)
    all_to_all x2, blocking collectives, exchange(): lax.all_to_all(blocks, ('ew', 'ns'), 0, 0, axis_index_groups=groups, tile...  25.9 us
    ppermute x6, starting transfers between devices, swap(): lax.ppermute(block, axis, [(i, j) for i, j in pairs if 0 <= j < count])  8.49 us
    pallas_call x10, Pallas kernels, call(): pl.pallas_call(kernel, out_shape=outs, in_specs=[VMEM] * len(args), out_s...  7.43 us
    ppermute x6, waiting for transfers between devices, swap(): lax.ppermute(block, axis, [(i, j) for i, j in pairs if 0 <= j < count])  2.93 us
    unnamed x20, local copies, waits for them, and re-layouts  1.48 us
  transfers between devices with their start and end apart: 6, of which 3 were waited for; matrix products, arithmetic and copies ran while one was open for 0% of the time, Pallas kernels for 8%

profile of v10, /device:TPU:0, one launch (start us, length us, event | category | flops | bytes accessed | tf_op | source)
XLA Modules:
  0.0 47.0 jit_solution(9507102515029853960)
XLA Ops:
  0.6 0.0 copy-start.8
  0.6 0.0 copy-start.9
  0.7 0.2 shard_map.137
  0.8 0.7 %copy-done.8 = bf16[2,64,8,128]{3,2,1,0:T(8,128)(2,1)S(1)} copy-done((bf16[2,64,8,128]{3,2,1,0:T(8,128)(2,1)S(1)}, bf16[2,64,8,128]{3,2,1,0:T(8,128)(2,1)}, u32[]{:S(2)}) %copy-start.8) | copy-done | bytes 262168
  1.6 0.1 copy-done.9
  1.6 0.0 copy-start
  1.6 0.0 copy-start.1
  1.6 0.0 copy-start.2
  1.6 0.0 copy-start.3
  1.6 0.0 copy-start.6
  1.7 0.5 %shard_map.138 = (bf16[1024,128]{1,0:T(8,128)(2,1)S(1)}, bf16[512,256]{1,0:T(8,128)(2,1)S(1)}, bf16[8,1024]{1,0:T(8,128)(2,1)S(1)}) custom-call(bf16[16,384]{1,0:T(8,128)(2,1)S(1)} %get-tuple-element.35.pick_ref, bf16[2,64,8,128]{3,2,1,0:T(8,128)(2,1)S(1)} %copy-done.8, bf16[2,12,16,256]{3,2,1,0:T(8,128)(2,1)S(1)} %copy-done.9), custom_call_target="tpu_custom_call" | custom-call | flops 8589934592 | bytes 1024 | tf_op jit(solution)/shard_map/pallas_call | solution.py:556
  2.2 3.9 %collective-permute-start = (bf16[8,1024]{1,0:T(8,128)(2,1)S(1)}, bf16[8,1024]{1,0:T(8,128)(2,1)S(1)}, u32[]{:S(2)}, u32[]{:S(2)}) collective-permute-start(bf16[8,1024]{1,0:T(8,128)(2,1)S(1)} %get-tuple-element.36), channel_id=1, source_target_pairs={{0,24},{8,16},{16,8},{24,0},{1,25},{9,17},{17,9},{25,1},{2,26},{10... | collective-permute-start | bytes 49160 | tf_op jit(solution)/shard_map/ppermute | solution.py:552
  6.1 0.5 %collective-permute-start.1 = (bf16[8,1024]{1,0:T(8,128)(2,1)S(1)}, bf16[8,1024]{1,0:T(8,128)(2,1)S(1)}, u32[]{:S(2)}, u32[]{:S(2)}) collective-permute-start(bf16[8,1024]{1,0:T(8,128)(2,1)S(1)} %get-tuple-element.36), channel_id=1, source_target_pairs={{0,8},{8,0},{16,24},{24,16},{1,9},{9,1},{17,25},{25,17},{2,10},{10... | collective-permute-start | bytes 49160 | tf_op jit(solution)/shard_map/ppermute | solution.py:552
  6.6 0.0 copy-start.4
  6.6 0.0 copy-start.5
  6.6 0.0 copy-start.7
  6.6 0.0 copy-done
  6.6 0.0 copy-done.1
  6.7 0.0 copy-done.2
  6.7 0.0 copy-done.3
  6.7 0.0 copy-done.6
  6.7 0.6 %copy-done.4 = bf16[768]{0:T(1024)(128)(2,1)S(1)} copy-done((bf16[768]{0:T(1024)(128)(2,1)S(1)}, bf16[768]{0:T(1024)(128)(2,1)}, u32[]{:S(2)}) %copy-start.4) | copy-done | bytes 1560
  7.3 0.0 copy-done.5
  7.3 0.0 copy-done.7
  7.3 0.8 %shard_map.139 = (bf16[48,512]{1,0:T(8,128)(2,1)S(1)}, bf16[64,256]{1,0:T(8,128)(2,1)S(1)}, bf16[48,512]{1,0:T(8,128)(2,1)S(1)}, bf16[64,256]{1,0:T(8,128)(2,1)S...) custom-call(s32[1,2]{1,0:T(1,128)S(1)} %bitcast.19, ...), custom_call_target="tpu_custom_call" | custom-call | flops 16777216 | bytes 1024 | tf_op jit(solution)/shard_map/pallas_call | solution.py:556
  8.2 0.0 collective-permute-done.sb_ref.eb_ref
  8.2 1.6 %collective-permute-done.1.sa_ref.ea_ref = bf16[8,1024]{1,0:T(8,128)(2,1)S(1)} collective-permute-done((bf16[8,1024]{1,0:T(8,128)(2,1)S(1)}, bf16[8,1024]{1,0:T(8,128)(2,1)S(1)}, u32[]{:S(2)}, u32[]{:S(2)}) %collective-permute-start.1) | collective-permute-done | bytes 16416 | tf_op jit(solution)/shard_map/ppermute | solution.py:552
  9.9 0.7 %collective-permute-start.2 = (bf16[64,768]{1,0:T(8,128)(2,1)S(1)}, bf16[64,768]{1,0:T(8,128)(2,1)S(1)}, u32[]{:S(2)}, u32[]{:S(2)}) collective-permute-start(bf16[64,768]{1,0:T(8,128)(2,1)S(1)} %get-tuple-element.43), channel_id=1, source_target_pairs={{1,2},{2,1},{3,4},{4,3},{5,6},{6,5},{9,10},{10,9},{11,12},{12,11},... | collective-permute-start | bytes 294920 | tf_op jit(solution)/shard_map/ppermute | solution.py:552
  10.5 3.0 %collective-permute-start.3 = (bf16[64,768]{1,0:T(8,128)(2,1)S(1)}, bf16[64,768]{1,0:T(8,128)(2,1)S(1)}, u32[]{:S(2)}, u32[]{:S(2)}) collective-permute-start(bf16[64,768]{1,0:T(8,128)(2,1)S(1)} %get-tuple-element.44), channel_id=1, source_target_pairs={{0,1},{1,0},{2,3},{3,2},{4,5},{5,4},{6,7},{7,6},{8,9},{9,8},{10,11... | collective-permute-start | bytes 294920 | tf_op jit(solution)/shard_map/ppermute | solution.py:552
  13.5 1.9 %shard_map.141 = (bf16[512,256]{1,0:T(8,128)(2,1)S(1)}, f32[128,128]{1,0:T(8,128)S(1)}, f32[512,128]{1,0:T(8,128)S(1)}, f32[2,128,256]{2,1,0:T(8,128)S(1)}, bf16...) custom-call(bf16[8,1024]{1,0:T(8,128)(2,1)S(1)} %collective-permute-done.sb_ref.eb_ref, ...), custom_call_target="tpu_custom_call" | custom-call | flops 134217728 | bytes 1024 | tf_op jit(solution)/shard_map/pallas_call | solution.py:556
  15.4 0.0 collective-permute-done.2.rb_ref
  15.4 0.0 collective-permute-done.3.ra_ref
  15.5 1.8 %shard_map.142 = (f32[608,128]{1,0:T(8,128)S(1)}, bf16[608,128]{1,0:T(8,128)(2,1)S(1)}) custom-call(bf16[64,768]{1,0:T(8,128)(2,1)S(1)} %collective-permute-done.2.rb_ref, bf16[64,768]{1,0:T(8,128)(2,1)S(1)} %collective-permute-done.3.ra_ref, bf16[384,1024]{1,0:T(8,128)(2,1)S(1)} %get-tuple-element.45.pix_ref, ...), custom_call_target="tpu_custom_call" | custom-call | flops 134217728 | bytes 1024 | tf_op jit(solution)/shard_map/pallas_call | solution.py:556
  17.3 0.4 collective-permute-start.4
  17.6 1.1 %collective-permute-done.4.got_ref = bf16[608,128]{1,0:T(8,128)(2,1)S(1)} collective-permute-done((bf16[608,128]{1,0:T(8,128)(2,1)S(1)}, bf16[608,128]{1,0:T(8,128)(2,1)S(1)}, u32[]{:S(2)}, u32[]{:S(2)}) %collective-permute-start.4) | collective-permute-done | bytes 155680 | tf_op jit(solution)/shard_map/ppermute | solution.py:552
  18.7 15.6 %all_to_all.10.arrived_ref.got_ref = bf16[16,56,128]{2,1,0:T(8,128)(2,1)S(1)} all-to-all(bf16[16,56,128]{2,1,0:T(8,128)(2,1)S(1)} %shard_map.143), channel_id=1, replica_groups={{0,2,4,6,8,10,12,14,16,18,20,22,24,26,28,30},{1,3,5,7,9,11,13,15,17,19,..., dimensions={0} | all-to-all | bytes 458752 | tf_op jit(solution)/shard_map/all_to_all | solution.py:689
  34.4 10.3 %all_to_all.11.mine_ref = bf16[16,32,128]{2,1,0:T(8,128)(2,1)S(1)} all-to-all(bf16[16,32,128]{2,1,0:T(8,128)(2,1)S(1)} %shard_map.145), channel_id=1, replica_groups={{0,2,4,6,8,10,12,14,16,18,20,22,24,26,28,30},{1,3,5,7,9,11,13,15,17,19,..., dimensions={0} | all-to-all | bytes 262144 | tf_op jit(solution)/shard_map/all_to_all | solution.py:689
  44.7 0.0 collective-permute-start.5
  44.7 1.1 %shard_map.144 = bf16[192,768]{1,0:T(8,128)(2,1)} custom-call(bf16[16,56,128]{2,1,0:T(8,128)(2,1)S(1)} %all_to_all.10.arrived_ref.got_ref, bf16[64,768]{1,0:T(8,128)(2,1)S(1)} %bitcast.12), custom_call_target="tpu_custom_call" | custom-call | flops 134217728 | bytes 1024 | tf_op jit(solution)/shard_map/pallas_call | solution.py:556
  45.8 0.2 collective-permute-done.5.other_ref
  46.0 1.0 %shard_map.146 = (f32[64,768]{1,0:T(8,128)}, f32[4,4,64,64]{3,2,1,0:T(8,128)}, f32[4,12,4,64]{3,2,1,0:T(4,128)}, f32[768]{0:T(1024)}) custom-call(bf16[16,32,128]{2,1,0:T(8,128)(2,1)S(1)} %all_to_all.11.mine_ref, bf16[16,32,128]{2,1,0:T(8,128)(2,1)S(1)} %collective-permute-done.5.other_ref, bf16[64,768]{1,0:T(8,128)(2,1)S(1)} %bitcast.13), custom_call_target="tpu_custom_call" | custom-call | flops 1048576 | bytes 1024 | tf_op jit(solution)/shard_map/pallas_call | solution.py:556
  (3 shorter events, 0.1 us)
Async XLA Ops:
  0.6 1.0 %copy-start.8 = (bf16[2,64,8,128]{3,2,1,0:T(8,128)(2,1)S(1)}, bf16[2,64,8,128]{3,2,1,0:T(8,128)(2,1)}, u32[]{:S(2)}) copy-start(bf16[2,64,8,128]{3,2,1,0:T(8,128)(2,1)} %pre_ref.1) | copy-start | bytes 786436
  0.6 1.0 %copy-start.9 = (bf16[2,12,16,256]{3,2,1,0:T(8,128)(2,1)S(1)}, bf16[2,12,16,256]{3,2,1,0:T(8,128)(2,1)}, u32[]{:S(2)}) copy-start(bf16[2,12,16,256]{3,2,1,0:T(8,128)(2,1)} %cot_ref.1) | copy-start | bytes 589828
  1.6 5.0 %copy-start = (bf16[768,64]{0,1:T(8,128)(2,1)S(1)}, bf16[768,64]{0,1:T(8,128)(2,1)}, u32[]{:S(2)}) copy-start(bf16[768,64]{0,1:T(8,128)(2,1)} %param.15) | copy-start | bytes 294916
  1.6 5.0 %copy-start.1 = (bf16[1,1,2,64,768]{4,3,2,1,0:T(8,128)(2,1)S(1)}, bf16[1,1,2,64,768]{4,3,2,1,0:T(8,128)(2,1)}, u32[]{:S(2)}) copy-start(bf16[1,1,2,64,768]{4,3,2,1,0:T(8,128)(2,1)} %param.10) | copy-start | bytes 589828
  1.6 5.0 %copy-start.2 = (bf16[4,4,64,64]{3,2,1,0:T(8,128)(2,1)S(1)}, bf16[4,4,64,64]{3,2,1,0:T(8,128)(2,1)}, u32[]{:S(2)}) copy-start(bf16[4,4,64,64]{3,2,1,0:T(8,128)(2,1)} %first_ref.1) | copy-start | bytes 393220
  1.6 5.0 %copy-start.3 = (bf16[4,4,12,64]{3,1,2,0:T(4,128)(2,1)S(1)}, bf16[4,4,12,64]{3,1,2,0:T(4,128)(2,1)}, u32[]{:S(2)}) copy-start(bf16[4,4,12,64]{3,1,2,0:T(4,128)(2,1)} %param.17) | copy-start | bytes 73732
  1.6 5.0 %copy-start.6 = (s32[1,1,2,64,1]{3,4,2,1,0:T(1,128)S(1)}, s32[1,1,2,64,1]{3,4,2,1,0:T(1,128)}, u32[]{:S(2)}) copy-start(s32[1,1,2,64,1]{3,4,2,1,0:T(1,128)} %param.13) | copy-start | bytes 1540
  2.2 6.0 %collective-permute-start = (bf16[8,1024]{1,0:T(8,128)(2,1)S(1)}, bf16[8,1024]{1,0:T(8,128)(2,1)S(1)}, u32[]{:S(2)}, u32[]{:S(2)}) collective-permute-start(bf16[8,1024]{1,0:T(8,128)(2,1)S(1)} %get-tuple-element.36), channel_id=1, source_target_pairs={{0,24},{8,16},{16,8},{24,0},{1,25},{9,17},{17,9},{25,1},{2,26},{10... | collective-permute-start | bytes 49160 | tf_op jit(solution)/shard_map/ppermute | solution.py:552
  6.1 3.7 %collective-permute-start.1 = (bf16[8,1024]{1,0:T(8,128)(2,1)S(1)}, bf16[8,1024]{1,0:T(8,128)(2,1)S(1)}, u32[]{:S(2)}, u32[]{:S(2)}) collective-permute-start(bf16[8,1024]{1,0:T(8,128)(2,1)S(1)} %get-tuple-element.36), channel_id=1, source_target_pairs={{0,8},{8,0},{16,24},{24,16},{1,9},{9,1},{17,25},{25,17},{2,10},{10... | collective-permute-start | bytes 49160 | tf_op jit(solution)/shard_map/ppermute | solution.py:552
  6.6 0.7 %copy-start.4 = (bf16[768]{0:T(1024)(128)(2,1)S(1)}, bf16[768]{0:T(1024)(128)(2,1)}, u32[]{:S(2)}) copy-start(bf16[768]{0:T(1024)(128)(2,1)} %mask_ref.3) | copy-start | bytes 4612
  6.6 0.7 %copy-start.5 = (s32[1,1,2,64]{3,2,1,0:T(2,128)S(1)}, s32[1,1,2,64]{3,2,1,0:T(2,128)}, u32[]{:S(2)}) copy-start(s32[1,1,2,64]{3,2,1,0:T(2,128)} %param.11) | copy-start | bytes 1540
  6.6 0.7 %copy-start.7 = (s32[1,1,2]{2,1,0:T(1,128)S(1)}, s32[1,1,2]{2,1,0:T(1,128)}, u32[]{:S(2)}) copy-start(s32[1,1,2]{2,1,0:T(1,128)} %param.12) | copy-start | bytes 28
  9.9 5.6 %collective-permute-start.2 = (bf16[64,768]{1,0:T(8,128)(2,1)S(1)}, bf16[64,768]{1,0:T(8,128)(2,1)S(1)}, u32[]{:S(2)}, u32[]{:S(2)}) collective-permute-start(bf16[64,768]{1,0:T(8,128)(2,1)S(1)} %get-tuple-element.43), channel_id=1, source_target_pairs={{1,2},{2,1},{3,4},{4,3},{5,6},{6,5},{9,10},{10,9},{11,12},{12,11},... | collective-permute-start | bytes 294920 | tf_op jit(solution)/shard_map/ppermute | solution.py:552
  10.5 4.9 %collective-permute-start.3 = (bf16[64,768]{1,0:T(8,128)(2,1)S(1)}, bf16[64,768]{1,0:T(8,128)(2,1)S(1)}, u32[]{:S(2)}, u32[]{:S(2)}) collective-permute-start(bf16[64,768]{1,0:T(8,128)(2,1)S(1)} %get-tuple-element.44), channel_id=1, source_target_pairs={{0,1},{1,0},{2,3},{3,2},{4,5},{5,4},{6,7},{7,6},{8,9},{9,8},{10,11... | collective-permute-start | bytes 294920 | tf_op jit(solution)/shard_map/ppermute | solution.py:552
  17.3 1.4 %collective-permute-start.4 = (bf16[608,128]{1,0:T(8,128)(2,1)S(1)}, bf16[608,128]{1,0:T(8,128)(2,1)S(1)}, u32[]{:S(2)}, u32[]{:S(2)}) collective-permute-start(bf16[608,128]{1,0:T(8,128)(2,1)S(1)} %get-tuple-element.60), channel_id=1, source_target_pairs={{0,1},{1,0},{2,3},{3,2},{4,5},{5,4},{6,7},{7,6},{8,9},{9,8},{10,11... | collective-permute-start | bytes 466952 | tf_op jit(solution)/shard_map/ppermute | solution.py:552
  44.7 1.3 %collective-permute-start.5 = (bf16[16,32,128]{2,1,0:T(8,128)(2,1)S(1)}, bf16[16,32,128]{2,1,0:T(8,128)(2,1)S(1)}, u32[]{:S(2)}, u32[]{:S(2)}) collective-permute-start(bf16[16,32,128]{2,1,0:T(8,128)(2,1)S(1)} %all_to_all.11.mine_ref), channel_id=1, source_target_pairs={{0,1},{1,0},{2,3},{3,2},{4,5},{5,4},{6,7},{7,6},{8,9},{9,8},{10,11... | collective-permute-start | bytes 393224 | tf_op jit(solution)/shard_map/ppermute | solution.py:552

commit v11 on v10

--- a/solution.py
+++ b/solution.py
@@ -342,6 +342,7 @@
     even_ns = lax.rem(ns, 2) == 0
     even_ew = lax.rem(ew, 2) == 0
     ra, rb = ra_ref[...], rb_ref[...]
+    rb = jnp.where((ns == 0) | (ns == n_ns - 1), jnp.zeros_like(rb), rb)
     north = jnp.where(even_ns, rb, ra)
     south = jnp.where(even_ns, ra, rb)
     span = frames * pcol
@@ -643,7 +644,7 @@
         (side_b, side_a, g_a, p_a, g_b, p_b),
         flops=1 << 20,
     )
-    got_b = swap(send_b, "ns", 1)
+    got_b = swap(send_b, "ns", 1, ring=True)
     got_a = swap(send_a, "ns", 0)
 
     delta_mid, second_mid, first_mid, turn_mid, edge_wins, edge_pre = call(

time: 47.2 us -> 46.5 us (0.985)
  waiting for transfers between devices: 2.93 us -> 6.07 us
  starting transfers between devices: 8.49 us -> 6.45 us
  blocking collectives: 25.9 us -> 24 us
    ppermute x6, waiting for transfers between devices: 2.93 us -> 6.07 us  [swap(): lax.ppermute(block, axis, [(i, j) for i, j in pairs if 0 <= j < count])]
    ppermute x6, starting transfers between devices: 8.49 us -> 6.45 us  [swap(): lax.ppermute(block, axis, [(i, j) for i, j in pairs if 0 <= j < count])]
    all_to_all x2, blocking collectives: 25.9 us -> 24 us  [exchange(): lax.all_to_all(blocks, ('ew', 'ns'), 0, 0, axis_index_groups=groups, tile...]
  transfers between devices with their start and end apart: 6 -> 6, of which waited for: 3 -> 4; matrix products, arithmetic and copies ran while one was open for 0% -> 0% of each run, Pallas kernels for 8% -> 8%
where the time goes in v11:
time: 46.5 us; the launch traced here: 46.2 us
  blocking collectives  24 us (52%)
  Pallas kernels  7.43 us (16%)
  starting transfers between devices  6.45 us (14%)
  waiting for transfers between devices  6.07 us (13%)
  local copies, waits for them, and re-layouts  1.48 us (3%)
  between operations  0.76 us (2%)
    all_to_all x2, blocking collectives, exchange(): lax.all_to_all(blocks, ('ew', 'ns'), 0, 0, axis_index_groups=groups, tile...  24 us
    pallas_call x10, Pallas kernels, call(): pl.pallas_call(kernel, out_shape=outs, in_specs=[VMEM] * len(args), out_s...  7.43 us
    ppermute x6, starting transfers between devices, swap(): lax.ppermute(block, axis, [(i, j) for i, j in pairs if 0 <= j < count])  6.45 us
    ppermute x6, waiting for transfers between devices, swap(): lax.ppermute(block, axis, [(i, j) for i, j in pairs if 0 <= j < count])  6.07 us
    unnamed x20, local copies, waits for them, and re-layouts  1.48 us
  transfers between devices with their start and end apart: 6, of which 4 were waited for; matrix products, arithmetic and copies ran while one was open for 0% of the time, Pallas kernels for 8%

profile of v11, /device:TPU:0, one launch (start us, length us, event | category | flops | bytes accessed | tf_op | source)
XLA Modules:
  0.0 46.2 jit_solution(8437060852633389296)
XLA Ops:
  0.6 0.0 copy-start.8
  0.6 0.0 copy-start.9
  0.7 0.2 shard_map.137
  0.8 0.7 %copy-done.8 = bf16[2,64,8,128]{3,2,1,0:T(8,128)(2,1)S(1)} copy-done((bf16[2,64,8,128]{3,2,1,0:T(8,128)(2,1)S(1)}, bf16[2,64,8,128]{3,2,1,0:T(8,128)(2,1)}, u32[]{:S(2)}) %copy-start.8) | copy-done | bytes 262168
  1.6 0.1 copy-done.9
  1.6 0.0 copy-start
  1.6 0.0 copy-start.1
  1.6 0.0 copy-start.2
  1.6 0.0 copy-start.3
  1.6 0.0 copy-start.6
  1.7 0.5 %shard_map.138 = (bf16[1024,128]{1,0:T(8,128)(2,1)S(1)}, bf16[512,256]{1,0:T(8,128)(2,1)S(1)}, bf16[8,1024]{1,0:T(8,128)(2,1)S(1)}) custom-call(bf16[16,384]{1,0:T(8,128)(2,1)S(1)} %get-tuple-element.35.pick_ref, bf16[2,64,8,128]{3,2,1,0:T(8,128)(2,1)S(1)} %copy-done.8, bf16[2,12,16,256]{3,2,1,0:T(8,128)(2,1)S(1)} %copy-done.9), custom_call_target="tpu_custom_call" | custom-call | flops 8589934592 | bytes 1024 | tf_op jit(solution)/shard_map/pallas_call | solution.py:557
  2.2 3.9 %collective-permute-start = (bf16[8,1024]{1,0:T(8,128)(2,1)S(1)}, bf16[8,1024]{1,0:T(8,128)(2,1)S(1)}, u32[]{:S(2)}, u32[]{:S(2)}) collective-permute-start(bf16[8,1024]{1,0:T(8,128)(2,1)S(1)} %get-tuple-element.36), channel_id=1, source_target_pairs={{0,24},{8,16},{16,8},{24,0},{1,25},{9,17},{17,9},{25,1},{2,26},{10... | collective-permute-start | bytes 49160 | tf_op jit(solution)/shard_map/ppermute | solution.py:553
  6.1 0.5 %collective-permute-start.1 = (bf16[8,1024]{1,0:T(8,128)(2,1)S(1)}, bf16[8,1024]{1,0:T(8,128)(2,1)S(1)}, u32[]{:S(2)}, u32[]{:S(2)}) collective-permute-start(bf16[8,1024]{1,0:T(8,128)(2,1)S(1)} %get-tuple-element.36), channel_id=1, source_target_pairs={{0,8},{8,0},{16,24},{24,16},{1,9},{9,1},{17,25},{25,17},{2,10},{10... | collective-permute-start | bytes 49160 | tf_op jit(solution)/shard_map/ppermute | solution.py:553
  6.6 0.0 copy-start.4
  6.6 0.0 copy-start.5
  6.6 0.0 copy-start.7
  6.6 0.0 copy-done
  6.6 0.0 copy-done.1
  6.7 0.0 copy-done.2
  6.7 0.0 copy-done.3
  6.7 0.0 copy-done.6
  6.7 0.6 %copy-done.4 = bf16[768]{0:T(1024)(128)(2,1)S(1)} copy-done((bf16[768]{0:T(1024)(128)(2,1)S(1)}, bf16[768]{0:T(1024)(128)(2,1)}, u32[]{:S(2)}) %copy-start.4) | copy-done | bytes 1560
  7.3 0.0 copy-done.5
  7.3 0.0 copy-done.7
  7.3 0.8 %shard_map.139 = (bf16[48,512]{1,0:T(8,128)(2,1)S(1)}, bf16[64,256]{1,0:T(8,128)(2,1)S(1)}, bf16[48,512]{1,0:T(8,128)(2,1)S(1)}, bf16[64,256]{1,0:T(8,128)(2,1)S...) custom-call(s32[1,2]{1,0:T(1,128)S(1)} %bitcast.19, ...), custom_call_target="tpu_custom_call" | custom-call | flops 16777216 | bytes 1024 | tf_op jit(solution)/shard_map/pallas_call | solution.py:557
  8.2 0.0 collective-permute-done.sb_ref.eb_ref
  8.2 1.6 %collective-permute-done.1.sa_ref.ea_ref = bf16[8,1024]{1,0:T(8,128)(2,1)S(1)} collective-permute-done((bf16[8,1024]{1,0:T(8,128)(2,1)S(1)}, bf16[8,1024]{1,0:T(8,128)(2,1)S(1)}, u32[]{:S(2)}, u32[]{:S(2)}) %collective-permute-start.1) | collective-permute-done | bytes 16416 | tf_op jit(solution)/shard_map/ppermute | solution.py:553
  9.9 1.9 %collective-permute-start.2 = (bf16[64,768]{1,0:T(8,128)(2,1)S(1)}, bf16[64,768]{1,0:T(8,128)(2,1)S(1)}, u32[]{:S(2)}, u32[]{:S(2)}) collective-permute-start(bf16[64,768]{1,0:T(8,128)(2,1)S(1)} %get-tuple-element.43), channel_id=1, source_target_pairs={{0,7},{1,2},{2,1},{3,4},{4,3},{5,6},{6,5},{7,0},{8,15},{9,10},{10,... | collective-permute-start | bytes 294920 | tf_op jit(solution)/shard_map/ppermute | solution.py:553
  11.8 0.0 collective-permute-start.3
  11.8 1.9 %shard_map.141 = (bf16[512,256]{1,0:T(8,128)(2,1)S(1)}, f32[128,128]{1,0:T(8,128)S(1)}, f32[512,128]{1,0:T(8,128)S(1)}, f32[2,128,256]{2,1,0:T(8,128)S(1)}, bf16...) custom-call(bf16[8,1024]{1,0:T(8,128)(2,1)S(1)} %collective-permute-done.sb_ref.eb_ref, ...), custom_call_target="tpu_custom_call" | custom-call | flops 134217728 | bytes 1024 | tf_op jit(solution)/shard_map/pallas_call | solution.py:557
  13.7 2.8 %collective-permute-done.2.rb_ref = bf16[64,768]{1,0:T(8,128)(2,1)S(1)} collective-permute-done((bf16[64,768]{1,0:T(8,128)(2,1)S(1)}, bf16[64,768]{1,0:T(8,128)(2,1)S(1)}, u32[]{:S(2)}, u32[]{:S(2)}) %collective-permute-start.2) | collective-permute-done | bytes 98336 | tf_op jit(solution)/shard_map/ppermute | solution.py:553
  16.5 0.0 collective-permute-done.3.ra_ref
  16.6 1.8 %shard_map.142 = (f32[608,128]{1,0:T(8,128)S(1)}, bf16[608,128]{1,0:T(8,128)(2,1)S(1)}) custom-call(bf16[64,768]{1,0:T(8,128)(2,1)S(1)} %collective-permute-done.2.rb_ref, bf16[64,768]{1,0:T(8,128)(2,1)S(1)} %collective-permute-done.3.ra_ref, bf16[384,1024]{1,0:T(8,128)(2,1)S(1)} %get-tuple-element.45.pix_ref, ...), custom_call_target="tpu_custom_call" | custom-call | flops 134217728 | bytes 1024 | tf_op jit(solution)/shard_map/pallas_call | solution.py:557
  18.3 0.1 collective-permute-start.4
  18.4 1.4 %collective-permute-done.4.got_ref = bf16[608,128]{1,0:T(8,128)(2,1)S(1)} collective-permute-done((bf16[608,128]{1,0:T(8,128)(2,1)S(1)}, bf16[608,128]{1,0:T(8,128)(2,1)S(1)}, u32[]{:S(2)}, u32[]{:S(2)}) %collective-permute-start.4) | collective-permute-done | bytes 155680 | tf_op jit(solution)/shard_map/ppermute | solution.py:553
  19.8 13.8 %all_to_all.10.arrived_ref.got_ref = bf16[16,56,128]{2,1,0:T(8,128)(2,1)S(1)} all-to-all(bf16[16,56,128]{2,1,0:T(8,128)(2,1)S(1)} %shard_map.143), channel_id=1, replica_groups={{0,2,4,6,8,10,12,14,16,18,20,22,24,26,28,30},{1,3,5,7,9,11,13,15,17,19,..., dimensions={0} | all-to-all | bytes 458752 | tf_op jit(solution)/shard_map/all_to_all | solution.py:690
  33.6 10.3 %all_to_all.11.mine_ref = bf16[16,32,128]{2,1,0:T(8,128)(2,1)S(1)} all-to-all(bf16[16,32,128]{2,1,0:T(8,128)(2,1)S(1)} %shard_map.145), channel_id=1, replica_groups={{0,2,4,6,8,10,12,14,16,18,20,22,24,26,28,30},{1,3,5,7,9,11,13,15,17,19,..., dimensions={0} | all-to-all | bytes 262144 | tf_op jit(solution)/shard_map/all_to_all | solution.py:690
  43.9 0.0 collective-permute-start.5
  43.9 1.1 %shard_map.144 = bf16[192,768]{1,0:T(8,128)(2,1)} custom-call(bf16[16,56,128]{2,1,0:T(8,128)(2,1)S(1)} %all_to_all.10.arrived_ref.got_ref, bf16[64,768]{1,0:T(8,128)(2,1)S(1)} %bitcast.12), custom_call_target="tpu_custom_call" | custom-call | flops 134217728 | bytes 1024 | tf_op jit(solution)/shard_map/pallas_call | solution.py:557
  45.1 0.2 collective-permute-done.5.other_ref
  45.3 1.0 %shard_map.146 = (f32[64,768]{1,0:T(8,128)}, f32[4,4,64,64]{3,2,1,0:T(8,128)}, f32[4,12,4,64]{3,2,1,0:T(4,128)}, f32[768]{0:T(1024)}) custom-call(bf16[16,32,128]{2,1,0:T(8,128)(2,1)S(1)} %all_to_all.11.mine_ref, bf16[16,32,128]{2,1,0:T(8,128)(2,1)S(1)} %collective-permute-done.5.other_ref, bf16[64,768]{1,0:T(8,128)(2,1)S(1)} %bitcast.13), custom_call_target="tpu_custom_call" | custom-call | flops 1048576 | bytes 1024 | tf_op jit(solution)/shard_map/pallas_call | solution.py:557
  (3 shorter events, 0.1 us)
Async XLA Ops:
  0.6 1.0 %copy-start.8 = (bf16[2,64,8,128]{3,2,1,0:T(8,128)(2,1)S(1)}, bf16[2,64,8,128]{3,2,1,0:T(8,128)(2,1)}, u32[]{:S(2)}) copy-start(bf16[2,64,8,128]{3,2,1,0:T(8,128)(2,1)} %pre_ref.1) | copy-start | bytes 786436
  0.6 1.0 %copy-start.9 = (bf16[2,12,16,256]{3,2,1,0:T(8,128)(2,1)S(1)}, bf16[2,12,16,256]{3,2,1,0:T(8,128)(2,1)}, u32[]{:S(2)}) copy-start(bf16[2,12,16,256]{3,2,1,0:T(8,128)(2,1)} %cot_ref.1) | copy-start | bytes 589828
  1.6 5.0 %copy-start = (bf16[768,64]{0,1:T(8,128)(2,1)S(1)}, bf16[768,64]{0,1:T(8,128)(2,1)}, u32[]{:S(2)}) copy-start(bf16[768,64]{0,1:T(8,128)(2,1)} %param.15) | copy-start | bytes 294916
  1.6 5.0 %copy-start.1 = (bf16[1,1,2,64,768]{4,3,2,1,0:T(8,128)(2,1)S(1)}, bf16[1,1,2,64,768]{4,3,2,1,0:T(8,128)(2,1)}, u32[]{:S(2)}) copy-start(bf16[1,1,2,64,768]{4,3,2,1,0:T(8,128)(2,1)} %param.10) | copy-start | bytes 589828
  1.6 5.0 %copy-start.2 = (bf16[4,4,64,64]{3,2,1,0:T(8,128)(2,1)S(1)}, bf16[4,4,64,64]{3,2,1,0:T(8,128)(2,1)}, u32[]{:S(2)}) copy-start(bf16[4,4,64,64]{3,2,1,0:T(8,128)(2,1)} %first_ref.1) | copy-start | bytes 393220
  1.6 5.0 %copy-start.3 = (bf16[4,4,12,64]{3,1,2,0:T(4,128)(2,1)S(1)}, bf16[4,4,12,64]{3,1,2,0:T(4,128)(2,1)}, u32[]{:S(2)}) copy-start(bf16[4,4,12,64]{3,1,2,0:T(4,128)(2,1)} %param.17) | copy-start | bytes 73732
  1.6 5.0 %copy-start.6 = (s32[1,1,2,64,1]{3,4,2,1,0:T(1,128)S(1)}, s32[1,1,2,64,1]{3,4,2,1,0:T(1,128)}, u32[]{:S(2)}) copy-start(s32[1,1,2,64,1]{3,4,2,1,0:T(1,128)} %param.13) | copy-start | bytes 1540
  2.2 6.0 %collective-permute-start = (bf16[8,1024]{1,0:T(8,128)(2,1)S(1)}, bf16[8,1024]{1,0:T(8,128)(2,1)S(1)}, u32[]{:S(2)}, u32[]{:S(2)}) collective-permute-start(bf16[8,1024]{1,0:T(8,128)(2,1)S(1)} %get-tuple-element.36), channel_id=1, source_target_pairs={{0,24},{8,16},{16,8},{24,0},{1,25},{9,17},{17,9},{25,1},{2,26},{10... | collective-permute-start | bytes 49160 | tf_op jit(solution)/shard_map/ppermute | solution.py:553
  6.1 3.7 %collective-permute-start.1 = (bf16[8,1024]{1,0:T(8,128)(2,1)S(1)}, bf16[8,1024]{1,0:T(8,128)(2,1)S(1)}, u32[]{:S(2)}, u32[]{:S(2)}) collective-permute-start(bf16[8,1024]{1,0:T(8,128)(2,1)S(1)} %get-tuple-element.36), channel_id=1, source_target_pairs={{0,8},{8,0},{16,24},{24,16},{1,9},{9,1},{17,25},{25,17},{2,10},{10... | collective-permute-start | bytes 49160 | tf_op jit(solution)/shard_map/ppermute | solution.py:553
  6.6 0.7 %copy-start.4 = (bf16[768]{0:T(1024)(128)(2,1)S(1)}, bf16[768]{0:T(1024)(128)(2,1)}, u32[]{:S(2)}) copy-start(bf16[768]{0:T(1024)(128)(2,1)} %mask_ref.3) | copy-start | bytes 4612
  6.6 0.7 %copy-start.5 = (s32[1,1,2,64]{3,2,1,0:T(2,128)S(1)}, s32[1,1,2,64]{3,2,1,0:T(2,128)}, u32[]{:S(2)}) copy-start(s32[1,1,2,64]{3,2,1,0:T(2,128)} %param.11) | copy-start | bytes 1540
  6.6 0.7 %copy-start.7 = (s32[1,1,2]{2,1,0:T(1,128)S(1)}, s32[1,1,2]{2,1,0:T(1,128)}, u32[]{:S(2)}) copy-start(s32[1,1,2]{2,1,0:T(1,128)} %param.12) | copy-start | bytes 28
  9.9 6.7 %collective-permute-start.2 = (bf16[64,768]{1,0:T(8,128)(2,1)S(1)}, bf16[64,768]{1,0:T(8,128)(2,1)S(1)}, u32[]{:S(2)}, u32[]{:S(2)}) collective-permute-start(bf16[64,768]{1,0:T(8,128)(2,1)S(1)} %get-tuple-element.43), channel_id=1, source_target_pairs={{0,7},{1,2},{2,1},{3,4},{4,3},{5,6},{6,5},{7,0},{8,15},{9,10},{10,... | collective-permute-start | bytes 294920 | tf_op jit(solution)/shard_map/ppermute | solution.py:553
  11.8 4.8 %collective-permute-start.3 = (bf16[64,768]{1,0:T(8,128)(2,1)S(1)}, bf16[64,768]{1,0:T(8,128)(2,1)S(1)}, u32[]{:S(2)}, u32[]{:S(2)}) collective-permute-start(bf16[64,768]{1,0:T(8,128)(2,1)S(1)} %get-tuple-element.44), channel_id=1, source_target_pairs={{0,1},{1,0},{2,3},{3,2},{4,5},{5,4},{6,7},{7,6},{8,9},{9,8},{10,11... | collective-permute-start | bytes 294920 | tf_op jit(solution)/shard_map/ppermute | solution.py:553
  18.3 1.4 %collective-permute-start.4 = (bf16[608,128]{1,0:T(8,128)(2,1)S(1)}, bf16[608,128]{1,0:T(8,128)(2,1)S(1)}, u32[]{:S(2)}, u32[]{:S(2)}) collective-permute-start(bf16[608,128]{1,0:T(8,128)(2,1)S(1)} %get-tuple-element.60), channel_id=1, source_target_pairs={{0,1},{1,0},{2,3},{3,2},{4,5},{5,4},{6,7},{7,6},{8,9},{9,8},{10,11... | collective-permute-start | bytes 466952 | tf_op jit(solution)/shard_map/ppermute | solution.py:553
  43.9 1.3 %collective-permute-start.5 = (bf16[16,32,128]{2,1,0:T(8,128)(2,1)S(1)}, bf16[16,32,128]{2,1,0:T(8,128)(2,1)S(1)}, u32[]{:S(2)}, u32[]{:S(2)}) collective-permute-start(bf16[16,32,128]{2,1,0:T(8,128)(2,1)S(1)} %all_to_all.11.mine_ref), channel_id=1, source_target_pairs={{0,1},{1,0},{2,3},{3,2},{4,5},{5,4},{6,7},{7,6},{8,9},{9,8},{10,11... | collective-permute-start | bytes 393224 | tf_op jit(solution)/shard_map/ppermute | solution.py:553
